TPU v7x, 512 devices: a whole 4x4x16 slice. The times are simulated.
512 devices in a mesh: inst: 32 (over z, core), tp: 16 (over x, y).
Axes of the slice: x: 4, y: 4, z: 16, core: 2. Of those that a mesh axis runs over, the one named last changes fastest.
Arguments:
- queries: bfloat16 [512, 8192], P('inst', 'tp'), may hold values from -5 to 5, as said below
- home_keys: bfloat16 [8192, 16, 1024], P(('inst', 'tp')), may hold values from -5 to 5
- home_values: bfloat16 [8192, 16, 1024], P(('inst', 'tp')), may hold values from -12 to 12
- home_table: int32 [512, 16, 1], P('inst', 'tp'), may hold values from 0 to 15
- home_len: int32 [512, 16], P('inst', 'tp'), may hold values from 2 to 16
- lent_keys: bfloat16 [16384, 16, 1024], P(('inst', 'tp')), may hold values from -5 to 5
- lent_values: bfloat16 [16384, 16, 1024], P(('inst', 'tp')), may hold values from -12 to 12
- lend_row: int32 [32, 32, 16, 2], P('inst', None, 'tp'), may hold values from 0 to 15
- lend_table: int32 [32, 32, 16, 2, 2], P('inst', None, 'tp'), may hold values from 0 to 31
- lend_len: int32 [32, 32, 16, 2], P('inst', None, 'tp'), may hold values from 0 to 32, as said below
Outputs:
- attended: bfloat16 [512, 8192], P('inst', 'tp')
Inputs may be any that keep to these rules, and one draw needn't show every extreme that they name: `queries`: hidden draws take other laws within the same range. `lend_len`: live slots hold 2 or more tokens; every creditor has a slot of exactly 32 tokens; creditors' loads differ.
All inputs are finite; a program needn't handle non-finite values.
Results may differ from a plain program's by a relative error of at most 0.004.
Values may be sent and summed in bfloat16 or wider, within the bound.
No kernel may reach another device: no remote copies, remote signals or barrier semaphores. Data moves between devices by JAX's collectives and lax.ppermute only.
A program may use at most 64 MiB of HBM per device.

v0:
```python
import jax
import jax.numpy as jnp
from jax import lax
from jax.sharding import PartitionSpec as P

QH = 64
KVH = 8
HD = 128


def merged_2(value, axis, join):
    pieces = jax.tree.map(lambda part: lax.all_gather(part, axis), value)
    head = jax.tree.map(lambda part: part[0], pieces)
    tail = jax.tree.map(lambda part: part[1:], pieces)
    so_far, _ = lax.scan(lambda so_far, section: (join(so_far, section), None), head, tail)
    return so_far


def attend(query, keys, values, length):
    scores = jnp.einsum(
        "rkgd,rskd->rkgs", query, keys, preferred_element_type=jnp.float32
    ) * HD ** (-0.5)
    live = (
        jnp.arange(keys.shape[1], dtype=jnp.int32)[None, None, None, :]
        < length[:, None, None, None]
    )
    peak = jnp.max(jnp.where(live, scores, -jnp.inf), axis=3)
    weights = jnp.where(live, jnp.exp(scores - peak[..., None]), 0.0).astype(jnp.bfloat16)
    total = jnp.sum(weights.astype(jnp.float32), axis=3)
    mixed = (
        jnp.einsum("rkgs,rskd->rkgd", weights, values, preferred_element_type=jnp.float32)
        / total[..., None]
    )
    return (mixed, peak + jnp.log(total))


def join_pair(first, second):
    mixed_a, lse_a = first
    mixed_b, lse_b = second
    top = jnp.maximum(lse_a, lse_b)
    weight_a = jnp.exp(lse_a - top)
    weight_b = jnp.exp(lse_b - top)
    total = weight_a + weight_b
    mixed = (weight_a[..., None] * mixed_a + weight_b[..., None] * mixed_b) / total[..., None]
    return (mixed, top + jnp.log(total))


def lent_attend(query_rows, lent_k, lent_v, lengths):
    lent_mixed, lent_lse = attend(query_rows, lent_k, lent_v, jnp.maximum(lengths, 1))
    live = (lengths > 0)[:, None, None]
    lent_mixed = jnp.where(live[..., None], lent_mixed, 0.0)
    lent_lse = jnp.where(live, lent_lse, -1e30)
    return (lent_mixed, lent_lse)


def per_device(
    queries,
    home_keys,
    home_values,
    home_table,
    home_len,
    lent_keys,
    lent_values,
    lend_row,
    lend_table,
    lend_len,
):
    group = QH // KVH
    whole = lax.all_gather(queries, "tp", axis=1, tiled=True)
    count_rows = whole.shape[0]
    query_heads = whole.reshape(count_rows, KVH, group, HD)
    home_ids = home_table[:, 0, :]
    home_k = home_keys[home_ids].reshape(count_rows, -1, KVH, HD)
    home_v = home_values[home_ids].reshape(count_rows, -1, KVH, HD)
    home_mixed, home_lse = attend(query_heads, home_k, home_v, home_len[:, 0])
    peers = lend_row.shape[1]
    slots = lend_row.shape[3]
    asked = lend_row.reshape(peers * slots)
    blocks = lend_table.reshape(peers * slots, -1)
    lengths = lend_len.reshape(peers * slots)
    lent_k = lent_keys[blocks].reshape(peers * slots, -1, KVH, HD)
    lent_v = lent_values[blocks].reshape(peers * slots, -1, KVH, HD)
    sent = whole[asked].reshape(peers, slots, QH * HD)
    received = lax.all_to_all(sent, "inst", split_axis=0, concat_axis=0, tiled=True)
    lent_mixed, lent_lse = lent_attend(
        received.reshape(peers * slots, KVH, group, HD), lent_k, lent_v, lengths
    )
    back_mixed, back_lse = (
        lax.all_to_all(
            lent_mixed.reshape(peers, slots, QH * HD),
            "inst",
            split_axis=0,
            concat_axis=0,
            tiled=True,
        ),
        lax.all_to_all(
            lent_lse.reshape(peers, slots, QH), "inst", split_axis=0, concat_axis=0, tiled=True
        ),
    )
    back_mixed = back_mixed.reshape(peers * slots, QH, HD)
    back_lse = back_lse.reshape(peers * slots, QH)
    onehot = (asked[:, None] == jnp.arange(count_rows, dtype=jnp.int32)[None, :]).astype(
        jnp.float32
    )
    home_mixed = home_mixed.reshape(count_rows, QH, HD)
    home_lse = home_lse.reshape(count_rows, QH)
    lent_top = jnp.max(jnp.where(onehot[:, :, None] > 0, back_lse[:, None, :], -1e30), axis=0)
    peak = jnp.maximum(home_lse, lent_top)
    lent_peak = jnp.dot(onehot, peak, precision=lax.Precision.HIGHEST)
    lent_weight = jnp.exp(back_lse - lent_peak)
    home_weight = jnp.exp(home_lse - peak)
    total = home_weight + jnp.dot(onehot.T, lent_weight, precision=lax.Precision.HIGHEST)
    spread = (lent_weight[:, :, None] * back_mixed).reshape(peers * slots, QH * HD)
    summed = home_weight[..., None] * home_mixed + jnp.dot(
        onehot.T, spread, precision=lax.Precision.HIGHEST
    ).reshape(count_rows, QH, HD)
    local_out = summed / total[..., None]
    local_lse = peak + jnp.log(total)
    width = QH // lax.axis_size("tp")
    merged, unused = merged_2((local_out, local_lse), "tp", join_pair)
    mine = lax.dynamic_slice_in_dim(merged, lax.axis_index("tp") * width, width, 1)
    return mine.reshape(count_rows, width * HD).astype(jnp.bfloat16)


def solution(mesh):
    in_specs = (
        P("inst", "tp"),
        P(("inst", "tp"), None, None),
        P(("inst", "tp"), None, None),
        P("inst", "tp", None),
        P("inst", "tp"),
        P(("inst", "tp"), None, None),
        P(("inst", "tp"), None, None),
        P("inst", None, "tp", None),
        P("inst", None, "tp", None, None),
        P("inst", None, "tp", None),
    )
    out_specs = P("inst", "tp")
    return jax.shard_map(
        per_device, mesh=mesh, in_specs=in_specs, out_specs=out_specs, check_vma=False
    )
```

profile of v0, /device:TPU:1, one launch (start us, length us, event | category | flops | bytes accessed | tf_op | source)
XLA Modules:
  0.0 373.9 jit_solution(15396745493745127085)
XLA Ops:
  6.5 19.8 %all_gather.15 = bf16[16,8192]{1,0:T(8,128)(2,1)S(1)} all-gather(bf16[16,512]{1,0:T(8,128)(2,1)} %param.12), channel_id=1, replica_groups=mesh['inst'=32,'tp'=16] {'tp'}, dimensions={1}, use_global_device_ids=true | all-gather | bytes 278528 | tf_op jit(solution)/shard_map/all_gather | solution.py:69
  26.4 0.8 copy.73
  27.2 1.2 gather_fusion.1
  28.5 1.5 reshape.243
  30.0 21.1 %all-to-all-start = ((bf16[32,2,8192]{2,1,0:T(2,128)(2,1)}), bf16[32,2,8192]{2,1,0:T(2,128)(2,1)S(1)}, u32[]{:S(2)}, u32[]{:S(2)}) async-start(bf16[32,2,8192]{2,1,0:T(2,128)(2,1)} %reshape.243), calls=%async_computation | async-start | bytes 2097152 | tf_op jit(solution)/shard_map/all_to_all | solution.py:84
  51.8 2.8 gather_fusion.2
  54.6 5.4 %copy.97 = bf16[256,8,8,128]{3,2,1,0:T(8,128)(2,1)} copy(bf16[256,8,8,128]{3,1,2,0:T(8,128)(2,1)} %bitcast.122) | data formatting | bytes 8388608
  60.0 2.8 gather_fusion.4
  62.8 5.2 %copy.99 = bf16[256,8,8,128]{3,2,1,0:T(8,128)(2,1)} copy(bf16[256,8,8,128]{3,1,2,0:T(8,128)(2,1)} %bitcast.121) | data formatting | bytes 8388608
  68.4 38.5 %all-to-all-done = bf16[32,2,8192]{2,1,0:T(2,128)(2,1)S(1)} async-done(((bf16[32,2,8192]{2,1,0:T(2,128)(2,1)}), bf16[32,2,8192]{2,1,0:T(2,128)(2,1)S(1)}, u32[]{:S(2)}, u32[]{:S(2)}) %all-to-all-start) | async-done | bytes 1048608 | tf_op jit(solution)/shard_map/all_to_all | solution.py:84
  106.8 1.6 reshape.244
  108.5 4.9 %select_reduce_fusion = (f32[64,8,8]{2,1,0:T(8,128)S(1)}, f32[64,8,8,32]{3,2,1,0:T(8,128)S(1)}) fusion(pred[64,32]{1,0:T(8,128)(4,1)S(1)} %iota_compare_fusion, bf16[64,8,8,128]{3,2,1,0:T(8,128)(2,1)} %reshape.244, bf16[64,32,8,128]{3,2,1,0:T(8,128)(2,1)} %bitcast.120), kind=kOutput, calls=%fused_computation.27 | convolution fusion | flops 33943552 | bytes 5785600 | tf_op jit(solution)/shard_map/rkgd,rskd->rkgs/dot_general | solution.py:20
  113.3 1.4 convert_reduce_fusion
  116.2 1.1 add.80
  118.1 4.0 %all-to-all-start.1 = ((f32[32,1,128]{2,1,0:T(1,128)}), f32[32,1,128]{2,1,0:T(1,128)S(1)}, u32[]{:S(2)}, u32[]{:S(2)}) async-start(f32[32,1,128]{2,1,0:T(1,128)} %reshape.307), calls=%async_computation.1 | async-start | bytes 32768 | tf_op jit(solution)/shard_map/all_to_all | solution.py:96
  122.1 4.4 %divide_select_fusion = f32[64,8,8,128]{3,2,1,0:T(8,128)} fusion(bf16[64,32,8,128]{3,2,1,0:T(8,128)(2,1)} %bitcast.125, f32[64,8,8]{2,1,0:T(8,128)} %copy-done.5, pred[64]{0:T(512)(128)(4,1)S(1)} %gt.32, f32[64,8,8,32]{3,2,1,0:T(8,128)S(1)} %get-tuple-element.70, f32[64,8,8]{2,1,0:T(8,128)} %copy-done.3, pred[64,32]{1,0:T(8,128)(4,1)S(1)} %iota_compare_fusion), kind=kOutput, calls=%fused_computation.24 | convolution fusion | flops 35127296 | bytes 6850624 | tf_op jit(solution)/shard_map/rkgs,rskd->rkgd/dot_general | solution.py:31
  126.5 3.5 reshape.250
  130.0 3.9 %all-to-all-done.1 = f32[32,1,128]{2,1,0:T(1,128)S(1)} async-done(((f32[32,1,128]{2,1,0:T(1,128)}), f32[32,1,128]{2,1,0:T(1,128)S(1)}, u32[]{:S(2)}, u32[]{:S(2)}) %all-to-all-start.1) | async-done | bytes 16416 | tf_op jit(solution)/shard_map/all_to_all | solution.py:96
  133.9 8.5 %all-to-all-start.2 = ((f32[32,2,8192]{2,1,0:T(2,128)}), f32[32,2,8192]{2,1,0:T(2,128)S(1)}, u32[]{:S(2)}, u32[]{:S(2)}) async-start(f32[32,2,8192]{2,1,0:T(2,128)} %reshape.250), calls=%async_computation.2 | async-start | bytes 4194304 | tf_op jit(solution)/shard_map/all_to_all | solution.py:89
  143.6 2.4 gather_fusion
  146.1 1.6 select_reduce_fusion.2
  147.7 0.8 copy-done.4
  149.1 2.4 gather_fusion.3
  151.5 2.4 fusion.18
  156.0 85.0 %all-to-all-done.2 = f32[32,2,8192]{2,1,0:T(2,128)S(1)} async-done(((f32[32,2,8192]{2,1,0:T(2,128)}), f32[32,2,8192]{2,1,0:T(2,128)S(1)}, u32[]{:S(2)}, u32[]{:S(2)}) %all-to-all-start.2) | async-done | bytes 2097184 | tf_op jit(solution)/shard_map/all_to_all | solution.py:89
  241.0 2.5 reshape.251
  244.1 1.0 copy-done.2
  245.1 4.2 %fusion.15 = f32[16,64,128]{2,0,1:T(8,128)} fusion(f32[16,64,128]{2,1,0:T(8,128)} %fusion.18, f32[16,64]{0,1:T(8,128)S(1)} %copy.89, f32[16,64]{0,1:T(8,128)S(1)} %copy.83, s32[64]{0:T(128)S(1)} %eq.19, f32[64,8192]{1,0:T(8,128)S(1)} %copy-done.2, f32[8,8,64,128]{3,2,1,0:T(8,128)S(1)} %bitcast.124), kind=kOutput, calls=%fused_computation.29 | convolution fusion | flops 101581824 | bytes 5251328 | tf_op jit(solution)/shard_map/dot_general | solution.py:114
  249.3 18.1 %all-gather.1 = f32[256,64]{1,0:T(8,128)S(1)} all-gather(f32[16,64]{1,0:T(8,128)S(1)} %get-tuple-element.73), channel_id=3, replica_groups=mesh['inst'=32,'tp'=16] {'tp'}, dimensions={0}, use_global_device_ids=true | all-gather | bytes 69632 | tf_op jit(solution)/shard_map/all_gather | solution.py:12
  267.4 66.5 %all-gather.4.cloned.1.call-done = f32[256,64,128]{2,0,1:T(8,128)} async-done(((f32[16,64,128]{2,0,1:T(8,128)}), f32[256,64,128]{2,0,1:T(8,128)}) %all-gather.4.cloned.1.call-update) | async-done | bytes 8388624 | tf_op jit(solution)/shard_map/all_gather | solution.py:12
  333.9 1.1 slice.30
  335.1 6.8 %slice.33 = f32[240,64,128]{2,0,1:T(8,128)} slice(f32[256,64,128]{2,0,1:T(8,128)} %all-gather.4.cloned.1.call-done), slice={[16:256], [0:64], [0:128]} | slice | bytes 15728640 | tf_op jit(solution)/shard_map/slice | solution.py:14
  342.0 24.4 %while.12 = (s32[]{:T(128)}, f32[16,64,128]{2,1,0:T(8,128)S(1)}, f32[16,64]{1,0:T(8,128)S(1)}, f32[15,16,64]{2,1,0:T(8,128)S(1)}, f32[15,16,64,128]{3,1,0,2:T(8,128)}, /*index=5*/s32[]{:T(128)}) while((s32[]{:T(128)}, f32[16,64,128]{2,1,0:T(8,128)S(1)}, f32[16,64]{1,0:T(8,128)S(1)}, f32[15,16,64]{2,1,0:T(8,128)S(1)}, ...), condition=%wide.region_6.7_spmd, body=%wide.region_5.6_spmd.sunk | while | flops 529410 | bytes 2658381 | solution.py:15
  342.0 1.1 constant_dynamic-slice_fusion.2
  343.6 1.1 constant_dynamic-slice_fusion.2
  345.2 1.1 constant_dynamic-slice_fusion.2
  346.9 1.1 constant_dynamic-slice_fusion.2
  348.5 1.1 constant_dynamic-slice_fusion.2
  350.1 1.1 constant_dynamic-slice_fusion.2
  351.8 1.1 constant_dynamic-slice_fusion.2
  353.4 1.1 constant_dynamic-slice_fusion.2
  355.0 1.1 constant_dynamic-slice_fusion.2
  356.6 1.1 constant_dynamic-slice_fusion.2
  358.3 1.1 constant_dynamic-slice_fusion.2
  359.9 1.1 constant_dynamic-slice_fusion.2
  361.5 1.1 constant_dynamic-slice_fusion.2
  363.2 1.1 constant_dynamic-slice_fusion.2
  364.8 1.1 constant_dynamic-slice_fusion.2
  (97 shorter events, 16.3 us)
Async XLA Ops:
  6.5 45.3 %copy-start = (bf16[32,16,1024]{2,1,0:T(8,128)(2,1)S(1)}, bf16[32,16,1024]{2,1,0:T(8,128)(2,1)}, u32[]{:S(2)}) copy-start(bf16[32,16,1024]{2,1,0:T(8,128)(2,1)} %param.17) | copy-start | bytes 3145732
  28.5 22.7 %copy-start.7 = (s32[1,32,1,2]{1,3,2,0:T(2,128)S(1)}, s32[1,32,1,2]{1,3,2,0:T(2,128)}, u32[]{:S(2)}) copy-start(s32[1,32,1,2]{1,3,2,0:T(2,128)} %param.21) | copy-start | bytes 772
  28.5 22.9 %copy-start.6 = (s32[1,32,1,2,2]{1,4,3,2,0:T(2,128)S(1)}, s32[1,32,1,2,2]{1,4,3,2,0:T(2,128)}, u32[]{:S(2)}) copy-start(s32[1,32,1,2,2]{1,4,3,2,0:T(2,128)} %param.20) | copy-start | bytes 1540
  30.0 76.8 %all-to-all-start = ((bf16[32,2,8192]{2,1,0:T(2,128)(2,1)}), bf16[32,2,8192]{2,1,0:T(2,128)(2,1)S(1)}, u32[]{:S(2)}, u32[]{:S(2)}) async-start(bf16[32,2,8192]{2,1,0:T(2,128)(2,1)} %reshape.243), calls=%async_computation | async-start | bytes 2097152 | tf_op jit(solution)/shard_map/all_to_all | solution.py:84
  54.6 5.5 %copy-start.1 = (bf16[32,16,1024]{2,1,0:T(8,128)(2,1)S(1)}, bf16[32,16,1024]{2,1,0:T(8,128)(2,1)}, u32[]{:S(2)}) copy-start(bf16[32,16,1024]{2,1,0:T(8,128)(2,1)} %param.18) | copy-start | bytes 3145732
  113.3 1.4 copy-start.3
  114.7 0.7 copy-start.5
  118.1 15.8 %all-to-all-start.1 = ((f32[32,1,128]{2,1,0:T(1,128)}), f32[32,1,128]{2,1,0:T(1,128)S(1)}, u32[]{:S(2)}, u32[]{:S(2)}) async-start(f32[32,1,128]{2,1,0:T(1,128)} %reshape.307), calls=%async_computation.1 | async-start | bytes 32768 | tf_op jit(solution)/shard_map/all_to_all | solution.py:96
  130.0 13.6 %copy-start.9 = (s32[16,1,1]{0,2,1:T(1,128)S(1)}, s32[16,1,1]{0,2,1:T(1,128)}, u32[]{:S(2)}) copy-start(s32[16,1,1]{0,2,1:T(1,128)} %param.15) | copy-start | bytes 196
  130.0 16.1 %copy-start.8 = (s32[16,1]{0,1:T(1,128)S(1)}, s32[16,1]{0,1:T(1,128)}, u32[]{:S(2)}) copy-start(s32[16,1]{0,1:T(1,128)} %param.16) | copy-start | bytes 196
  133.9 107.1 %all-to-all-start.2 = ((f32[32,2,8192]{2,1,0:T(2,128)}), f32[32,2,8192]{2,1,0:T(2,128)S(1)}, u32[]{:S(2)}, u32[]{:S(2)}) async-start(f32[32,2,8192]{2,1,0:T(2,128)} %reshape.250), calls=%async_computation.2 | async-start | bytes 4194304 | tf_op jit(solution)/shard_map/all_to_all | solution.py:89
  142.4 191.4 %all-gather.4.cloned.1.call-start = ((), (), s32[]{:S(2)}) async-start(), calls=%async_computation.3 | async-start | bytes 8912896 | tf_op jit(solution)/shard_map/all_gather | solution.py:12
  147.7 0.8 copy-start.4
  243.5 1.6 copy-start.2
Sparse Core Ops, SparseCore 0:
  249.4 84.4 all-gather.3
where the time goes:
time: 375 us; the launch traced here: 374 us
  waiting for transfers between devices  194 us (52%)
  local copies, waits for them, and re-layouts  65 us (17%)
  blocking collectives  37.9 us (10%)
  starting transfers between devices  33.8 us (9%)
  matrix products  17.8 us (5%)
  between operations  13.7 us (4%)
  other arithmetic  11.3 us (3%)
    all_to_all x1, waiting for transfers between devices, per_device(): lax.all_to_all(lent_mixed.reshape(peers, slots, QH * HD), 'inst', split_a...  85 us
    all_gather x1, waiting for transfers between devices, merged_2(): pieces = jax.tree.map(lambda part: lax.all_gather(part, axis), value)  66.5 us
    all_to_all x1, waiting for transfers between devices, per_device(): lax.all_to_all(sent, 'inst', split_axis=0, concat_axis=0, tiled=True)  38.5 us
    all_to_all x1, starting transfers between devices, per_device(): lax.all_to_all(sent, 'inst', split_axis=0, concat_axis=0, tiled=True)  21.1 us
    all_gather x1, blocking collectives, per_device(): whole = lax.all_gather(queries, 'tp', axis=1, tiled=True)  19.8 us
    all_gather x1, blocking collectives, merged_2(): pieces = jax.tree.map(lambda part: lax.all_gather(part, axis), value)  18.1 us
    dynamic_slice x15, local copies, waits for them, and re-layouts, merged_2(): lax.scan(lambda so_far, section: (join(so_far, section), None), head, tail)  16.4 us
    unnamed x28, local copies, waits for them, and re-layouts  16.1 us
  transfers between devices with their start and end apart: 4, of which 4 were waited for; matrix products, arithmetic and copies ran while one was open for 10% of the time, Pallas kernels for 0%

commit v1 on v0

v1 whole, which is shorter than its diff:
```python
import functools
import math

import jax
import jax.numpy as jnp
from jax import lax
from jax.experimental import pallas as pl
from jax.experimental.pallas import tpu as pltpu
from jax.sharding import PartitionSpec as P

QH = 64
KVH = 8
HD = 128
N_INST = 32
N_TP = 16
ROWS = 16
SLOTS = 64
WIDTH = 512
GROUPS = 4
SEGS = SLOTS + ROWS
DEAD = -1e30
SCALE = HD ** (-0.5)
F32 = jnp.float32
BF16 = jnp.bfloat16


def iota(shape, axis):
    return lax.broadcasted_iota(jnp.int32, shape, axis)


def dot(a, b):
    return jnp.dot(a, b, preferred_element_type=F32)


def dot_nt(a, b):
    return lax.dot_general(a, b, (((1,), (1,)), ((), ())), preferred_element_type=F32)


def split3(x):
    hi = x.astype(BF16).astype(F32)
    rest = x - hi
    mid = rest.astype(BF16).astype(F32)
    return hi, mid, rest - mid


def spread3(x):
    hi, mid, low = split3(x)
    return hi + pltpu.roll(mid, 4, 1) + pltpu.roll(low, 8, 1)


def pick_kernel(me_ref, all_ref, out_ref, target_ref):
    me = me_ref[0]
    k = iota((256, 128), 0)
    n = iota((256, 128), 1)
    local = jnp.bitwise_and(jnp.right_shift(k, 1), 7)
    order = jnp.where(n == local * 16 + jnp.right_shift(k, 4), 1.0, 0.0).astype(BF16)
    second = jnp.bitwise_and(k, 1) == 1
    base = local.astype(F32) * 16.0
    lane = n.astype(F32)
    row = iota((128, 128), 0)
    for g in range(GROUPS):
        rows = pl.ds(g * 128, 128)
        asked = all_ref[rows, WIDTH:]
        found = []
        for s in range(2):
            column = jnp.where(row == 2 * me + s, 1.0, 0.0).astype(BF16)
            found.append(dot(order, dot(asked, column).astype(BF16)))
        target = jnp.where(second, found[1], found[0]) + base
        onehot = jnp.where(lane == target, 1.0, 0.0).astype(BF16)
        picked = dot(onehot, all_ref[rows, :WIDTH]).astype(BF16)
        out_ref[:, g * 16 : (g + 1) * 16, :] = picked.reshape(N_TP, 16, WIDTH)
        target_ref[g] = target.T[:8]
    own = all_ref[pl.ds(pl.multiple_of(me * ROWS, ROWS), ROWS), :WIDTH]
    for t in range(N_TP):
        out_ref[t, SLOTS:, :] = own


def attend_kernel(
    lent_ref, home_ref, x_ref, lk_ref, lv_ref, hk_ref, hv_ref, out_ref, count_s, bias_s, hbias_s
):
    @pl.when(pl.program_id(0) == 0)
    def _():
        token = iota((SLOTS, 512), 1)
        block = jnp.right_shift(token, 4)
        place = jnp.bitwise_and(token, 15)
        length = lent_ref[:, 2:3]
        first = (block == lent_ref[:, 0:1]) & (place < length)
        other = (block == lent_ref[:, 1:2]) & (place + 16 < length)
        count = jnp.where(first, 1.0, 0.0) + jnp.where(other, 1.0, 0.0)
        count_s[...] = count
        bias_s[...] = jnp.where(count > 0, 0.0, DEAD)
        token = iota((ROWS, 256), 1)
        live = (jnp.right_shift(token, 4) == home_ref[:, 0:1]) & (
            jnp.bitwise_and(token, 15) < home_ref[:, 1:2]
        )
        hbias_s[...] = jnp.where(live, 0.0, DEAD)

    factor = SCALE * math.log2(math.e)
    lent_k = lk_ref[...].reshape(512, HD)
    lent_v = lv_ref[...].reshape(512, HD)
    home_k = hk_ref[...].reshape(256, HD)
    home_v = hv_ref[...].reshape(256, HD)
    lane = iota((SLOTS, 128), 1)
    hlane = iota((ROWS, 128), 1)
    for tt in range(2):
        query = jnp.concatenate(
            [x_ref[tt, :SLOTS, h * HD : (h + 1) * HD] for h in range(4)], axis=0
        )
        scores = dot_nt(query, lent_k)
        lse = jnp.zeros((SLOTS, 128), F32)
        weights = []
        totals = []
        for h in range(4):
            part = scores[h * SLOTS : (h + 1) * SLOTS] + bias_s[...]
            peak = jnp.max(part, axis=1, keepdims=True)
            weight = (jnp.exp2((part - peak) * factor) * count_s[...]).astype(BF16)
            total = jnp.sum(weight.astype(F32), axis=1, keepdims=True)
            live = total > 0
            total = jnp.where(live, total, 1.0)
            lse = jnp.where(
                lane == h, jnp.where(live, peak * SCALE + jnp.log(total), DEAD), lse
            )
            weights.append(weight)
            totals.append(total)
        mixed = dot(jnp.concatenate(weights, axis=0), lent_v)
        for h in range(4):
            out_ref[tt, :SLOTS, h * HD : (h + 1) * HD] = (
                mixed[h * SLOTS : (h + 1) * SLOTS] / totals[h]
            ).astype(BF16)
        query = jnp.concatenate(
            [x_ref[tt, SLOTS:, h * HD : (h + 1) * HD] for h in range(4)], axis=0
        )
        scores = dot_nt(query, home_k)
        hlse = jnp.zeros((ROWS, 128), F32)
        weights = []
        totals = []
        for h in range(4):
            part = scores[h * ROWS : (h + 1) * ROWS] + hbias_s[...]
            peak = jnp.max(part, axis=1, keepdims=True)
            weight = jnp.exp2((part - peak) * factor).astype(BF16)
            total = jnp.sum(weight.astype(F32), axis=1, keepdims=True)
            hlse = jnp.where(hlane == h, peak * SCALE + jnp.log(total), hlse)
            weights.append(weight)
            totals.append(total)
        mixed = dot(jnp.concatenate(weights, axis=0), home_v)
        for h in range(4):
            out_ref[tt, SLOTS:SEGS, h * HD : (h + 1) * HD] = (
                mixed[h * ROWS : (h + 1) * ROWS] / totals[h]
            ).astype(BF16)
        column = jnp.concatenate([lse, hlse, jnp.zeros((128 - SEGS, 128), F32)], axis=0)
        out_ref[tt, SEGS:, :128] = spread3(column).T[:16].astype(BF16)
        out_ref[tt, SEGS:, 128:] = jnp.zeros((16, WIDTH - 128), BF16)


def merge_kernel(target_ref, x_ref, lent_ref, home_ref):
    lane = iota((8, 128), 1)
    lses = []
    for t in range(N_TP):
        parts = x_ref[t, SEGS:, :128].astype(F32)
        lses.append(parts[0:4] + parts[4:8] + parts[8:12])
    lses = [jnp.concatenate([x, x], axis=0) for x in lses]
    for g in range(GROUPS + 1):
        halves = []
        for half in range(2):
            row = jnp.zeros((8, 128), F32)
            for j in range(8):
                shift = (16 * j - 16 * g) % 128
                moved = lses[half * 8 + j]
                moved = pltpu.roll(moved, shift, 1) if shift else moved
                row = jnp.where(jnp.right_shift(lane, 4) == j, moved, row)
            halves.append(row)
        lse = jnp.concatenate(halves, axis=1)
        high = 128 if g < GROUPS else ROWS
        rows = iota((high, 256), 0)
        if g < GROUPS:
            mask = rows.astype(F32) == target_ref[g, 0:1, :]
        else:
            mask = rows == jnp.bitwise_and(iota((high, 256), 1), 15)
        values = x_ref[:, g * 16 : (g + 1) * 16, :].reshape(256, WIDTH)
        out_lse = jnp.zeros((high, 128), F32)
        out_lane = iota((high, 128), 1)
        mixed = []
        for h in range(4):
            score = jnp.where(mask, lse[h : h + 1, :], DEAD)
            peak = jnp.max(score, axis=1, keepdims=True)
            weight = jnp.exp(score - peak)
            total = jnp.sum(weight, axis=1, keepdims=True)
            upper = weight.astype(BF16)
            lower = (weight - upper.astype(F32)).astype(BF16)
            both = dot(
                jnp.concatenate([upper, lower], axis=0), values[:, h * HD : (h + 1) * HD]
            )
            mixed.append((both[:high] + both[high:]) / total)
            out_lse = jnp.where(out_lane == h, peak + jnp.log(total), out_lse)
        if g < GROUPS:
            block = slice(g * 8, (g + 1) * 8)
            for h in range(4):
                lent_ref[block, :, h * HD : (h + 1) * HD] = (
                    mixed[h].astype(BF16).reshape(8, ROWS, HD)
                )
            lent_ref[block, :, WIDTH:] = (
                spread3(out_lse).astype(BF16).reshape(8, ROWS, 128)
            )
        else:
            for h in range(4):
                home_ref[:, h * HD : (h + 1) * HD] = mixed[h]
            home_ref[:, WIDTH:] = out_lse


def final_kernel(home_ref, x_ref, out_ref):
    pieces = x_ref.shape[0]
    lses = [home_ref[:, WIDTH:]]
    for c in range(pieces):
        parts = x_ref[c, :, WIDTH:].astype(F32)
        lses.append(parts + pltpu.roll(parts, 124, 1) + pltpu.roll(parts, 120, 1))
    peak = functools.reduce(jnp.maximum, lses)
    weights = [jnp.exp(lse - peak) for lse in lses]
    total = sum(weights)
    for h in range(4):
        cut = slice(h * HD, (h + 1) * HD)
        mixed = weights[0][:, h : h + 1] * home_ref[:, cut]
        for c in range(pieces):
            mixed = mixed + weights[c + 1][:, h : h + 1] * x_ref[c, :, cut].astype(F32)
        out_ref[:, cut] = (mixed / total[:, h : h + 1]).astype(BF16)


VMEM = pl.BlockSpec(memory_space=pltpu.VMEM)
SMEM = pl.BlockSpec(memory_space=pltpu.SMEM)
PARAMS = pltpu.CompilerParams(vmem_limit_bytes=48 * 1024 * 1024)


def exchange(x, axis):
    return lax.all_to_all(x, axis, split_axis=0, concat_axis=0, tiled=True)


def per_device(
    queries,
    home_keys,
    home_values,
    home_table,
    home_len,
    lent_keys,
    lent_values,
    lend_row,
    lend_table,
    lend_len,
):
    me = lax.axis_index("inst").astype(jnp.int32).reshape(1)
    asked = exchange(jnp.broadcast_to(lend_row.reshape(1, SLOTS), (N_TP, SLOTS)), "tp")
    sent = jnp.concatenate(
        [queries, asked.astype(BF16), jnp.zeros((ROWS, 128 - SLOTS), BF16)], axis=1
    )
    gathered = lax.all_gather(sent, "inst", axis=0, tiled=True)
    picked, target = pl.pallas_call(
        pick_kernel,
        out_shape=(
            jax.ShapeDtypeStruct((N_TP, SEGS, WIDTH), BF16),
            jax.ShapeDtypeStruct((GROUPS, 8, 256), F32),
        ),
        in_specs=[SMEM, VMEM],
        out_specs=(VMEM, VMEM),
        compiler_params=PARAMS,
        name="pick",
    )(me, gathered)
    arrived = exchange(picked, "tp")
    lent_meta = jnp.concatenate(
        [lend_table.reshape(SLOTS, 2), lend_len.reshape(SLOTS, 1)], axis=1
    )
    home_meta = jnp.concatenate([home_table.reshape(ROWS, 1), home_len], axis=1)
    partial = pl.pallas_call(
        attend_kernel,
        grid=(KVH,),
        out_shape=jax.ShapeDtypeStruct((N_TP, SEGS + 16, WIDTH), BF16),
        in_specs=[
            pl.BlockSpec((SLOTS, 3), lambda k: (0, 0)),
            pl.BlockSpec((ROWS, 2), lambda k: (0, 0)),
            pl.BlockSpec((2, SEGS, WIDTH), lambda k: (k, 0, 0)),
            pl.BlockSpec((32, 16, HD), lambda k: (0, 0, k)),
            pl.BlockSpec((32, 16, HD), lambda k: (0, 0, k)),
            pl.BlockSpec((16, 16, HD), lambda k: (0, 0, k)),
            pl.BlockSpec((16, 16, HD), lambda k: (0, 0, k)),
        ],
        out_specs=pl.BlockSpec((2, SEGS + 16, WIDTH), lambda k: (k, 0, 0)),
        scratch_shapes=[
            pltpu.VMEM((SLOTS, 512), F32),
            pltpu.VMEM((SLOTS, 512), F32),
            pltpu.VMEM((ROWS, 256), F32),
        ],
        compiler_params=PARAMS,
        name="attend",
    )(lent_meta, home_meta, arrived, lent_keys, lent_values, home_keys, home_values)
    returned = exchange(partial, "tp")
    lent, home = pl.pallas_call(
        merge_kernel,
        out_shape=(
            jax.ShapeDtypeStruct((N_INST, ROWS, WIDTH + 128), BF16),
            jax.ShapeDtypeStruct((ROWS, WIDTH + 128), F32),
        ),
        in_specs=[VMEM, VMEM],
        out_specs=(VMEM, VMEM),
        compiler_params=PARAMS,
        name="merge",
    )(target, returned)
    back = exchange(lent, "inst")
    return pl.pallas_call(
        final_kernel,
        out_shape=jax.ShapeDtypeStruct((ROWS, WIDTH), BF16),
        in_specs=[VMEM, VMEM],
        out_specs=VMEM,
        compiler_params=PARAMS,
        name="final",
    )(home, back)


def solution(mesh):
    in_specs = (
        P("inst", "tp"),
        P(("inst", "tp"), None, None),
        P(("inst", "tp"), None, None),
        P("inst", "tp", None),
        P("inst", "tp"),
        P(("inst", "tp"), None, None),
        P(("inst", "tp"), None, None),
        P("inst", None, "tp", None),
        P("inst", None, "tp", None, None),
        P("inst", None, "tp", None),
    )
    out_specs = P("inst", "tp")
    return jax.shard_map(
        per_device, mesh=mesh, in_specs=in_specs, out_specs=out_specs, check_vma=False
    )
```

time: 375 us -> 173 us (0.46)
  waiting for transfers between devices: 194 us -> 26.5 us
  blocking collectives: 37.9 us -> 112 us
  local copies, waits for them, and re-layouts: 65 us -> 4.23 us
  starting transfers between devices: 33.8 us -> 11.3 us
  matrix products: 17.8 us -> 0 us
  Pallas kernels: 0 us -> 17.4 us
  between operations: 13.7 us -> 0.11 us
  other arithmetic: 11.3 us -> 0.75 us
    all_to_all x3 -> x2, waiting for transfers between devices: 127 us -> 26.5 us  [exchange(): return lax.all_to_all(x, axis, split_axis=0, concat_axis=0, tiled=True)]
    all_to_all x0 -> x2, blocking collectives: none -> 72.4 us  [exchange(): return lax.all_to_all(x, axis, split_axis=0, concat_axis=0, tiled=True)]
    all_gather x1 -> x0, waiting for transfers between devices: 66.5 us -> none  [merged_2(): pieces = jax.tree.map(lambda part: lax.all_gather(part, axis), value)]
    all_to_all x3 -> x2, starting transfers between devices: 33.6 us -> 11.3 us  [exchange(): return lax.all_to_all(x, axis, split_axis=0, concat_axis=0, tiled=True)]
    dot_general x7 -> x0, matrix products: 17.8 us -> none  [the longest x2 6.83 us: attend(): jnp.einsum('rkgs,rskd->rkgd', weights, values, preferred_element_type=jnp...]
    pallas_call x0 -> x4, Pallas kernels: none -> 17.4 us  [the longest x1 11.8 us: per_device(): pl.pallas_call(attend_kernel, grid=(KVH,), out_shape=jax.ShapeDtypeStruct...]
    dynamic_slice x15 -> x0, local copies, waits for them, and re-layouts: 16.4 us -> none  [merged_2(): lax.scan(lambda so_far, section: (join(so_far, section), None), head, tail)]
    unnamed x28 -> x19, local copies, waits for them, and re-layouts: 16.1 us -> 3.05 us
  transfers between devices with their start and end apart: 4 -> 2, of which waited for: 4 -> 2; matrix products, arithmetic and copies ran while one was open for 10% -> 0% of each run, Pallas kernels for 0% -> 0%
where the time goes in v1:
time: 173 us
  blocking collectives  112 us (65%)
  waiting for transfers between devices  26.5 us (15%)
  Pallas kernels  17.4 us (10%)
  starting transfers between devices  11.3 us (7%)
  local copies, waits for them, and re-layouts  4.23 us (2%)
    all_to_all x2, blocking collectives, exchange(): return lax.all_to_all(x, axis, split_axis=0, concat_axis=0, tiled=True)  72.4 us
    all_gather x1, blocking collectives, per_device(): gathered = lax.all_gather(sent, 'inst', axis=0, tiled=True)  39.9 us
    all_to_all x2, waiting for transfers between devices, exchange(): return lax.all_to_all(x, axis, split_axis=0, concat_axis=0, tiled=True)  26.5 us
    pallas_call x1, Pallas kernels, per_device(): pl.pallas_call(attend_kernel, grid=(KVH,), out_shape=jax.ShapeDtypeStruct...  11.8 us
    all_to_all x2, starting transfers between devices, exchange(): return lax.all_to_all(x, axis, split_axis=0, concat_axis=0, tiled=True)  11.3 us
  transfers between devices with their start and end apart: 2, of which 2 were waited for; matrix products, arithmetic and copies ran while one was open for 0% of the time, Pallas kernels for 0%

profile of v1, /device:TPU:1, one launch (start us, length us, event | category | flops | bytes accessed | tf_op | source)
XLA Modules:
  0.0 172.6 jit_solution(3658293561923790909)
XLA Ops:
  0.0 0.8 copy.25
  0.8 0.1 broadcast_in_dim.10
  0.9 0.6 broadcast_in_dim.11
  1.5 7.6 %all-to-all-start = ((s32[16,1,64]{2,1,0:T(1,128)}), s32[16,1,64]{2,1,0:T(1,128)S(1)}, u32[]{:S(2)}, u32[]{:S(2)}) async-start(s32[16,1,64]{2,1,0:T(1,128)} %broadcast_in_dim.11), calls=%async_computation | async-start | bytes 16384 | tf_op jit(solution)/shard_map/all_to_all | solution.py:233
  9.1 0.1 pad.6.clone
  9.2 6.2 %all-to-all-done = s32[16,1,64]{2,1,0:T(1,128)S(1)} async-done(((s32[16,1,64]{2,1,0:T(1,128)}), s32[16,1,64]{2,1,0:T(1,128)S(1)}, u32[]{:S(2)}, u32[]{:S(2)}) %all-to-all-start) | async-done | bytes 4128 | tf_op jit(solution)/shard_map/all_to_all | solution.py:233
  15.4 0.7 maximum_maximum_fusion
  16.1 39.9 %all_gather.3.all_ref = bf16[512,640]{1,0:T(8,128)(2,1)S(1)} all-gather(bf16[16,640]{1,0:T(8,128)(2,1)S(1)} %maximum_maximum_fusion), channel_id=1, replica_groups=mesh['inst'=32,'tp'=16] {'inst'}, dimensions={0}, use_global_device_ids=true | all-gather | bytes 675840 | tf_op jit(solution)/shard_map/all_gather | solution.py:253
  56.1 0.0 copy-start.6
  56.1 0.0 copy-start.7
  56.1 0.0 copy-start.5
  56.1 0.0 copy-start.4
  56.1 0.0 copy-start
  56.1 0.0 copy-start.1
  56.1 2.6 %pick.1 = (bf16[16,80,512]{2,1,0:T(8,128)(2,1)}, f32[4,8,256]{2,1,0:T(8,128)S(1)}) custom-call(s32[1]{0:T(128)} %bitcast.me_ref, bf16[512,640]{1,0:T(8,128)(2,1)S(1)} %all_gather.3.all_ref), custom_call_target="tpu_custom_call" | custom-call | tf_op jit(solution)/shard_map/pick/pallas_call | solution.py:254
  58.7 3.7 %all-to-all-start.1 = ((bf16[16,80,512]{2,1,0:T(8,128)(2,1)}), bf16[16,80,512]{2,1,0:T(8,128)(2,1)S(1)}, u32[]{:S(2)}, u32[]{:S(2)}) async-start(bf16[16,80,512]{2,1,0:T(8,128)(2,1)} %get-tuple-element.10), calls=%async_computation.1 | async-start | bytes 2621440 | tf_op jit(solution)/shard_map/all_to_all | solution.py:233
  62.5 0.0 copy-done.6
  62.5 0.0 copy-done.7
  62.5 0.1 copy.30.home_ref
  62.6 0.0 copy-done.5
  62.6 0.1 copy.28
  62.7 0.1 reshape.24
  62.8 0.0 copy-done.4
  62.8 0.1 copy.27
  62.9 0.1 reshape.23
  63.0 0.1 copy.29.lent_ref
  63.1 20.3 %all-to-all-done.1.x_ref = bf16[16,80,512]{2,1,0:T(8,128)(2,1)S(1)} async-done(((bf16[16,80,512]{2,1,0:T(8,128)(2,1)}), bf16[16,80,512]{2,1,0:T(8,128)(2,1)S(1)}, u32[]{:S(2)}, u32[]{:S(2)}) %all-to-all-start.1) | async-done | bytes 1310752 | tf_op jit(solution)/shard_map/all_to_all | solution.py:233
  83.4 0.0 copy-done
  83.4 0.0 copy-done.1
  83.4 0.0 copy-start.2
  83.4 1.0 copy-done.2
  84.4 0.0 copy-start.3
  84.4 1.0 copy-done.3
  85.4 11.8 %attend.1 = bf16[16,96,512]{2,1,0:T(8,128)(2,1)S(1)} custom-call(s32[64,3]{1,0:T(8,128)S(1)} %copy.29.lent_ref, s32[16,2]{1,0:T(8,128)S(1)} %copy.30.home_ref, bf16[16,80,512]{2,1,0:T(8,128)(2,1)S(1)} %all-to-all-done.1.x_ref, bf16[32,16,1024]{2,1,0:T(8,128)(2,1)S(1)} %copy-done, bf16[32,16,1024]{2,1,0:T(8,128)(2,1)S(1)} %copy-done.1, ...), custom_call_target="tpu_custom_call" | custom-call | tf_op jit(solution)/shard_map/attend/pallas_call | solution.py:270
  97.2 23.2 %all_to_all.21.x_ref = bf16[16,96,512]{2,1,0:T(8,128)(2,1)S(1)} all-to-all(bf16[16,96,512]{2,1,0:T(8,128)(2,1)S(1)} %attend.1), channel_id=1, replica_groups=mesh['inst'=32,'tp'=16] {'tp'}, dimensions={0} | all-to-all | bytes 3145728 | tf_op jit(solution)/shard_map/all_to_all | solution.py:233
  120.4 1.9 %merge.1 = (bf16[32,16,640]{2,1,0:T(8,128)(2,1)S(1)}, f32[16,640]{1,0:T(8,128)S(1)}) custom-call(f32[4,8,256]{2,1,0:T(8,128)S(1)} %get-tuple-element.9.target_ref, bf16[16,96,512]{2,1,0:T(8,128)(2,1)S(1)} %all_to_all.21.x_ref), custom_call_target="tpu_custom_call" | custom-call | tf_op jit(solution)/shard_map/merge/pallas_call | solution.py:293
  122.3 49.2 %all_to_all.22.x_ref = bf16[32,16,640]{2,1,0:T(8,128)(2,1)S(1)} all-to-all(bf16[32,16,640]{2,1,0:T(8,128)(2,1)S(1)} %get-tuple-element.12), channel_id=1, replica_groups=mesh['inst'=32,'tp'=16] {'inst'}, dimensions={0} | all-to-all | bytes 1310720 | tf_op jit(solution)/shard_map/all_to_all | solution.py:233
  171.5 1.1 final.1
  (4 shorter events, 0.0 us)
Async XLA Ops:
  1.5 13.9 %all-to-all-start = ((s32[16,1,64]{2,1,0:T(1,128)}), s32[16,1,64]{2,1,0:T(1,128)S(1)}, u32[]{:S(2)}, u32[]{:S(2)}) async-start(s32[16,1,64]{2,1,0:T(1,128)} %broadcast_in_dim.11), calls=%async_computation | async-start | bytes 16384 | tf_op jit(solution)/shard_map/all_to_all | solution.py:233
  56.1 6.4 %copy-start.6 = (s32[16,1]{0,1:T(1,128)S(1)}, s32[16,1]{0,1:T(1,128)}, u32[]{:S(2)}) copy-start(s32[16,1]{0,1:T(1,128)} %param.14) | copy-start | bytes 196
  56.1 6.4 %copy-start.7 = (s32[16,1,1]{0,2,1:T(1,128)S(1)}, s32[16,1,1]{0,2,1:T(1,128)}, u32[]{:S(2)}) copy-start(s32[16,1,1]{0,2,1:T(1,128)} %param.13) | copy-start | bytes 196
  56.1 6.5 %copy-start.5 = (s32[1,32,1,2]{1,3,2,0:T(2,128)S(1)}, s32[1,32,1,2]{1,3,2,0:T(2,128)}, u32[]{:S(2)}) copy-start(s32[1,32,1,2]{1,3,2,0:T(2,128)} %param.19) | copy-start | bytes 772
  56.1 6.7 %copy-start.4 = (s32[1,32,1,2,2]{1,4,3,2,0:T(2,128)S(1)}, s32[1,32,1,2,2]{1,4,3,2,0:T(2,128)}, u32[]{:S(2)}) copy-start(s32[1,32,1,2,2]{1,4,3,2,0:T(2,128)} %param.18) | copy-start | bytes 1540
  56.1 27.3 %copy-start = (bf16[32,16,1024]{2,1,0:T(8,128)(2,1)S(1)}, bf16[32,16,1024]{2,1,0:T(8,128)(2,1)}, u32[]{:S(2)}) copy-start(bf16[32,16,1024]{2,1,0:T(8,128)(2,1)} %lk_ref.1) | copy-start | bytes 3145732
  56.1 27.3 %copy-start.1 = (bf16[32,16,1024]{2,1,0:T(8,128)(2,1)S(1)}, bf16[32,16,1024]{2,1,0:T(8,128)(2,1)}, u32[]{:S(2)}) copy-start(bf16[32,16,1024]{2,1,0:T(8,128)(2,1)} %lv_ref.1) | copy-start | bytes 3145732
  58.7 24.6 %all-to-all-start.1 = ((bf16[16,80,512]{2,1,0:T(8,128)(2,1)}), bf16[16,80,512]{2,1,0:T(8,128)(2,1)S(1)}, u32[]{:S(2)}, u32[]{:S(2)}) async-start(bf16[16,80,512]{2,1,0:T(8,128)(2,1)} %get-tuple-element.10), calls=%async_computation.1 | async-start | bytes 2621440 | tf_op jit(solution)/shard_map/all_to_all | solution.py:233
  83.4 1.0 copy-start.2
  84.4 1.0 copy-start.3

commit v2 on v1

v2 whole, which is shorter than its diff:
```python
import functools
import math

import jax
import jax.numpy as jnp
import ml_dtypes
import numpy as np
from jax import lax
from jax.experimental import pallas as pl
from jax.experimental.pallas import tpu as pltpu
from jax.sharding import PartitionSpec as P

QH = 64
KVH = 8
HD = 128
N_INST = 32
N_TP = 16
ROWS = 16
SLOTS = 64
WIDTH = 512
GROUPS = 4
SEGS = SLOTS + ROWS
DEAD = -1e30
SCALE = HD ** (-0.5)
F32 = jnp.float32
BF16 = jnp.bfloat16
FACTOR = SCALE * math.log2(math.e)
TWICE_HI = float(np.float32(1 / FACTOR).astype(ml_dtypes.bfloat16))
TWICE_LO = 1 / FACTOR - TWICE_HI
UNROLL = 2


def iota(shape, axis):
    return lax.broadcasted_iota(jnp.int32, shape, axis)


def dot(a, b):
    return jnp.dot(a, b, preferred_element_type=F32)


def dot_nt(a, b):
    return lax.dot_general(a, b, (((1,), (1,)), ((), ())), preferred_element_type=F32)


def split3(x):
    hi = x.astype(BF16).astype(F32)
    rest = x - hi
    mid = rest.astype(BF16).astype(F32)
    return hi, mid, rest - mid


def spread3(x):
    hi, mid, low = split3(x)
    return hi + pltpu.roll(mid, 4, 1) + pltpu.roll(low, 8, 1)


def pick_kernel(me_ref, mine_ref, other_ref, out_ref, target_ref):
    me = me_ref[0]
    k = iota((256, 128), 0)
    n = iota((256, 128), 1)
    local = jnp.bitwise_and(jnp.right_shift(k, 1), 7)
    order = jnp.where(n == local * 16 + jnp.right_shift(k, 4), 1.0, 0.0).astype(BF16)
    second = jnp.bitwise_and(k, 1) == 1
    base = local.astype(F32) * 16.0
    lane = n.astype(F32)
    row = iota((128, 128), 0)
    for g in range(GROUPS):
        source = mine_ref if g < 2 else other_ref
        block = source[(g % 2) * 8 : (g % 2 + 1) * 8].reshape(128, WIDTH + 128)
        asked = block[:, WIDTH:]
        found = []
        for s in range(2):
            column = jnp.where(row == 2 * me + s, 1.0, 0.0).astype(BF16)
            found.append(dot(order, dot(asked, column).astype(BF16)))
        target = jnp.where(second, found[1], found[0]) + base
        onehot = jnp.where(lane == target, 1.0, 0.0).astype(BF16)
        picked = dot(onehot, block[:, :WIDTH]).astype(BF16)
        out_ref[:, g * 16 : (g + 1) * 16, :] = picked.reshape(N_TP, 16, WIDTH)
        target_ref[g] = target.T[:8]
    own = mine_ref[jnp.right_shift(me, 1), :, :WIDTH]
    for t in range(N_TP):
        out_ref[t, SLOTS:, :] = own


def prepare_kernel(
    lent_ref, home_ref, lk_ref, lv_ref, hk_ref, hv_ref, klent_ref, vlent_ref, khome_ref, vhome_ref
):
    token = iota((512, 128), 0)
    block = jnp.right_shift(token, 4)
    place = jnp.bitwise_and(token, 15)
    length = lent_ref[2:3, :]
    first = (block == lent_ref[0:1, :]) & (place < length)
    other = (block == lent_ref[1:2, :]) & (place + 16 < length)
    twice = first & other
    upper = jnp.where(first | other, jnp.where(twice, TWICE_HI, 0.0), DEAD)
    lower = jnp.where(twice, TWICE_LO, 0.0)
    lent_mask = jnp.where(iota((512, 128), 1) < SLOTS, upper, lower).astype(BF16)
    token = iota((256, 128), 0)
    live = (jnp.right_shift(token, 4) == home_ref[0:1, :]) & (
        jnp.bitwise_and(token, 15) < home_ref[1:2, :]
    )
    home_mask = jnp.where(live, 0.0, DEAD).astype(BF16)
    ones = jnp.ones((512, 128), BF16)
    for k in range(KVH):
        cut = slice(k * HD, (k + 1) * HD)
        klent_ref[k, :, :HD] = lk_ref[:, :, cut].reshape(512, HD)
        klent_ref[k, :, HD:] = lent_mask
        vlent_ref[k, :, :HD] = lv_ref[:, :, cut].reshape(512, HD)
        vlent_ref[k, :, HD:] = ones
        khome_ref[k, :, :HD] = hk_ref[:, :, cut].reshape(256, HD)
        khome_ref[k, :, HD:] = home_mask
        vhome_ref[k, :, :HD] = hv_ref[:, :, cut].reshape(256, HD)
        vhome_ref[k, :, HD:] = ones[:256]


def attend_kernel(x_ref, klent_ref, vlent_ref, khome_ref, vhome_ref, out_ref):
    def pool(query, pick, keys, values, count):
        query = jnp.concatenate([query, jnp.concatenate([pick] * 8, axis=0)], axis=1)
        scores = dot_nt(query, keys)
        weights = []
        peaks = []
        for j in range(8):
            part = scores[j * count : (j + 1) * count]
            peak = jnp.max(part, axis=1, keepdims=True)
            weights.append(jnp.exp2((part - peak) * FACTOR).astype(BF16))
            peaks.append(peak)
        mixed = dot(jnp.concatenate(weights, axis=0), values)
        total = mixed[:, HD:]
        return (mixed[:, :HD] / total).astype(BF16), peaks, total

    def stack(k, rows):
        return jnp.concatenate(
            [
                x_ref[2 * k + tt, rows, h * HD : (h + 1) * HD]
                for tt in range(2)
                for h in range(4)
            ],
            axis=0,
        )

    def columns(tt, peaks, total, count):
        lane = iota((count, 128), 1)
        top = jnp.zeros((count, 128), F32)
        amount = jnp.ones((count, 128), F32)
        for h in range(4):
            j = tt * 4 + h
            top = jnp.where(lane == h, peaks[j], top)
            amount = jnp.where(lane == h, total[j * count : (j + 1) * count], amount)
        return jnp.where(top > DEAD / 2, top * SCALE + jnp.log(amount), DEAD)

    lane = iota((SLOTS, 128), 1)
    lent_pick = jnp.where(
        jnp.bitwise_and(lane, SLOTS - 1) == iota((SLOTS, 128), 0), 1.0, 0.0
    ).astype(BF16)
    home_pick = jnp.where(iota((ROWS, 128), 1) == iota((ROWS, 128), 0), 1.0, 0.0).astype(BF16)

    def step(k, carry):
        lent, lent_peaks, lent_total = pool(
            stack(k, slice(0, SLOTS)), lent_pick, klent_ref[k], vlent_ref[k], SLOTS
        )
        home, home_peaks, home_total = pool(
            stack(k, slice(SLOTS, SEGS)), home_pick, khome_ref[k], vhome_ref[k], ROWS
        )
        for tt in range(2):
            for h in range(4):
                j = tt * 4 + h
                at = h * SEGS
                out_ref[2 * k + tt, at : at + SLOTS, :] = lent[j * SLOTS : (j + 1) * SLOTS]
                out_ref[2 * k + tt, at + SLOTS : at + SEGS, :] = home[j * ROWS : (j + 1) * ROWS]
            column = jnp.concatenate(
                [
                    columns(tt, lent_peaks, lent_total, SLOTS),
                    columns(tt, home_peaks, home_total, ROWS),
                    jnp.zeros((128 - SEGS, 128), F32),
                ],
                axis=0,
            )
            column = jnp.where(iota((128, 128), 1) < 4, column, 0.0)
            out_ref[2 * k + tt, 4 * SEGS :, :] = spread3(column).T[:16].astype(BF16)
        return carry

    lax.fori_loop(0, KVH, step, 0, unroll=UNROLL)


def merge_kernel(target_ref, x_ref, keep_ref, give_ref, home_ref):
    lane = iota((8, 128), 1)
    lses = []
    for t in range(N_TP):
        parts = x_ref[t, 4 * SEGS :, :].astype(F32)
        lses.append(parts[0:4] + parts[4:8] + parts[8:12])
    lses = [jnp.concatenate([x, x], axis=0) for x in lses]
    for g in range(GROUPS + 1):
        halves = []
        for half in range(2):
            row = jnp.zeros((8, 128), F32)
            for j in range(8):
                shift = (16 * j - 16 * g) % 128
                moved = lses[half * 8 + j]
                moved = pltpu.roll(moved, shift, 1) if shift else moved
                row = jnp.where(jnp.right_shift(lane, 4) == j, moved, row)
            halves.append(row)
        lse = jnp.concatenate(halves, axis=1)
        high = 128 if g < GROUPS else ROWS
        rows = iota((high, 256), 0)
        if g < GROUPS:
            mask = rows.astype(F32) == target_ref[g, 0:1, :]
        else:
            mask = rows == jnp.bitwise_and(iota((high, 256), 1), 15)
        out_lse = jnp.zeros((high, 128), F32)
        out_lane = iota((high, 128), 1)
        mixed = []
        for h in range(4):
            at = h * SEGS + 16 * g
            values = x_ref[:, at : at + 16, :].reshape(256, HD)
            score = jnp.where(mask, lse[h : h + 1, :], DEAD)
            peak = jnp.max(score, axis=1, keepdims=True)
            weight = jnp.exp(score - peak)
            total = jnp.sum(weight, axis=1, keepdims=True)
            upper = weight.astype(BF16)
            lower = (weight - upper.astype(F32)).astype(BF16)
            both = dot(jnp.concatenate([upper, lower], axis=0), values)
            mixed.append((both[:high] + both[high:]) / total)
            out_lse = jnp.where(out_lane == h, peak + jnp.log(total), out_lse)
        mixed = jnp.concatenate(mixed + [out_lse], axis=1)
        if g < GROUPS:
            result = keep_ref if g < 2 else give_ref
            result[(g % 2) * 8 : (g % 2 + 1) * 8] = mixed.reshape(8, ROWS, WIDTH + 128)
        else:
            home_ref[...] = mixed


def join_kernel(keep_ref, come_ref, out_ref):
    for z in range(N_INST // 2):
        ours = keep_ref[z, :, WIDTH:]
        theirs = come_ref[z, :, WIDTH:]
        peak = jnp.maximum(ours, theirs)
        first = jnp.exp(ours - peak)
        second = jnp.exp(theirs - peak)
        total = first + second
        first = first / total
        second = second / total
        for h in range(4):
            cut = slice(h * HD, (h + 1) * HD)
            out_ref[z, :, cut] = (
                first[:, h : h + 1] * keep_ref[z, :, cut]
                + second[:, h : h + 1] * come_ref[z, :, cut]
            ).astype(BF16)
        lse = jnp.where(iota((ROWS, 128), 1) < 4, peak + jnp.log(total), 0.0)
        out_ref[z, :, WIDTH:] = spread3(lse).astype(BF16)


def final_kernel(home_ref, x_ref, out_ref):
    pieces = x_ref.shape[0]
    lses = [home_ref[:, WIDTH:]]
    for c in range(pieces):
        parts = x_ref[c, :, WIDTH:].astype(F32)
        lses.append(parts + pltpu.roll(parts, 124, 1) + pltpu.roll(parts, 120, 1))
    peak = functools.reduce(jnp.maximum, lses)
    weights = [jnp.exp(lse - peak) for lse in lses]
    total = sum(weights)
    for h in range(4):
        cut = slice(h * HD, (h + 1) * HD)
        mixed = weights[0][:, h : h + 1] * home_ref[:, cut]
        for c in range(pieces):
            mixed = mixed + weights[c + 1][:, h : h + 1] * x_ref[c, :, cut].astype(F32)
        out_ref[:, cut] = (mixed / total[:, h : h + 1]).astype(BF16)


VMEM = pl.BlockSpec(memory_space=pltpu.VMEM)
SMEM = pl.BlockSpec(memory_space=pltpu.SMEM)
PARAMS = pltpu.CompilerParams(vmem_limit_bytes=48 * 1024 * 1024)


def exchange(x, axis, groups=None):
    return lax.all_to_all(
        x, axis, split_axis=0, concat_axis=0, axis_index_groups=groups, tiled=True
    )


def call(kernel, name, out_shape, args, smem=0):
    specs = [SMEM] * smem + [VMEM] * (len(args) - smem)
    outs = jax.tree.map(lambda _: VMEM, out_shape)
    return pl.pallas_call(
        kernel,
        out_shape=out_shape,
        in_specs=specs,
        out_specs=outs,
        compiler_params=PARAMS,
        name=name,
    )(*args)


def per_device(
    queries,
    home_keys,
    home_values,
    home_table,
    home_len,
    lent_keys,
    lent_values,
    lend_row,
    lend_table,
    lend_len,
):
    chips = N_INST // 2
    same_core = [[2 * z + core for z in range(chips)] for core in range(2)]
    sibling = [(i, i ^ 1) for i in range(N_INST)]
    wide = WIDTH + 128
    me = lax.axis_index("inst").astype(jnp.int32)
    core = jnp.bitwise_and(me, 1)

    asked = exchange(jnp.broadcast_to(lend_row.reshape(1, SLOTS), (N_TP, SLOTS)), "tp")
    sent = jnp.concatenate(
        [queries, asked.astype(BF16), jnp.zeros((ROWS, 128 - SLOTS), BF16)], axis=1
    )
    mine = exchange(jnp.broadcast_to(sent[None], (chips, ROWS, wide)), "inst", same_core)
    other = lax.ppermute(mine, "inst", sibling)
    picked, target = call(
        pick_kernel,
        "pick",
        (
            jax.ShapeDtypeStruct((N_TP, SEGS, WIDTH), BF16),
            jax.ShapeDtypeStruct((GROUPS, 8, 256), F32),
        ),
        (me.reshape(1), mine, other),
        smem=1,
    )
    arrived = exchange(picked, "tp")

    meta = jnp.concatenate(
        [lend_table.reshape(chips, 2, 2, 2), lend_len.reshape(chips, 2, 2, 1)], axis=3
    )
    meta = jnp.stack([meta, meta[:, ::-1]])[core].transpose(3, 1, 0, 2).reshape(3, SLOTS)
    lent_meta = jnp.concatenate([meta, meta], axis=1)
    home_meta = jnp.concatenate([home_table.reshape(ROWS, 1), home_len], axis=1).T
    home_meta = jnp.pad(home_meta, ((0, 0), (0, 128 - ROWS)), constant_values=16)
    pools = call(
        prepare_kernel,
        "prepare",
        tuple(jax.ShapeDtypeStruct((KVH, n, 2 * HD), BF16) for n in (512, 512, 256, 256)),
        (lent_meta, home_meta, lent_keys, lent_values, home_keys, home_values),
    )
    partial = call(
        attend_kernel,
        "attend",
        jax.ShapeDtypeStruct((N_TP, 4 * SEGS + 16, HD), BF16),
        (arrived, *pools),
    )
    returned = exchange(partial, "tp")
    keep, give, home = call(
        merge_kernel,
        "merge",
        (
            jax.ShapeDtypeStruct((chips, ROWS, wide), F32),
            jax.ShapeDtypeStruct((chips, ROWS, wide), F32),
            jax.ShapeDtypeStruct((ROWS, wide), F32),
        ),
        (target, returned),
    )
    come = lax.ppermute(give, "inst", sibling)
    joined = call(
        join_kernel, "join", jax.ShapeDtypeStruct((chips, ROWS, wide), BF16), (keep, come)
    )
    back = exchange(joined, "inst", same_core)
    return call(
        final_kernel, "final", jax.ShapeDtypeStruct((ROWS, WIDTH), BF16), (home, back)
    )


def solution(mesh):
    in_specs = (
        P("inst", "tp"),
        P(("inst", "tp"), None, None),
        P(("inst", "tp"), None, None),
        P("inst", "tp", None),
        P("inst", "tp"),
        P(("inst", "tp"), None, None),
        P(("inst", "tp"), None, None),
        P("inst", None, "tp", None),
        P("inst", None, "tp", None, None),
        P("inst", None, "tp", None),
    )
    out_specs = P("inst", "tp")
    return jax.shard_map(
        per_device, mesh=mesh, in_specs=in_specs, out_specs=out_specs, check_vma=False
    )
```

time: 173 us -> 150 us (0.87)
  the two profiles are of different devices: /device:TPU:1 before, /device:TPU:32 now
where the time goes in v2:
time: 150 us; the launch traced here: 149 us
  blocking collectives  83.7 us (56%)
  waiting for transfers between devices  24.7 us (16%)
  Pallas kernels  16.4 us (11%)
  starting transfers between devices  14.7 us (10%)
  local copies, waits for them, and re-layouts  8.68 us (6%)
    all_to_all x3, blocking collectives, exchange(): lax.all_to_all(x, axis, split_axis=0, concat_axis=0, axis_index_groups=gr...  83.7 us
    all_to_all x2, waiting for transfers between devices, exchange(): lax.all_to_all(x, axis, split_axis=0, concat_axis=0, axis_index_groups=gr...  21 us
    pallas_call x6, Pallas kernels, call(): pl.pallas_call(kernel, out_shape=out_shape, in_specs=specs, out_specs=out...  16.4 us
    all_to_all x2, starting transfers between devices, exchange(): lax.all_to_all(x, axis, split_axis=0, concat_axis=0, axis_index_groups=gr...  10.9 us
    unnamed x25, local copies, waits for them, and re-layouts  7.27 us
  transfers between devices with their start and end apart: 4, of which 4 were waited for; matrix products, arithmetic and copies ran while one was open for 1% of the time, Pallas kernels for 2%

profile of v2, /device:TPU:32, one launch (start us, length us, event | category | flops | bytes accessed | tf_op | source)
XLA Modules:
  0.0 149.2 jit_solution(16212678384437976825)
XLA Ops:
  0.0 0.8 copy.21
  0.8 0.1 broadcast_in_dim.16
  0.9 0.6 broadcast_in_dim.17
  1.5 7.0 %all-to-all-start = ((s32[16,1,64]{2,1,0:T(1,128)}), s32[16,1,64]{2,1,0:T(1,128)S(1)}, u32[]{:S(2)}, u32[]{:S(2)}) async-start(s32[16,1,64]{2,1,0:T(1,128)} %broadcast_in_dim.17), calls=%async_computation | async-start | bytes 16384 | tf_op jit(solution)/shard_map/all_to_all | solution.py:275
  8.5 0.1 pad.15.clone
  8.6 7.4 %all-to-all-done = s32[16,1,64]{2,1,0:T(1,128)S(1)} async-done(((s32[16,1,64]{2,1,0:T(1,128)}), s32[16,1,64]{2,1,0:T(1,128)S(1)}, u32[]{:S(2)}, u32[]{:S(2)}) %all-to-all-start) | async-done | bytes 4128 | tf_op jit(solution)/shard_map/all_to_all | solution.py:275
  16.0 0.7 maximum_maximum_fusion
  16.8 34.1 %all_to_all.26.mine_ref = bf16[16,16,640]{2,1,0:T(8,128)(2,1)S(1)} all-to-all(bf16[16,16,640]{2,1,0:T(8,128)(2,1)S(1)} %broadcast_in_dim.19), channel_id=1, replica_groups={{0,32,64,96,128,160,192,224,256,288,320,352,384,416,448,480},{16,48,80,..., dimensions={0} | all-to-all | bytes 655360 | tf_op jit(solution)/shard_map/all_to_all | solution.py:275
  50.9 1.9 %collective-permute-start = (bf16[16,16,640]{2,1,0:T(8,128)(2,1)S(1)}, bf16[16,16,640]{2,1,0:T(8,128)(2,1)S(1)}, u32[]{:S(2)}, u32[]{:S(2)}) collective-permute-start(bf16[16,16,640]{2,1,0:T(8,128)(2,1)S(1)} %all_to_all.26.mine_ref), channel_id=1, source_target_pairs={{0,16},{16,0},{32,48},{48,32},{64,80},{80,64},{96,112},{112,96},{1... | collective-permute-start | bytes 983048 | tf_op jit(solution)/shard_map/ppermute | solution.py:317
  52.8 1.6 %collective-permute-done.other_ref = bf16[16,16,640]{2,1,0:T(8,128)(2,1)S(1)} collective-permute-done((bf16[16,16,640]{2,1,0:T(8,128)(2,1)S(1)}, bf16[16,16,640]{2,1,0:T(8,128)(2,1)S(1)}, u32[]{:S(2)}, u32[]{:S(2)}) %collective-permute-start) | collective-permute-done | bytes 327712 | tf_op jit(solution)/shard_map/ppermute | solution.py:317
  54.4 2.6 %pick.1 = (bf16[16,80,512]{2,1,0:T(8,128)(2,1)}, f32[4,8,256]{2,1,0:T(8,128)S(1)}) custom-call(s32[1]{0:T(128)} %bitcast.me_ref, bf16[16,16,640]{2,1,0:T(8,128)(2,1)S(1)} %all_to_all.26.mine_ref, bf16[16,16,640]{2,1,0:T(8,128)(2,1)S(1)} %collective-permute-done.other_ref), custom_call_target="tpu_custom_call" | custom-call | tf_op jit(solution)/shard_map/pick/pallas_call | solution.py:283
  57.0 0.0 copy-start.9
  57.0 0.0 copy-start.8
  57.0 0.0 copy-start.10
  57.0 0.0 copy-start.11
  57.0 0.0 copy-start
  57.1 0.0 copy-start.1
  57.1 3.8 %all-to-all-start.2 = ((bf16[16,80,512]{2,1,0:T(8,128)(2,1)}), bf16[16,80,512]{2,1,0:T(8,128)(2,1)S(1)}, u32[]{:S(2)}, u32[]{:S(2)}) async-start(bf16[16,80,512]{2,1,0:T(8,128)(2,1)} %get-tuple-element.15), calls=%async_computation.2 | async-start | bytes 2621440 | tf_op jit(solution)/shard_map/all_to_all | solution.py:275
  60.9 0.0 copy-done.9
  60.9 0.1 reshape.28
  61.0 0.1 copy.24
  61.1 0.0 copy-done.8
  61.1 0.1 reshape.27
  61.2 0.1 copy.23
  61.4 0.1 copy.25
  61.5 0.1 reshape.29
  61.6 0.0 copy-done.10
  61.6 0.0 copy-done.11
  61.6 0.1 pad_add_fusion.1.lent_ref
  61.7 0.0 copy-done
  61.7 0.0 copy-done.1
  61.7 0.0 copy-start.6
  61.7 1.0 copy-done.6
  62.7 1.0 copy-done.7
  63.8 3.1 %prepare.1 = (bf16[8,512,256]{2,1,0:T(8,128)(2,1)}, bf16[8,512,256]{2,1,0:T(8,128)(2,1)}, bf16[8,256,256]{2,1,0:T(8,128)(2,1)S(1)}, bf16[8,256,256]{2,1,0:T(8,128)(2,1)S(1)}) custom-call(s32[3,128]{1,0:T(4,128)S(1)} %pad_add_fusion.1.lent_ref, s32[2,128]{1,0:T(2,128)S(1)} %pad.4.home_ref, bf16[32,16,1024]{2,1,0:T(8,128)(2,1)S(1)} %copy-done, ...), custom_call_target="tpu_custom_call" | custom-call | tf_op jit(solution)/shard_map/prepare/pallas_call | solution.py:283
  66.9 1.0 copy-done.2
  67.9 1.0 copy-done.4
  68.8 13.6 %all-to-all-done.2.x_ref = bf16[16,80,512]{2,1,0:T(8,128)(2,1)S(1)} async-done(((bf16[16,80,512]{2,1,0:T(8,128)(2,1)}), bf16[16,80,512]{2,1,0:T(8,128)(2,1)S(1)}, u32[]{:S(2)}, u32[]{:S(2)}) %all-to-all-start.2) | async-done | bytes 1310752 | tf_op jit(solution)/shard_map/all_to_all | solution.py:275
  82.4 1.2 copy-done.3
  83.6 1.2 copy-done.5
  84.9 7.9 %attend.1 = bf16[16,336,128]{2,1,0:T(8,128)(2,1)S(1)} custom-call(bf16[16,80,512]{2,1,0:T(8,128)(2,1)S(1)} %all-to-all-done.2.x_ref, bf16[8,512,256]{2,1,0:T(8,128)(2,1)} %get-tuple-element.16.klent_ref, bf16[8,512,256]{2,1,0:T(8,128)(2,1)} %get-tuple-element.17.vlent_ref, bf16[8,256,256]{2,1,0:T(8,128)(2,1)S(1)} %copy-done.3, bf16[8,256,256]{2,1,0:T(8,128)(2,1)S(1)} %copy-done.5), custom_call_target="tpu_custom_call" | custom-call | tf_op jit(solution)/shard_map/attend/pallas_call | solution.py:283
  92.7 22.8 %all_to_all.27.x_ref = bf16[16,336,128]{2,1,0:T(8,128)(2,1)S(1)} all-to-all(bf16[16,336,128]{2,1,0:T(8,128)(2,1)S(1)} %attend.1), channel_id=1, replica_groups=mesh['inst'=32,'tp'=16] {'tp'}, dimensions={0} | all-to-all | bytes 2752512 | tf_op jit(solution)/shard_map/all_to_all | solution.py:275
  115.5 1.4 merge.1
  116.9 1.9 %collective-permute-start.1 = (f32[16,16,640]{2,1,0:T(8,128)S(1)}, f32[16,16,640]{2,1,0:T(8,128)S(1)}, u32[]{:S(2)}, u32[]{:S(2)}) collective-permute-start(f32[16,16,640]{2,1,0:T(8,128)S(1)} %get-tuple-element.22), channel_id=1, source_target_pairs={{0,16},{16,0},{32,48},{48,32},{64,80},{80,64},{96,112},{112,96},{1... | collective-permute-start | bytes 1966088 | tf_op jit(solution)/shard_map/ppermute | solution.py:360
  118.8 2.1 %collective-permute-done.1.come_ref = f32[16,16,640]{2,1,0:T(8,128)S(1)} collective-permute-done((f32[16,16,640]{2,1,0:T(8,128)S(1)}, f32[16,16,640]{2,1,0:T(8,128)S(1)}, u32[]{:S(2)}, u32[]{:S(2)}) %collective-permute-start.1) | collective-permute-done | bytes 655392 | tf_op jit(solution)/shard_map/ppermute | solution.py:360
  120.9 0.5 join.1
  121.4 26.8 %all_to_all.28.x_ref = bf16[16,16,640]{2,1,0:T(8,128)(2,1)S(1)} all-to-all(bf16[16,16,640]{2,1,0:T(8,128)(2,1)S(1)} %join.1), channel_id=1, replica_groups={{0,32,64,96,128,160,192,224,256,288,320,352,384,416,448,480},{16,48,80,..., dimensions={0} | all-to-all | bytes 655360 | tf_op jit(solution)/shard_map/all_to_all | solution.py:275
  148.2 0.9 final.1
  (13 shorter events, 0.1 us)
Async XLA Ops:
  1.5 14.5 %all-to-all-start = ((s32[16,1,64]{2,1,0:T(1,128)}), s32[16,1,64]{2,1,0:T(1,128)S(1)}, u32[]{:S(2)}, u32[]{:S(2)}) async-start(s32[16,1,64]{2,1,0:T(1,128)} %broadcast_in_dim.17), calls=%async_computation | async-start | bytes 16384 | tf_op jit(solution)/shard_map/all_to_all | solution.py:275
  50.9 3.5 %collective-permute-start = (bf16[16,16,640]{2,1,0:T(8,128)(2,1)S(1)}, bf16[16,16,640]{2,1,0:T(8,128)(2,1)S(1)}, u32[]{:S(2)}, u32[]{:S(2)}) collective-permute-start(bf16[16,16,640]{2,1,0:T(8,128)(2,1)S(1)} %all_to_all.26.mine_ref), channel_id=1, source_target_pairs={{0,16},{16,0},{32,48},{48,32},{64,80},{80,64},{96,112},{112,96},{1... | collective-permute-start | bytes 983048 | tf_op jit(solution)/shard_map/ppermute | solution.py:317
  57.0 3.9 %copy-start.9 = (s32[1,32,1,2]{1,3,2,0:T(2,128)S(1)}, s32[1,32,1,2]{1,3,2,0:T(2,128)}, u32[]{:S(2)}) copy-start(s32[1,32,1,2]{1,3,2,0:T(2,128)} %param.19) | copy-start | bytes 772
  57.0 4.1 %copy-start.8 = (s32[1,32,1,2,2]{1,4,3,2,0:T(2,128)S(1)}, s32[1,32,1,2,2]{1,4,3,2,0:T(2,128)}, u32[]{:S(2)}) copy-start(s32[1,32,1,2,2]{1,4,3,2,0:T(2,128)} %param.18) | copy-start | bytes 1540
  57.0 4.5 %copy-start.10 = (s32[16,1]{0,1:T(1,128)S(1)}, s32[16,1]{0,1:T(1,128)}, u32[]{:S(2)}) copy-start(s32[16,1]{0,1:T(1,128)} %param.14) | copy-start | bytes 196
  57.0 4.6 %copy-start.11 = (s32[16,1,1]{0,2,1:T(1,128)S(1)}, s32[16,1,1]{0,2,1:T(1,128)}, u32[]{:S(2)}) copy-start(s32[16,1,1]{0,2,1:T(1,128)} %param.13) | copy-start | bytes 196
  57.0 4.7 %copy-start = (bf16[32,16,1024]{2,1,0:T(8,128)(2,1)S(1)}, bf16[32,16,1024]{2,1,0:T(8,128)(2,1)}, u32[]{:S(2)}) copy-start(bf16[32,16,1024]{2,1,0:T(8,128)(2,1)} %lk_ref.1) | copy-start | bytes 3145732
  57.1 4.7 %copy-start.1 = (bf16[32,16,1024]{2,1,0:T(8,128)(2,1)S(1)}, bf16[32,16,1024]{2,1,0:T(8,128)(2,1)}, u32[]{:S(2)}) copy-start(bf16[32,16,1024]{2,1,0:T(8,128)(2,1)} %lv_ref.1) | copy-start | bytes 3145732
  57.1 25.4 %all-to-all-start.2 = ((bf16[16,80,512]{2,1,0:T(8,128)(2,1)}), bf16[16,80,512]{2,1,0:T(8,128)(2,1)S(1)}, u32[]{:S(2)}, u32[]{:S(2)}) async-start(bf16[16,80,512]{2,1,0:T(8,128)(2,1)} %get-tuple-element.15), calls=%async_computation.2 | async-start | bytes 2621440 | tf_op jit(solution)/shard_map/all_to_all | solution.py:275
  61.7 1.0 copy-start.6
  62.7 1.0 copy-start.7
  66.9 1.0 copy-start.2
  67.9 1.0 copy-start.4
  82.4 1.2 copy-start.3
  83.6 1.2 copy-start.5
  116.9 4.0 %collective-permute-start.1 = (f32[16,16,640]{2,1,0:T(8,128)S(1)}, f32[16,16,640]{2,1,0:T(8,128)S(1)}, u32[]{:S(2)}, u32[]{:S(2)}) collective-permute-start(f32[16,16,640]{2,1,0:T(8,128)S(1)} %get-tuple-element.22), channel_id=1, source_target_pairs={{0,16},{16,0},{32,48},{48,32},{64,80},{80,64},{96,112},{112,96},{1... | collective-permute-start | bytes 1966088 | tf_op jit(solution)/shard_map/ppermute | solution.py:360

commit v3 on v2

v3 whole, which is shorter than its diff:
```python
import functools
import math

import jax
import jax.numpy as jnp
import ml_dtypes
import numpy as np
from jax import lax
from jax.experimental import pallas as pl
from jax.experimental.pallas import tpu as pltpu
from jax.sharding import PartitionSpec as P

QH = 64
KVH = 8
HD = 128
N_INST = 32
N_TP = 16
ROWS = 16
SLOTS = 64
WIDTH = 512
CHIPS = N_INST // 2
HALF = SLOTS // 2
PIECE = 4 * HALF + 2 * ROWS + 16
DEAD = -1e30
SCALE = HD ** (-0.5)
F32 = jnp.float32
BF16 = jnp.bfloat16
FACTOR = SCALE * math.log2(math.e)
TWICE_HI = float(np.float32(1 / FACTOR).astype(ml_dtypes.bfloat16))
TWICE_LO = 1 / FACTOR - TWICE_HI
UNROLL = 8


def iota(shape, axis):
    return lax.broadcasted_iota(jnp.int32, shape, axis)


def dot(a, b):
    return jnp.dot(a, b, preferred_element_type=F32)


def dot_nt(a, b):
    return lax.dot_general(a, b, (((1,), (1,)), ((), ())), preferred_element_type=F32)


def split3(x):
    hi = x.astype(BF16).astype(F32)
    rest = x - hi
    mid = rest.astype(BF16).astype(F32)
    return hi, mid, rest - mid


def spread3(x):
    hi, mid, low = split3(x)
    return hi + pltpu.roll(mid, 4, 1) + pltpu.roll(low, 8, 1)


def spread_kernel(queries_ref, first_ref, out_ref):
    row = iota((ROWS, 128), 0)
    asked = jnp.zeros((ROWS, 128), F32)
    for t in range(N_TP):
        asked = jnp.where(row == t, first_ref[t, :, WIDTH:].astype(F32), asked)
    block = jnp.concatenate([queries_ref[...], asked.astype(BF16)], axis=1)
    for z in range(CHIPS):
        out_ref[z] = block


def pick_kernel(me_ref, mine_ref, out_ref, target_ref):
    chip = jnp.right_shift(me_ref[0], 1)
    k = iota((256, 128), 0)
    n = iota((256, 128), 1)
    local = jnp.bitwise_and(jnp.right_shift(k, 1), 7)
    order = jnp.where(n == local * 16 + jnp.right_shift(k, 4), 1.0, 0.0).astype(BF16)
    second = jnp.bitwise_and(k, 1) == 1
    base = local.astype(F32) * 16.0
    lane = n.astype(F32)
    row = iota((128, 128), 0)
    for g in range(2):
        block = mine_ref[g * 8 : (g + 1) * 8].reshape(128, WIDTH + 128)
        asked = dot(order, block[:, WIDTH:]).astype(BF16)
        for d in range(2):
            found = []
            for s in range(2):
                column = jnp.where(row == 4 * chip + 2 * d + s, 1.0, 0.0).astype(BF16)
                found.append(dot(asked, column))
            target = jnp.where(second, found[1], found[0]) + base
            onehot = jnp.where(lane == target, 1.0, 0.0).astype(BF16)
            picked = dot(onehot, block[:, :WIDTH]).astype(BF16)
            out_ref[d * N_TP : (d + 1) * N_TP, g * 16 : (g + 1) * 16, :] = picked.reshape(
                N_TP, 16, WIDTH
            )
            target_ref[g, :, d * 256 : (d + 1) * 256] = target.T[:8]


def prepare_kernel(
    lent_ref, home_ref, lk_ref, lv_ref, hk_ref, hv_ref, klent_ref, vlent_ref, khome_ref, vhome_ref
):
    token = iota((512, 128), 0)
    block = jnp.right_shift(token, 4)
    place = jnp.bitwise_and(token, 15)
    length = lent_ref[2:3, :]
    first = (block == lent_ref[0:1, :]) & (place < length)
    other = (block == lent_ref[1:2, :]) & (place + 16 < length)
    twice = first & other
    upper = jnp.where(first | other, jnp.where(twice, TWICE_HI, 0.0), DEAD)
    lower = jnp.where(twice, TWICE_LO, 0.0)
    lent_mask = jnp.where(iota((512, 128), 1) < SLOTS, upper, lower).astype(BF16)
    token = iota((256, 128), 0)
    live = (jnp.right_shift(token, 4) == home_ref[0:1, :]) & (
        jnp.bitwise_and(token, 15) < home_ref[1:2, :]
    )
    home_mask = jnp.where(live, 0.0, DEAD).astype(BF16)
    ones = jnp.ones((512, 128), BF16)
    for k in range(KVH):
        cut = slice(k * HD, (k + 1) * HD)
        klent_ref[k, :, :HD] = lk_ref[:, :, cut].reshape(512, HD)
        klent_ref[k, :, HD:] = lent_mask
        vlent_ref[k, :, :HD] = lv_ref[:, :, cut].reshape(512, HD)
        vlent_ref[k, :, HD:] = ones
        khome_ref[k, :, :HD] = hk_ref[:, :, cut].reshape(256, HD)
        khome_ref[k, :, HD:] = home_mask
        vhome_ref[k, :, :HD] = hv_ref[:, :, cut].reshape(256, HD)
        vhome_ref[k, :, HD:] = ones[:256]


def attend_kernel(x_ref, first_ref, klent_ref, vlent_ref, khome_ref, vhome_ref, out_ref):
    def pool(query, pick, keys, values, count):
        query = jnp.concatenate([query, jnp.concatenate([pick] * 8, axis=0)], axis=1)
        scores = dot_nt(query, keys)
        weights = []
        peaks = []
        for j in range(8):
            part = scores[j * count : (j + 1) * count]
            peak = jnp.max(part, axis=1, keepdims=True)
            weights.append(jnp.exp2((part - peak) * FACTOR).astype(BF16))
            peaks.append(peak)
        mixed = dot(jnp.concatenate(weights, axis=0), values)
        total = mixed[:, HD:]
        return (mixed[:, :HD] / total).astype(BF16), peaks, total

    def columns(tt, peaks, total, count):
        lane = iota((count, 128), 1)
        top = jnp.zeros((count, 128), F32)
        amount = jnp.ones((count, 128), F32)
        for h in range(4):
            j = tt * 4 + h
            top = jnp.where(lane == h, peaks[j], top)
            amount = jnp.where(lane == h, total[j * count : (j + 1) * count], amount)
        return jnp.where(top > DEAD / 2, top * SCALE + jnp.log(amount), DEAD)

    lane = iota((SLOTS, 128), 1)
    lent_pick = jnp.where(
        jnp.bitwise_and(lane, SLOTS - 1) == iota((SLOTS, 128), 0), 1.0, 0.0
    ).astype(BF16)
    home_pick = jnp.where(iota((ROWS, 128), 1) == iota((ROWS, 128), 0), 1.0, 0.0).astype(BF16)
    heads = [(tt, h) for tt in range(2) for h in range(4)]

    def step(k, carry):
        query = [
            x_ref[d * N_TP + 2 * k + tt, :, h * HD : (h + 1) * HD]
            for tt, h in heads
            for d in range(2)
        ]
        lent, lent_peaks, lent_total = pool(
            jnp.concatenate(query, axis=0), lent_pick, klent_ref[k], vlent_ref[k], SLOTS
        )
        query = [first_ref[2 * k + tt, :, h * HD : (h + 1) * HD] for tt, h in heads]
        home, home_peaks, home_total = pool(
            jnp.concatenate(query, axis=0), home_pick, khome_ref[k], vhome_ref[k], ROWS
        )
        for tt in range(2):
            lent_lse = columns(tt, lent_peaks, lent_total, SLOTS)
            home_lse = columns(tt, home_peaks, home_total, ROWS)
            rest = jnp.zeros((ROWS, 128), F32)
            column = jnp.concatenate(
                [lent_lse[:HALF], home_lse, rest, lent_lse[HALF:], home_lse, rest], axis=0
            )
            column = jnp.where(iota((128, 128), 1) < 4, column, 0.0)
            lse = spread3(column).T[:16]
            for d in range(2):
                to = d * N_TP + 2 * k + tt
                for h in range(4):
                    at = (tt * 4 + h) * SLOTS + d * HALF
                    out_ref[to, h * HALF : (h + 1) * HALF, :] = lent[at : at + HALF]
                for hh in range(2):
                    at = (tt * 4 + 2 * d + hh) * ROWS
                    to_row = 4 * HALF + hh * ROWS
                    out_ref[to, to_row : to_row + ROWS, :] = home[at : at + ROWS]
                out_ref[to, PIECE - 16 :, :] = (pltpu.roll(lse, 64, 1) if d else lse).astype(BF16)
        return carry

    lax.fori_loop(0, KVH, step, 0, unroll=UNROLL)


def merge_kernel(me_ref, target_ref, x_ref, out_ref, keep_ref, give_ref):
    core = jnp.bitwise_and(me_ref[0], 1)
    lane = iota((8, 128), 1)
    lses = []
    for t in range(2 * N_TP):
        parts = x_ref[t, PIECE - 16 :, :].astype(F32)
        lses.append(parts[0:4] + parts[4:8] + parts[8:12])
    lses = [jnp.concatenate([x, x], axis=0) for x in lses]

    def gather(sources, first):
        chunks = []
        for at in range(0, len(sources), 8):
            row = jnp.zeros((8, 128), F32)
            for j in range(8):
                shift = (16 * j - first) % 128
                moved = lses[sources[at + j]]
                moved = pltpu.roll(moved, shift, 1) if shift else moved
                row = jnp.where(jnp.right_shift(lane, 4) == j, moved, row)
            chunks.append(row)
        return jnp.concatenate(chunks, axis=1)

    def join(mask, lse, values):
        score = jnp.where(mask, lse, DEAD)
        peak = jnp.max(score, axis=1, keepdims=True)
        weight = jnp.exp(score - peak)
        total = jnp.sum(weight, axis=1, keepdims=True)
        upper = weight.astype(BF16)
        lower = (weight - upper.astype(F32)).astype(BF16)
        both = dot(jnp.concatenate([upper, lower], axis=0), values)
        count = mask.shape[0]
        return (both[:count] + both[count:]) / total, peak + jnp.log(total)

    rows = iota((128, 512), 0).astype(F32)
    out_lane = iota((128, 128), 1)
    for g in range(2):
        lse = gather(list(range(2 * N_TP)), 16 * g)
        mask = rows == target_ref[g, 0:1, :]
        out_lse = jnp.zeros((128, 128), F32)
        block = slice(g * 8, (g + 1) * 8)
        for h in range(4):
            at = h * HALF + 16 * g
            values = x_ref[:, at : at + 16, :].reshape(512, HD)
            mixed, total = join(mask, lse[h : h + 1, :], values)
            out_lse = jnp.where(out_lane == h, total, out_lse)
            out_ref[block, :, h * HD : (h + 1) * HD] = mixed.astype(BF16).reshape(8, ROWS, HD)
        out_ref[block, :, WIDTH:] = spread3(out_lse).astype(BF16).reshape(8, ROWS, 128)
    mask = iota((ROWS, 256), 0) == jnp.bitwise_and(iota((ROWS, 256), 1), 15)
    home_lane = iota((ROWS, 128), 1)
    homes = []
    for d in range(2):
        lse = gather(list(range(d * N_TP, (d + 1) * N_TP)), HALF)
        lse = jnp.where(core == 0, lse[0:2], lse[2:4])
        out_lse = jnp.zeros((ROWS, 128), F32)
        parts = []
        for hh in range(2):
            at = 4 * HALF + hh * ROWS
            values = x_ref[d * N_TP : (d + 1) * N_TP, at : at + ROWS, :].reshape(256, HD)
            mixed, total = join(mask, lse[hh : hh + 1, :], values)
            parts.append(mixed)
            out_lse = jnp.where(home_lane == hh, total, out_lse)
        homes.append(jnp.concatenate(parts + [out_lse], axis=1))
    keep_ref[...] = jnp.where(core == 0, homes[0], homes[1])
    give_ref[...] = jnp.where(core == 0, homes[1], homes[0])


def final_kernel(me_ref, keep_ref, come_ref, x_ref, out_ref):
    core = jnp.bitwise_and(me_ref[0], 1)
    low = jnp.where(core == 0, keep_ref[...], come_ref[...])
    high = jnp.where(core == 0, come_ref[...], keep_ref[...])
    lane = iota((ROWS, 128), 1)
    lses = [jnp.where(lane < 2, low[:, 2 * HD :], pltpu.roll(high[:, 2 * HD :], 2, 1))]
    for c in range(CHIPS):
        parts = x_ref[c, :, WIDTH:].astype(F32)
        lses.append(parts + pltpu.roll(parts, 124, 1) + pltpu.roll(parts, 120, 1))
    peak = functools.reduce(jnp.maximum, lses)
    weights = [jnp.exp(lse - peak) for lse in lses]
    total = sum(weights)
    for h in range(4):
        cut = slice(h * HD, (h + 1) * HD)
        home = (low if h < 2 else high)[:, (h % 2) * HD : (h % 2 + 1) * HD]
        mixed = weights[0][:, h : h + 1] * home
        for c in range(CHIPS):
            mixed = mixed + weights[c + 1][:, h : h + 1] * x_ref[c, :, cut].astype(F32)
        out_ref[:, cut] = (mixed / total[:, h : h + 1]).astype(BF16)


VMEM = pl.BlockSpec(memory_space=pltpu.VMEM)
SMEM = pl.BlockSpec(memory_space=pltpu.SMEM)
PARAMS = pltpu.CompilerParams(vmem_limit_bytes=24 * 1024 * 1024)


def exchange(x, axis, groups=None):
    return lax.all_to_all(
        x, axis, split_axis=0, concat_axis=0, axis_index_groups=groups, tiled=True
    )


def call(kernel, name, out_shape, args, smem=0):
    specs = [SMEM] * smem + [VMEM] * (len(args) - smem)
    outs = jax.tree.map(lambda _: VMEM, out_shape)
    return pl.pallas_call(
        kernel,
        out_shape=out_shape,
        in_specs=specs,
        out_specs=outs,
        compiler_params=PARAMS,
        name=name,
    )(*args)


def per_device(
    queries,
    home_keys,
    home_values,
    home_table,
    home_len,
    lent_keys,
    lent_values,
    lend_row,
    lend_table,
    lend_len,
):
    same_core = [[2 * z + core for z in range(CHIPS)] for core in range(2)]
    plane = [[(2 * z) * N_TP + j for j in range(2 * N_TP)] for z in range(CHIPS)]
    sibling = [(i, i ^ 1) for i in range(N_INST)]
    wide = WIDTH + 128
    me = lax.axis_index("inst").astype(jnp.int32).reshape(1)

    asked = jnp.broadcast_to(lend_row.reshape(1, SLOTS).astype(BF16), (ROWS, SLOTS))
    asked = jnp.pad(asked, ((0, 0), (0, 128 - SLOTS)))
    sent = jnp.concatenate([queries, asked], axis=1)
    first = exchange(jnp.broadcast_to(sent[None], (N_TP, ROWS, wide)), "tp")
    sent = call(
        spread_kernel, "spread", jax.ShapeDtypeStruct((CHIPS, ROWS, wide), BF16), (queries, first)
    )
    mine = exchange(sent, "inst", same_core)
    picked, target = call(
        pick_kernel,
        "pick",
        (
            jax.ShapeDtypeStruct((2 * N_TP, HALF, WIDTH), BF16),
            jax.ShapeDtypeStruct((2, 8, 512), F32),
        ),
        (me, mine),
        smem=1,
    )
    arrived = exchange(picked, ("inst", "tp"), plane)

    meta = jnp.concatenate(
        [lend_table.reshape(CHIPS, 2, 2, 2), lend_len.reshape(CHIPS, 2, 2, 1)], axis=3
    )
    meta = meta.transpose(3, 1, 0, 2).reshape(3, SLOTS)
    lent_meta = jnp.concatenate([meta, meta], axis=1)
    home_meta = jnp.concatenate([home_table.reshape(ROWS, 1), home_len], axis=1).T
    home_meta = jnp.pad(home_meta, ((0, 0), (0, 128 - ROWS)), constant_values=16)
    pools = call(
        prepare_kernel,
        "prepare",
        tuple(jax.ShapeDtypeStruct((KVH, n, 2 * HD), BF16) for n in (512, 512, 256, 256)),
        (lent_meta, home_meta, lent_keys, lent_values, home_keys, home_values),
    )
    partial = call(
        attend_kernel,
        "attend",
        jax.ShapeDtypeStruct((2 * N_TP, PIECE, HD), BF16),
        (arrived, first, *pools),
    )
    returned = exchange(partial, ("inst", "tp"), plane)
    merged, keep, give = call(
        merge_kernel,
        "merge",
        (
            jax.ShapeDtypeStruct((CHIPS, ROWS, wide), BF16),
            jax.ShapeDtypeStruct((ROWS, 3 * HD), F32),
            jax.ShapeDtypeStruct((ROWS, 3 * HD), F32),
        ),
        (me, target, returned),
        smem=1,
    )
    come = lax.ppermute(give, "inst", sibling)
    back = exchange(merged, "inst", same_core)
    return call(
        final_kernel,
        "final",
        jax.ShapeDtypeStruct((ROWS, WIDTH), BF16),
        (me, keep, come, back),
        smem=1,
    )


def solution(mesh):
    in_specs = (
        P("inst", "tp"),
        P(("inst", "tp"), None, None),
        P(("inst", "tp"), None, None),
        P("inst", "tp", None),
        P("inst", "tp"),
        P(("inst", "tp"), None, None),
        P(("inst", "tp"), None, None),
        P("inst", None, "tp", None),
        P("inst", None, "tp", None, None),
        P("inst", None, "tp", None),
    )
    out_specs = P("inst", "tp")
    return jax.shard_map(
        per_device, mesh=mesh, in_specs=in_specs, out_specs=out_specs, check_vma=False
    )
```

time: 150 us -> 143 us (0.953)
  the two profiles are of different devices: /device:TPU:32 before, /device:TPU:64 now
where the time goes in v3:
time: 143 us; the launch traced here: 142 us
  waiting for transfers between devices  45.9 us (32%)
  blocking collectives  41.2 us (29%)
  starting transfers between devices  26.8 us (19%)
  local copies, waits for them, and re-layouts  13.5 us (9%)
  Pallas kernels  12.7 us (9%)
  other arithmetic  1.51 us (1%)
    all_to_all x3, waiting for transfers between devices, exchange(): lax.all_to_all(x, axis, split_axis=0, concat_axis=0, axis_index_groups=gr...  44.7 us
    all_to_all x2, blocking collectives, exchange(): lax.all_to_all(x, axis, split_axis=0, concat_axis=0, axis_index_groups=gr...  41.2 us
    all_to_all x3, starting transfers between devices, exchange(): lax.all_to_all(x, axis, split_axis=0, concat_axis=0, axis_index_groups=gr...  24.9 us
    pallas_call x6, Pallas kernels, call(): pl.pallas_call(kernel, out_shape=out_shape, in_specs=specs, out_specs=out...  12.7 us
    unnamed x30, local copies, waits for them, and re-layouts  12.6 us
  transfers between devices with their start and end apart: 4, of which 4 were waited for; matrix products, arithmetic and copies ran while one was open for 0% of the time, Pallas kernels for 1%

profile of v3, /device:TPU:64, one launch (start us, length us, event | category | flops | bytes accessed | tf_op | source)
XLA Modules:
  0.0 141.6 jit_solution(1784215790383048924)
XLA Ops:
  0.0 0.7 convert_element_type.13
  0.7 0.1 copy.17
  0.8 0.1 convert_element_type.14
  0.9 0.7 pad_maximum_fusion
  1.7 0.0 copy-start.12
  1.7 0.0 copy-start.11
  1.7 16.0 %all_to_all.25.first_ref = bf16[16,16,640]{2,1,0:T(8,128)(2,1)S(1)} all-to-all(bf16[16,16,640]{2,1,0:T(8,128)(2,1)S(1)} %broadcast_in_dim.2), channel_id=1, replica_groups=mesh['inst'=32,'tp'=16] {'tp'}, dimensions={0} | all-to-all | bytes 655360 | tf_op jit(solution)/shard_map/all_to_all | solution.py:287
  17.7 0.0 copy-start.10
  17.7 0.7 copy-done.10
  18.4 0.0 copy-start.13
  18.4 0.0 copy-start.14
  18.4 0.8 spread.1
  19.2 14.8 %all-to-all-start.1 = ((bf16[16,16,640]{2,1,0:T(8,128)(2,1)}), bf16[16,16,640]{2,1,0:T(8,128)(2,1)S(1)}, u32[]{:S(2)}, u32[]{:S(2)}) async-start(bf16[16,16,640]{2,1,0:T(8,128)(2,1)} %spread.1), calls=%async_computation.1 | async-start | bytes 655360 | tf_op jit(solution)/shard_map/all_to_all | solution.py:287
  33.9 19.6 %all-to-all-done.1.mine_ref = bf16[16,16,640]{2,1,0:T(8,128)(2,1)S(1)} async-done(((bf16[16,16,640]{2,1,0:T(8,128)(2,1)}), bf16[16,16,640]{2,1,0:T(8,128)(2,1)S(1)}, u32[]{:S(2)}, u32[]{:S(2)}) %all-to-all-start.1) | async-done | bytes 327712 | tf_op jit(solution)/shard_map/all_to_all | solution.py:287
  53.6 2.2 %pick.1 = (bf16[32,32,512]{2,1,0:T(8,128)(2,1)}, f32[2,8,512]{2,1,0:T(8,128)S(1)}) custom-call(s32[1]{0:T(128)} %bitcast.me_ref, bf16[16,16,640]{2,1,0:T(8,128)(2,1)S(1)} %all-to-all-done.1.mine_ref), custom_call_target="tpu_custom_call" | custom-call | tf_op jit(solution)/shard_map/pick/pallas_call | solution.py:295
  55.8 3.9 %all-to-all-start.2 = ((bf16[32,32,512]{2,1,0:T(8,128)(2,1)}), bf16[32,32,512]{2,1,0:T(8,128)(2,1)S(1)}, u32[]{:S(2)}, u32[]{:S(2)}) async-start(bf16[32,32,512]{2,1,0:T(8,128)(2,1)} %get-tuple-element.15), calls=%async_computation.2 | async-start | bytes 2097152 | tf_op jit(solution)/shard_map/all_to_all | solution.py:287
  59.7 0.0 copy-done.12
  59.7 0.1 reshape.27
  59.8 0.1 copy.19
  59.9 0.0 copy-done.11
  59.9 0.1 reshape.26
  60.0 0.1 copy.18
  60.1 0.1 copy.20
  60.2 0.1 reshape.28
  60.3 0.0 copy-done.13
  60.3 0.0 copy-done.14
  60.4 0.1 pad_add_fusion.lent_ref
  60.5 1.2 copy-done.2
  61.7 1.2 copy-done.3
  62.9 1.0 copy-done.8
  64.0 1.0 copy-done.9
  65.0 1.2 prepare.1
  66.2 0.0 copy-start
  66.2 1.3 copy-done
  67.5 1.0 copy-done.4
  68.5 1.0 copy-done.6
  69.5 7.7 %all-to-all-done.2.x_ref = bf16[32,32,512]{2,1,0:T(8,128)(2,1)S(1)} async-done(((bf16[32,32,512]{2,1,0:T(8,128)(2,1)}), bf16[32,32,512]{2,1,0:T(8,128)(2,1)S(1)}, u32[]{:S(2)}, u32[]{:S(2)}) %all-to-all-start.2) | async-done | bytes 1048608 | tf_op jit(solution)/shard_map/all_to_all | solution.py:287
  77.2 1.6 %copy-done.1 = bf16[8,512,256]{2,1,0:T(8,128)(2,1)S(1)} copy-done((bf16[8,512,256]{2,1,0:T(8,128)(2,1)S(1)}, bf16[8,512,256]{2,1,0:T(8,128)(2,1)}, u32[]{:S(2)}) %copy-start.1) | copy-done | bytes 2097176
  78.8 1.2 copy-done.5
  80.0 1.2 copy-done.7
  81.2 5.5 %attend.1 = bf16[32,176,128]{2,1,0:T(8,128)(2,1)S(1)} custom-call(bf16[32,32,512]{2,1,0:T(8,128)(2,1)S(1)} %all-to-all-done.2.x_ref, bf16[16,16,640]{2,1,0:T(8,128)(2,1)S(1)} %all_to_all.25.first_ref, bf16[8,512,256]{2,1,0:T(8,128)(2,1)S(1)} %get-tuple-element.16.klent_ref, bf16[8,512,256]{2,1,0:T(8,128)(2,1)S(1)} %copy-done.1, ...), custom_call_target="tpu_custom_call" | custom-call | tf_op jit(solution)/shard_map/attend/pallas_call | solution.py:295
  86.7 25.2 %all_to_all.26.x_ref = bf16[32,176,128]{2,1,0:T(8,128)(2,1)S(1)} all-to-all(bf16[32,176,128]{2,1,0:T(8,128)(2,1)S(1)} %attend.1), channel_id=1, replica_groups={{0,1,2,3,4,5,6,7,8,9,10,11,12,13,14,15,16,17,18,19,20,21,22,23,24,25,26..., dimensions={0} | all-to-all | bytes 2883584 | tf_op jit(solution)/shard_map/all_to_all | solution.py:287
  111.9 2.1 %merge.1 = (bf16[16,16,640]{2,1,0:T(8,128)(2,1)}, f32[16,384]{1,0:T(8,128)S(1)}, f32[16,384]{1,0:T(8,128)S(1)}) custom-call(s32[1]{0:T(128)} %bitcast.me_ref, f32[2,8,512]{2,1,0:T(8,128)S(1)} %get-tuple-element.14.target_ref, bf16[32,176,128]{2,1,0:T(8,128)(2,1)S(1)} %all_to_all.26.x_ref), custom_call_target="tpu_custom_call" | custom-call | tf_op jit(solution)/shard_map/merge/pallas_call | solution.py:295
  114.0 6.2 %all-to-all-start.4 = ((bf16[16,16,640]{2,1,0:T(8,128)(2,1)}), bf16[16,16,640]{2,1,0:T(8,128)(2,1)S(1)}, u32[]{:S(2)}, u32[]{:S(2)}) async-start(bf16[16,16,640]{2,1,0:T(8,128)(2,1)} %get-tuple-element.22), calls=%async_computation.4 | async-start | bytes 655360 | tf_op jit(solution)/shard_map/all_to_all | solution.py:287
  120.2 1.9 %collective-permute-start = (f32[16,384]{1,0:T(8,128)S(1)}, f32[16,384]{1,0:T(8,128)S(1)}, u32[]{:S(2)}, u32[]{:S(2)}) collective-permute-start(f32[16,384]{1,0:T(8,128)S(1)} %get-tuple-element.21), channel_id=1, source_target_pairs={{0,16},{16,0},{32,48},{48,32},{64,80},{80,64},{96,112},{112,96},{1... | collective-permute-start | bytes 73736 | tf_op jit(solution)/shard_map/ppermute | solution.py:374
  122.1 1.2 collective-permute-done.come_ref
  123.3 17.4 %all-to-all-done.4.x_ref = bf16[16,16,640]{2,1,0:T(8,128)(2,1)S(1)} async-done(((bf16[16,16,640]{2,1,0:T(8,128)(2,1)}), bf16[16,16,640]{2,1,0:T(8,128)(2,1)S(1)}, u32[]{:S(2)}, u32[]{:S(2)}) %all-to-all-start.4) | async-done | bytes 327712 | tf_op jit(solution)/shard_map/all_to_all | solution.py:287
  140.7 0.9 final.1
  (14 shorter events, 0.1 us)
Async XLA Ops:
  1.7 58.0 %copy-start.12 = (s32[1,32,1,2]{1,3,2,0:T(2,128)S(1)}, s32[1,32,1,2]{1,3,2,0:T(2,128)}, u32[]{:S(2)}) copy-start(s32[1,32,1,2]{1,3,2,0:T(2,128)} %param.19) | copy-start | bytes 772
  1.7 58.2 %copy-start.11 = (s32[1,32,1,2,2]{1,4,3,2,0:T(2,128)S(1)}, s32[1,32,1,2,2]{1,4,3,2,0:T(2,128)}, u32[]{:S(2)}) copy-start(s32[1,32,1,2,2]{1,4,3,2,0:T(2,128)} %param.18) | copy-start | bytes 1540
  17.7 0.7 copy-start.10
  18.4 41.9 %copy-start.13 = (s32[16,1]{0,1:T(1,128)S(1)}, s32[16,1]{0,1:T(1,128)}, u32[]{:S(2)}) copy-start(s32[16,1]{0,1:T(1,128)} %param.14) | copy-start | bytes 196
  18.4 41.9 %copy-start.14 = (s32[16,1,1]{0,2,1:T(1,128)S(1)}, s32[16,1,1]{0,2,1:T(1,128)}, u32[]{:S(2)}) copy-start(s32[16,1,1]{0,2,1:T(1,128)} %param.13) | copy-start | bytes 196
  19.2 34.4 %all-to-all-start.1 = ((bf16[16,16,640]{2,1,0:T(8,128)(2,1)}), bf16[16,16,640]{2,1,0:T(8,128)(2,1)S(1)}, u32[]{:S(2)}, u32[]{:S(2)}) async-start(bf16[16,16,640]{2,1,0:T(8,128)(2,1)} %spread.1), calls=%async_computation.1 | async-start | bytes 655360 | tf_op jit(solution)/shard_map/all_to_all | solution.py:287
  55.8 21.4 %all-to-all-start.2 = ((bf16[32,32,512]{2,1,0:T(8,128)(2,1)}), bf16[32,32,512]{2,1,0:T(8,128)(2,1)S(1)}, u32[]{:S(2)}, u32[]{:S(2)}) async-start(bf16[32,32,512]{2,1,0:T(8,128)(2,1)} %get-tuple-element.15), calls=%async_computation.2 | async-start | bytes 2097152 | tf_op jit(solution)/shard_map/all_to_all | solution.py:287
  60.5 1.2 copy-start.2
  61.7 1.2 copy-start.3
  62.9 1.0 copy-start.8
  63.9 1.0 copy-start.9
  66.2 1.3 copy-start
  67.5 1.0 copy-start.4
  68.5 1.0 copy-start.6
  77.2 1.6 %copy-start.1 = (bf16[8,512,256]{2,1,0:T(8,128)(2,1)S(1)}, bf16[8,512,256]{2,1,0:T(8,128)(2,1)}, u32[]{:S(2)}) copy-start(bf16[8,512,256]{2,1,0:T(8,128)(2,1)} %copy-done) | copy-start | bytes 6291460
  78.8 1.2 copy-start.5
  80.0 1.2 copy-start.7
  114.0 26.6 %all-to-all-start.4 = ((bf16[16,16,640]{2,1,0:T(8,128)(2,1)}), bf16[16,16,640]{2,1,0:T(8,128)(2,1)S(1)}, u32[]{:S(2)}, u32[]{:S(2)}) async-start(bf16[16,16,640]{2,1,0:T(8,128)(2,1)} %get-tuple-element.22), calls=%async_computation.4 | async-start | bytes 655360 | tf_op jit(solution)/shard_map/all_to_all | solution.py:287
  120.2 3.1 %collective-permute-start = (f32[16,384]{1,0:T(8,128)S(1)}, f32[16,384]{1,0:T(8,128)S(1)}, u32[]{:S(2)}, u32[]{:S(2)}) collective-permute-start(f32[16,384]{1,0:T(8,128)S(1)} %get-tuple-element.21), channel_id=1, source_target_pairs={{0,16},{16,0},{32,48},{48,32},{64,80},{80,64},{96,112},{112,96},{1... | collective-permute-start | bytes 73736 | tf_op jit(solution)/shard_map/ppermute | solution.py:374

commit v4 on v3

--- a/solution.py
+++ b/solution.py
@@ -28,7 +28,6 @@
 FACTOR = SCALE * math.log2(math.e)
 TWICE_HI = float(np.float32(1 / FACTOR).astype(ml_dtypes.bfloat16))
 TWICE_LO = 1 / FACTOR - TWICE_HI
-UNROLL = 8
 
 
 def iota(shape, axis):
@@ -55,46 +54,81 @@
     return hi + pltpu.roll(mid, 4, 1) + pltpu.roll(low, 8, 1)
 
 
-def spread_kernel(queries_ref, first_ref, out_ref):
-    row = iota((ROWS, 128), 0)
-    asked = jnp.zeros((ROWS, 128), F32)
+def turn(x, by):
+    return pltpu.roll(x, by % 128, 1) if by % 128 else x
+
+
+def head_rows(h):
+    return slice(h * ROWS, (h + 1) * ROWS)
+
+
+def open_kernel(lend_ref, queries_ref, out_ref, lend_s):
+    lend_s[...] = jnp.zeros_like(lend_s)
+    lend_s[0:2, 0:N_INST] = lend_ref[...]
+    lend = lend_s[...].astype(F32).astype(BF16)
     for t in range(N_TP):
-        asked = jnp.where(row == t, first_ref[t, :, WIDTH:].astype(F32), asked)
-    block = jnp.concatenate([queries_ref[...], asked.astype(BF16)], axis=1)
+        for h in range(4):
+            out_ref[t, head_rows(h), :] = queries_ref[:, h * HD : (h + 1) * HD]
+        out_ref[t, 4 * ROWS :, :] = lend
+
+
+def spread_kernel(me_ref, first_ref, out_ref):
+    row = iota((8, 128), 0)
+    asked = jnp.zeros((8, 128), F32)
+    for t in range(N_TP):
+        part = first_ref[t, 4 * ROWS :, :].astype(F32)
+        place = 64 * (t // 8)
+        line = turn(part, place)[0:1] + turn(part, place + 32)[1:2]
+        asked = asked + jnp.where(row == t % 8, line, 0.0)
+    asked = asked.astype(BF16)
+    queries = first_ref[me_ref[1], : 4 * ROWS, :]
     for z in range(CHIPS):
-        out_ref[z] = block
-
-
-def pick_kernel(me_ref, mine_ref, out_ref, target_ref):
-    chip = jnp.right_shift(me_ref[0], 1)
+        out_ref[z, : 4 * ROWS, :] = queries
+        out_ref[z, 4 * ROWS :, :] = asked
+
+
+def places(me, mine_ref, g, d):
+    k = iota((256, 64), 0)
+    local = jnp.bitwise_and(jnp.right_shift(k, 1), 7)
+    source = local * 8 + jnp.bitwise_and(jnp.right_shift(k, 4), 7)
+    order = jnp.where(iota((256, 64), 1) == source, 1.0, 0.0).astype(BF16)
+    asked = mine_ref[g * 8 : (g + 1) * 8, 4 * ROWS :, :].astype(F32).reshape(64, 128)
+    asked = dot(order, asked.astype(BF16))
     k = iota((256, 128), 0)
-    n = iota((256, 128), 1)
+    creditor = 2 * jnp.right_shift(me, 1) + d
+    column = jnp.right_shift(k, 7) * 64 + jnp.bitwise_and(k, 1) * 32 + creditor
+    asked = jnp.where(iota((256, 128), 1) == column, asked, 0.0).astype(BF16)
     local = jnp.bitwise_and(jnp.right_shift(k, 1), 7)
-    order = jnp.where(n == local * 16 + jnp.right_shift(k, 4), 1.0, 0.0).astype(BF16)
-    second = jnp.bitwise_and(k, 1) == 1
-    base = local.astype(F32) * 16.0
-    lane = n.astype(F32)
-    row = iota((128, 128), 0)
+    return dot(asked, jnp.ones((128, 128), BF16)) + local.astype(F32) * 16.0
+
+
+def pick_kernel(me_ref, mine_ref, out_ref):
+    lane = iota((256, 128), 1).astype(F32)
     for g in range(2):
-        block = mine_ref[g * 8 : (g + 1) * 8].reshape(128, WIDTH + 128)
-        asked = dot(order, block[:, WIDTH:]).astype(BF16)
+        block = jnp.concatenate(
+            [
+                mine_ref[g * 8 : (g + 1) * 8, head_rows(h), :].reshape(128, HD)
+                for h in range(4)
+            ],
+            axis=1,
+        )
         for d in range(2):
-            found = []
-            for s in range(2):
-                column = jnp.where(row == 4 * chip + 2 * d + s, 1.0, 0.0).astype(BF16)
-                found.append(dot(asked, column))
-            target = jnp.where(second, found[1], found[0]) + base
+            target = places(me_ref[0], mine_ref, g, d)
             onehot = jnp.where(lane == target, 1.0, 0.0).astype(BF16)
-            picked = dot(onehot, block[:, :WIDTH]).astype(BF16)
+            picked = dot(onehot, block).astype(BF16)
             out_ref[d * N_TP : (d + 1) * N_TP, g * 16 : (g + 1) * 16, :] = picked.reshape(
                 N_TP, 16, WIDTH
             )
-            target_ref[g, :, d * 256 : (d + 1) * 256] = target.T[:8]
-
-
-def prepare_kernel(
-    lent_ref, home_ref, lk_ref, lv_ref, hk_ref, hv_ref, klent_ref, vlent_ref, khome_ref, vhome_ref
-):
+
+
+def places_kernel(me_ref, mine_ref, out_ref):
+    for g in range(2):
+        for d in range(2):
+            target = places(me_ref[0], mine_ref, g, d)
+            out_ref[g, :, d * 256 : (d + 1) * 256] = target.T[:8]
+
+
+def masks_kernel(lent_ref, home_ref, lent_out, home_out):
     token = iota((512, 128), 0)
     block = jnp.right_shift(token, 4)
     place = jnp.bitwise_and(token, 15)
@@ -104,26 +138,43 @@
     twice = first & other
     upper = jnp.where(first | other, jnp.where(twice, TWICE_HI, 0.0), DEAD)
     lower = jnp.where(twice, TWICE_LO, 0.0)
-    lent_mask = jnp.where(iota((512, 128), 1) < SLOTS, upper, lower).astype(BF16)
+    lent_out[...] = jnp.where(iota((512, 128), 1) < SLOTS, upper, lower).astype(BF16)
     token = iota((256, 128), 0)
     live = (jnp.right_shift(token, 4) == home_ref[0:1, :]) & (
         jnp.bitwise_and(token, 15) < home_ref[1:2, :]
     )
-    home_mask = jnp.where(live, 0.0, DEAD).astype(BF16)
-    ones = jnp.ones((512, 128), BF16)
-    for k in range(KVH):
+    home_out[...] = jnp.where(live, 0.0, DEAD).astype(BF16)
+
+
+def attend_kernel(
+    x_ref,
+    first_ref,
+    lent_mask_ref,
+    home_mask_ref,
+    lk_ref,
+    lv_ref,
+    hk_ref,
+    hv_ref,
+    out_ref,
+    lk_s,
+    lv_s,
+    hk_s,
+    hv_s,
+    sems,
+):
+    def fetch(k):
         cut = slice(k * HD, (k + 1) * HD)
-        klent_ref[k, :, :HD] = lk_ref[:, :, cut].reshape(512, HD)
-        klent_ref[k, :, HD:] = lent_mask
-        vlent_ref[k, :, :HD] = lv_ref[:, :, cut].reshape(512, HD)
-        vlent_ref[k, :, HD:] = ones
-        khome_ref[k, :, :HD] = hk_ref[:, :, cut].reshape(256, HD)
-        khome_ref[k, :, HD:] = home_mask
-        vhome_ref[k, :, :HD] = hv_ref[:, :, cut].reshape(256, HD)
-        vhome_ref[k, :, HD:] = ones[:256]
-
-
-def attend_kernel(x_ref, first_ref, klent_ref, vlent_ref, khome_ref, vhome_ref, out_ref):
+        pairs = ((lk_ref, lk_s), (lv_ref, lv_s), (hk_ref, hk_s), (hv_ref, hv_s))
+        return [
+            pltpu.make_async_copy(source.at[:, :, cut], to.at[k], sems.at[k, j])
+            for j, (source, to) in enumerate(pairs)
+        ]
+
+    copies = [fetch(k) for k in range(KVH)]
+    for group in copies:
+        for copy in group:
+            copy.start()
+
     def pool(query, pick, keys, values, count):
         query = jnp.concatenate([query, jnp.concatenate([pick] * 8, axis=0)], axis=1)
         scores = dot_nt(query, keys)
@@ -155,18 +206,27 @@
     home_pick = jnp.where(iota((ROWS, 128), 1) == iota((ROWS, 128), 0), 1.0, 0.0).astype(BF16)
     heads = [(tt, h) for tt in range(2) for h in range(4)]
 
-    def step(k, carry):
+    lent_mask = lent_mask_ref[...]
+    home_mask = home_mask_ref[...]
+    ones = jnp.ones((512, 128), BF16)
+    for k in range(KVH):
+        for copy in copies[k]:
+            copy.wait()
+        lent_k = jnp.concatenate([lk_s[k].reshape(512, HD), lent_mask], axis=1)
+        lent_v = jnp.concatenate([lv_s[k].reshape(512, HD), ones], axis=1)
+        home_k = jnp.concatenate([hk_s[k].reshape(256, HD), home_mask], axis=1)
+        home_v = jnp.concatenate([hv_s[k].reshape(256, HD), ones[:256]], axis=1)
         query = [
             x_ref[d * N_TP + 2 * k + tt, :, h * HD : (h + 1) * HD]
             for tt, h in heads
             for d in range(2)
         ]
         lent, lent_peaks, lent_total = pool(
-            jnp.concatenate(query, axis=0), lent_pick, klent_ref[k], vlent_ref[k], SLOTS
+            jnp.concatenate(query, axis=0), lent_pick, lent_k, lent_v, SLOTS
         )
-        query = [first_ref[2 * k + tt, :, h * HD : (h + 1) * HD] for tt, h in heads]
+        query = [first_ref[2 * k + tt, head_rows(h), :] for tt, h in heads]
         home, home_peaks, home_total = pool(
-            jnp.concatenate(query, axis=0), home_pick, khome_ref[k], vhome_ref[k], ROWS
+            jnp.concatenate(query, axis=0), home_pick, home_k, home_v, ROWS
         )
         for tt in range(2):
             lent_lse = columns(tt, lent_peaks, lent_total, SLOTS)
@@ -187,9 +247,6 @@
                     to_row = 4 * HALF + hh * ROWS
                     out_ref[to, to_row : to_row + ROWS, :] = home[at : at + ROWS]
                 out_ref[to, PIECE - 16 :, :] = (pltpu.roll(lse, 64, 1) if d else lse).astype(BF16)
-        return carry
-
-    lax.fori_loop(0, KVH, step, 0, unroll=UNROLL)
 
 
 def merge_kernel(me_ref, target_ref, x_ref, out_ref, keep_ref, give_ref):
@@ -206,9 +263,7 @@
         for at in range(0, len(sources), 8):
             row = jnp.zeros((8, 128), F32)
             for j in range(8):
-                shift = (16 * j - first) % 128
-                moved = lses[sources[at + j]]
-                moved = pltpu.roll(moved, shift, 1) if shift else moved
+                moved = turn(lses[sources[at + j]], 16 * j - first)
                 row = jnp.where(jnp.right_shift(lane, 4) == j, moved, row)
             chunks.append(row)
         return jnp.concatenate(chunks, axis=1)
@@ -236,8 +291,15 @@
             values = x_ref[:, at : at + 16, :].reshape(512, HD)
             mixed, total = join(mask, lse[h : h + 1, :], values)
             out_lse = jnp.where(out_lane == h, total, out_lse)
-            out_ref[block, :, h * HD : (h + 1) * HD] = mixed.astype(BF16).reshape(8, ROWS, HD)
-        out_ref[block, :, WIDTH:] = spread3(out_lse).astype(BF16).reshape(8, ROWS, 128)
+            out_ref[block, head_rows(h), :] = mixed.astype(BF16).reshape(8, ROWS, HD)
+        hi, mid, low = split3(out_lse.T[:8])
+        for j in range(8):
+            line = jnp.where(lane < 32, turn(mid, 16 - 16 * j), 0.0)
+            line = jnp.where(lane < 16, turn(hi, -16 * j), line)
+            line = jnp.where(
+                (lane >= 32) & (lane < 48), turn(low, 32 - 16 * j), line
+            )
+            out_ref[g * 8 + j, 4 * ROWS :, :] = line.astype(BF16)
     mask = iota((ROWS, 256), 0) == jnp.bitwise_and(iota((ROWS, 256), 1), 15)
     home_lane = iota((ROWS, 128), 1)
     homes = []
@@ -262,24 +324,29 @@
     low = jnp.where(core == 0, keep_ref[...], come_ref[...])
     high = jnp.where(core == 0, come_ref[...], keep_ref[...])
     lane = iota((ROWS, 128), 1)
-    lses = [jnp.where(lane < 2, low[:, 2 * HD :], pltpu.roll(high[:, 2 * HD :], 2, 1))]
+    lse = jnp.where(lane < 2, low[:, 2 * HD :], pltpu.roll(high[:, 2 * HD :], 2, 1))
+    lses = [jnp.concatenate([lse, jnp.zeros((128 - ROWS, 128), F32)], axis=0).T[:8]]
     for c in range(CHIPS):
-        parts = x_ref[c, :, WIDTH:].astype(F32)
-        lses.append(parts + pltpu.roll(parts, 124, 1) + pltpu.roll(parts, 120, 1))
+        parts = x_ref[c, 4 * ROWS :, :].astype(F32)
+        lses.append(parts + turn(parts, -16) + turn(parts, -32))
     peak = functools.reduce(jnp.maximum, lses)
     weights = [jnp.exp(lse - peak) for lse in lses]
     total = sum(weights)
+    weights = [weight / total for weight in weights]
+    home_weight = jnp.concatenate([weights[0], jnp.zeros((120, 128), F32)], axis=0).T[:ROWS]
+    lent_weight = jnp.concatenate(weights[1:], axis=0).T[:ROWS]
     for h in range(4):
-        cut = slice(h * HD, (h + 1) * HD)
         home = (low if h < 2 else high)[:, (h % 2) * HD : (h % 2 + 1) * HD]
-        mixed = weights[0][:, h : h + 1] * home
+        mixed = home_weight[:, h : h + 1] * home
         for c in range(CHIPS):
-            mixed = mixed + weights[c + 1][:, h : h + 1] * x_ref[c, :, cut].astype(F32)
-        out_ref[:, cut] = (mixed / total[:, h : h + 1]).astype(BF16)
+            at = c * 8 + h
+            mixed = mixed + lent_weight[:, at : at + 1] * x_ref[c, head_rows(h), :].astype(F32)
+        out_ref[:, h * HD : (h + 1) * HD] = mixed.astype(BF16)
 
 
 VMEM = pl.BlockSpec(memory_space=pltpu.VMEM)
 SMEM = pl.BlockSpec(memory_space=pltpu.SMEM)
+ANY = pl.BlockSpec(memory_space=pl.ANY)
 PARAMS = pltpu.CompilerParams(vmem_limit_bytes=24 * 1024 * 1024)
 
 
@@ -289,14 +356,14 @@
     )
 
 
-def call(kernel, name, out_shape, args, smem=0):
-    specs = [SMEM] * smem + [VMEM] * (len(args) - smem)
-    outs = jax.tree.map(lambda _: VMEM, out_shape)
+def call(kernel, name, out_shape, args, smem=0, any_last=0, scratch=()):
+    specs = [SMEM] * smem + [VMEM] * (len(args) - smem - any_last) + [ANY] * any_last
     return pl.pallas_call(
         kernel,
         out_shape=out_shape,
         in_specs=specs,
-        out_specs=outs,
+        out_specs=jax.tree.map(lambda _: VMEM, out_shape),
+        scratch_shapes=scratch,
         compiler_params=PARAMS,
         name=name,
     )(*args)
@@ -317,28 +384,30 @@
     same_core = [[2 * z + core for z in range(CHIPS)] for core in range(2)]
     plane = [[(2 * z) * N_TP + j for j in range(2 * N_TP)] for z in range(CHIPS)]
     sibling = [(i, i ^ 1) for i in range(N_INST)]
-    wide = WIDTH + 128
-    me = lax.axis_index("inst").astype(jnp.int32).reshape(1)
-
-    asked = jnp.broadcast_to(lend_row.reshape(1, SLOTS).astype(BF16), (ROWS, SLOTS))
-    asked = jnp.pad(asked, ((0, 0), (0, 128 - SLOTS)))
-    sent = jnp.concatenate([queries, asked], axis=1)
-    first = exchange(jnp.broadcast_to(sent[None], (N_TP, ROWS, wide)), "tp")
+    block = (CHIPS, 4 * ROWS + 8, HD)
+    me = jnp.stack([lax.axis_index("inst"), lax.axis_index("tp")]).astype(jnp.int32)
+
     sent = call(
-        spread_kernel, "spread", jax.ShapeDtypeStruct((CHIPS, ROWS, wide), BF16), (queries, first)
-    )
+        open_kernel,
+        "open",
+        jax.ShapeDtypeStruct(block, BF16),
+        (lend_row.reshape(N_INST, 2).T, queries),
+        scratch=(pltpu.VMEM((8, 128), jnp.int32),),
+    )
+    first = exchange(sent, "tp")
+    sent = call(spread_kernel, "spread", jax.ShapeDtypeStruct(block, BF16), (me, first), smem=1)
     mine = exchange(sent, "inst", same_core)
-    picked, target = call(
+    picked = call(
         pick_kernel,
         "pick",
-        (
-            jax.ShapeDtypeStruct((2 * N_TP, HALF, WIDTH), BF16),
-            jax.ShapeDtypeStruct((2, 8, 512), F32),
-        ),
+        jax.ShapeDtypeStruct((2 * N_TP, HALF, WIDTH), BF16),
         (me, mine),
         smem=1,
     )
     arrived = exchange(picked, ("inst", "tp"), plane)
+    target = call(
+        places_kernel, "places", jax.ShapeDtypeStruct((2, 8, 512), F32), (me, mine), smem=1
+    )
 
     meta = jnp.concatenate(
         [lend_table.reshape(CHIPS, 2, 2, 2), lend_len.reshape(CHIPS, 2, 2, 1)], axis=3
@@ -347,24 +416,32 @@
     lent_meta = jnp.concatenate([meta, meta], axis=1)
     home_meta = jnp.concatenate([home_table.reshape(ROWS, 1), home_len], axis=1).T
     home_meta = jnp.pad(home_meta, ((0, 0), (0, 128 - ROWS)), constant_values=16)
-    pools = call(
-        prepare_kernel,
-        "prepare",
-        tuple(jax.ShapeDtypeStruct((KVH, n, 2 * HD), BF16) for n in (512, 512, 256, 256)),
-        (lent_meta, home_meta, lent_keys, lent_values, home_keys, home_values),
+    masks = call(
+        masks_kernel,
+        "masks",
+        (jax.ShapeDtypeStruct((512, 128), BF16), jax.ShapeDtypeStruct((256, 128), BF16)),
+        (lent_meta, home_meta),
     )
     partial = call(
         attend_kernel,
         "attend",
         jax.ShapeDtypeStruct((2 * N_TP, PIECE, HD), BF16),
-        (arrived, first, *pools),
+        (arrived, first, *masks, lent_keys, lent_values, home_keys, home_values),
+        any_last=4,
+        scratch=(
+            pltpu.VMEM((KVH, 32, 16, HD), BF16),
+            pltpu.VMEM((KVH, 32, 16, HD), BF16),
+            pltpu.VMEM((KVH, 16, 16, HD), BF16),
+            pltpu.VMEM((KVH, 16, 16, HD), BF16),
+            pltpu.SemaphoreType.DMA((KVH, 4)),
+        ),
     )
     returned = exchange(partial, ("inst", "tp"), plane)
     merged, keep, give = call(
         merge_kernel,
         "merge",
         (
-            jax.ShapeDtypeStruct((CHIPS, ROWS, wide), BF16),
+            jax.ShapeDtypeStruct(block, BF16),
             jax.ShapeDtypeStruct((ROWS, 3 * HD), F32),
             jax.ShapeDtypeStruct((ROWS, 3 * HD), F32),
         ),

time: 143 us -> 144 us (level)
  the two profiles are of different devices: /device:TPU:64 before, /device:TPU:2 now
where the time goes in v4:
time: 144 us
  waiting for transfers between devices  60.4 us (42%)
  blocking collectives  31.9 us (22%)
  starting transfers between devices  27.4 us (19%)
  Pallas kernels  19.4 us (13%)
  local copies, waits for them, and re-layouts  4.28 us (3%)
    all_to_all x4, waiting for transfers between devices, exchange(): lax.all_to_all(x, axis, split_axis=0, concat_axis=0, axis_index_groups=gr...  59.3 us
    all_to_all x1, blocking collectives, exchange(): lax.all_to_all(x, axis, split_axis=0, concat_axis=0, axis_index_groups=gr...  31.9 us
    all_to_all x4, starting transfers between devices, exchange(): lax.all_to_all(x, axis, split_axis=0, concat_axis=0, axis_index_groups=gr...  25.4 us
    pallas_call x8, Pallas kernels, call(): pl.pallas_call(kernel, out_shape=out_shape, in_specs=specs, out_specs=jax...  19.4 us
    unnamed x20, local copies, waits for them, and re-layouts  3.68 us
  transfers between devices with their start and end apart: 5, of which 5 were waited for; matrix products, arithmetic and copies ran while one was open for 1% of the time, Pallas kernels for 1%

profile of v4, /device:TPU:2, one launch (start us, length us, event | category | flops | bytes accessed | tf_op | source)
XLA Modules:
  0.0 143.6 jit_solution(8622035818053514767)
XLA Ops:
  0.0 0.0 copy-start.4
  0.0 0.7 copy-done.4
  0.7 0.0 copy-start.5
  0.7 0.7 copy-done.5
  1.4 0.7 open.1
  2.1 9.3 %all-to-all-start = ((bf16[16,72,128]{2,1,0:T(8,128)(2,1)}), bf16[16,72,128]{2,1,0:T(8,128)(2,1)S(1)}, u32[]{:S(2)}, u32[]{:S(2)}) async-start(bf16[16,72,128]{2,1,0:T(8,128)(2,1)} %open.1), calls=%async_computation | async-start | bytes 589824 | tf_op jit(solution)/shard_map/all_to_all | solution.py:354
  11.4 0.1 pad_add_fusion.1.me_ref
  11.5 6.9 %all-to-all-done.first_ref = bf16[16,72,128]{2,1,0:T(8,128)(2,1)S(1)} async-done(((bf16[16,72,128]{2,1,0:T(8,128)(2,1)}), bf16[16,72,128]{2,1,0:T(8,128)(2,1)S(1)}, u32[]{:S(2)}, u32[]{:S(2)}) %all-to-all-start) | async-done | bytes 294944 | tf_op jit(solution)/shard_map/all_to_all | solution.py:354
  18.4 0.6 spread.1
  19.0 31.9 %all_to_all.25.mine_ref = bf16[16,72,128]{2,1,0:T(8,128)(2,1)S(1)} all-to-all(bf16[16,72,128]{2,1,0:T(8,128)(2,1)S(1)} %spread.1), channel_id=1, replica_groups={{0,32,64,96,128,160,192,224,256,288,320,352,384,416,448,480},{16,48,80,..., dimensions={0} | all-to-all | bytes 589824 | tf_op jit(solution)/shard_map/all_to_all | solution.py:354
  50.9 0.0 copy-start.7
  50.9 0.0 copy-start.6
  50.9 2.9 %pick.1 = bf16[32,32,512]{2,1,0:T(8,128)(2,1)} custom-call(s32[2]{0:T(128)S(1)} %pad_add_fusion.1.me_ref, bf16[16,72,128]{2,1,0:T(8,128)(2,1)S(1)} %all_to_all.25.mine_ref), custom_call_target="tpu_custom_call" | custom-call | tf_op jit(solution)/shard_map/pick/pallas_call | solution.py:361
  53.8 0.0 copy-start.8
  53.8 0.0 copy-start.9
  53.8 0.0 copy-start
  53.8 0.0 copy-start.2
  53.8 5.8 %all-to-all-start.2 = ((bf16[32,32,512]{2,1,0:T(8,128)(2,1)}), bf16[32,32,512]{2,1,0:T(8,128)(2,1)S(1)}, u32[]{:S(2)}, u32[]{:S(2)}) async-start(bf16[32,32,512]{2,1,0:T(8,128)(2,1)} %pick.1), calls=%async_computation.2 | async-start | bytes 2097152 | tf_op jit(solution)/shard_map/all_to_all | solution.py:354
  59.6 0.0 copy-done.7
  59.6 0.1 reshape.17
  59.7 0.1 copy.16
  59.8 0.0 copy-done.6
  59.8 0.1 reshape.16
  59.9 0.1 copy.15
  60.0 0.1 copy.17
  60.1 0.1 reshape.18
  60.2 0.0 copy-done.8
  60.2 0.0 copy-done.9
  60.3 0.1 pad_add_fusion.lent_ref
  60.3 0.2 masks.1
  60.5 15.8 %all-to-all-done.2.x_ref = bf16[32,32,512]{2,1,0:T(8,128)(2,1)S(1)} async-done(((bf16[32,32,512]{2,1,0:T(8,128)(2,1)}), bf16[32,32,512]{2,1,0:T(8,128)(2,1)S(1)}, u32[]{:S(2)}, u32[]{:S(2)}) %all-to-all-start.2) | async-done | bytes 1048608 | tf_op jit(solution)/shard_map/all_to_all | solution.py:354
  76.3 0.0 copy-done
  76.3 0.0 copy-done.2
  76.3 0.0 copy-start.1
  76.3 1.2 copy-done.1
  77.5 0.0 copy-start.3
  77.5 1.0 copy-done.3
  78.6 9.7 %attend.1 = bf16[32,176,128]{2,1,0:T(8,128)(2,1)} custom-call(bf16[32,32,512]{2,1,0:T(8,128)(2,1)S(1)} %all-to-all-done.2.x_ref, bf16[16,72,128]{2,1,0:T(8,128)(2,1)S(1)} %all-to-all-done.first_ref, bf16[512,128]{1,0:T(8,128)(2,1)S(1)} %get-tuple-element.10.lent_mask_ref, bf16[256,128]{1,0:T(8,128)(2,1)S(1)} %get-tuple-element.11.home_mask_ref, ...), custom_call_target="tpu_custom_call" | custom-call | tf_op jit(solution)/shard_map/attend/pallas_call | solution.py:361
  88.3 4.6 %all-to-all-start.3 = ((bf16[32,176,128]{2,1,0:T(8,128)(2,1)}), bf16[32,176,128]{2,1,0:T(8,128)(2,1)S(1)}, u32[]{:S(2)}, u32[]{:S(2)}) async-start(bf16[32,176,128]{2,1,0:T(8,128)(2,1)} %attend.1), calls=%async_computation.3 | async-start | bytes 2883584 | tf_op jit(solution)/shard_map/all_to_all | solution.py:354
  92.9 1.0 places.1.target_ref
  93.9 20.4 %all-to-all-done.3.x_ref = bf16[32,176,128]{2,1,0:T(8,128)(2,1)S(1)} async-done(((bf16[32,176,128]{2,1,0:T(8,128)(2,1)}), bf16[32,176,128]{2,1,0:T(8,128)(2,1)S(1)}, u32[]{:S(2)}, u32[]{:S(2)}) %all-to-all-start.3) | async-done | bytes 1441824 | tf_op jit(solution)/shard_map/all_to_all | solution.py:354
  114.3 2.6 %merge.1 = (bf16[16,72,128]{2,1,0:T(8,128)(2,1)}, f32[16,384]{1,0:T(8,128)S(1)}, f32[16,384]{1,0:T(8,128)S(1)}) custom-call(s32[2]{0:T(128)S(1)} %pad_add_fusion.1.me_ref, f32[2,8,512]{2,1,0:T(8,128)S(1)} %places.1.target_ref, bf16[32,176,128]{2,1,0:T(8,128)(2,1)S(1)} %all-to-all-done.3.x_ref), custom_call_target="tpu_custom_call" | custom-call | tf_op jit(solution)/shard_map/merge/pallas_call | solution.py:361
  116.9 5.8 %all-to-all-start.4 = ((bf16[16,72,128]{2,1,0:T(8,128)(2,1)}), bf16[16,72,128]{2,1,0:T(8,128)(2,1)S(1)}, u32[]{:S(2)}, u32[]{:S(2)}) async-start(bf16[16,72,128]{2,1,0:T(8,128)(2,1)} %get-tuple-element.14), calls=%async_computation.4 | async-start | bytes 589824 | tf_op jit(solution)/shard_map/all_to_all | solution.py:354
  122.7 1.9 %collective-permute-start = (f32[16,384]{1,0:T(8,128)S(1)}, f32[16,384]{1,0:T(8,128)S(1)}, u32[]{:S(2)}, u32[]{:S(2)}) collective-permute-start(f32[16,384]{1,0:T(8,128)S(1)} %get-tuple-element.13), channel_id=1, source_target_pairs={{0,16},{16,0},{32,48},{48,32},{64,80},{80,64},{96,112},{112,96},{1... | collective-permute-start | bytes 73736 | tf_op jit(solution)/shard_map/ppermute | solution.py:451
  124.6 1.2 collective-permute-done.come_ref
  125.8 16.2 %all-to-all-done.4.x_ref = bf16[16,72,128]{2,1,0:T(8,128)(2,1)S(1)} async-done(((bf16[16,72,128]{2,1,0:T(8,128)(2,1)}), bf16[16,72,128]{2,1,0:T(8,128)(2,1)S(1)}, u32[]{:S(2)}, u32[]{:S(2)}) %all-to-all-start.4) | async-done | bytes 294944 | tf_op jit(solution)/shard_map/all_to_all | solution.py:354
  141.9 1.7 %final.1 = bf16[16,512]{1,0:T(8,128)(2,1)} custom-call(s32[2]{0:T(128)S(1)} %pad_add_fusion.1.me_ref, f32[16,384]{1,0:T(8,128)S(1)} %get-tuple-element.12.keep_ref, f32[16,384]{1,0:T(8,128)S(1)} %collective-permute-done.come_ref, bf16[16,72,128]{2,1,0:T(8,128)(2,1)S(1)} %all-to-all-done.4.x_ref), custom_call_target="tpu_custom_call" | custom-call | tf_op jit(solution)/shard_map/final/pallas_call | solution.py:361
  (3 shorter events, 0.0 us)
Async XLA Ops:
  0.0 0.7 copy-start.4
  0.7 0.7 copy-start.5
  2.1 16.2 %all-to-all-start = ((bf16[16,72,128]{2,1,0:T(8,128)(2,1)}), bf16[16,72,128]{2,1,0:T(8,128)(2,1)S(1)}, u32[]{:S(2)}, u32[]{:S(2)}) async-start(bf16[16,72,128]{2,1,0:T(8,128)(2,1)} %open.1), calls=%async_computation | async-start | bytes 589824 | tf_op jit(solution)/shard_map/all_to_all | solution.py:354
  50.9 8.7 %copy-start.7 = (s32[1,32,1,2]{1,3,2,0:T(2,128)S(1)}, s32[1,32,1,2]{1,3,2,0:T(2,128)}, u32[]{:S(2)}) copy-start(s32[1,32,1,2]{1,3,2,0:T(2,128)} %param.19) | copy-start | bytes 772
  50.9 8.9 %copy-start.6 = (s32[1,32,1,2,2]{1,4,3,2,0:T(2,128)S(1)}, s32[1,32,1,2,2]{1,4,3,2,0:T(2,128)}, u32[]{:S(2)}) copy-start(s32[1,32,1,2,2]{1,4,3,2,0:T(2,128)} %param.18) | copy-start | bytes 1540
  53.8 6.4 %copy-start.8 = (s32[16,1]{0,1:T(1,128)S(1)}, s32[16,1]{0,1:T(1,128)}, u32[]{:S(2)}) copy-start(s32[16,1]{0,1:T(1,128)} %param.14) | copy-start | bytes 196
  53.8 6.4 %copy-start.9 = (s32[16,1,1]{0,2,1:T(1,128)S(1)}, s32[16,1,1]{0,2,1:T(1,128)}, u32[]{:S(2)}) copy-start(s32[16,1,1]{0,2,1:T(1,128)} %param.13) | copy-start | bytes 196
  53.8 22.5 %copy-start = (bf16[32,16,1024]{2,1,0:T(8,128)(2,1)S(1)}, bf16[32,16,1024]{2,1,0:T(8,128)(2,1)}, u32[]{:S(2)}) copy-start(bf16[32,16,1024]{2,1,0:T(8,128)(2,1)} %lk_ref.1) | copy-start | bytes 3145732
  53.8 22.5 %copy-start.2 = (bf16[16,16,1024]{2,1,0:T(8,128)(2,1)S(1)}, bf16[16,16,1024]{2,1,0:T(8,128)(2,1)}, u32[]{:S(2)}) copy-start(bf16[16,16,1024]{2,1,0:T(8,128)(2,1)} %hk_ref.1) | copy-start | bytes 1572868
  53.8 22.4 %all-to-all-start.2 = ((bf16[32,32,512]{2,1,0:T(8,128)(2,1)}), bf16[32,32,512]{2,1,0:T(8,128)(2,1)S(1)}, u32[]{:S(2)}, u32[]{:S(2)}) async-start(bf16[32,32,512]{2,1,0:T(8,128)(2,1)} %pick.1), calls=%async_computation.2 | async-start | bytes 2097152 | tf_op jit(solution)/shard_map/all_to_all | solution.py:354
  76.3 1.2 copy-start.1
  77.5 1.0 copy-start.3
  88.3 26.0 %all-to-all-start.3 = ((bf16[32,176,128]{2,1,0:T(8,128)(2,1)}), bf16[32,176,128]{2,1,0:T(8,128)(2,1)S(1)}, u32[]{:S(2)}, u32[]{:S(2)}) async-start(bf16[32,176,128]{2,1,0:T(8,128)(2,1)} %attend.1), calls=%async_computation.3 | async-start | bytes 2883584 | tf_op jit(solution)/shard_map/all_to_all | solution.py:354
  116.9 25.1 %all-to-all-start.4 = ((bf16[16,72,128]{2,1,0:T(8,128)(2,1)}), bf16[16,72,128]{2,1,0:T(8,128)(2,1)S(1)}, u32[]{:S(2)}, u32[]{:S(2)}) async-start(bf16[16,72,128]{2,1,0:T(8,128)(2,1)} %get-tuple-element.14), calls=%async_computation.4 | async-start | bytes 589824 | tf_op jit(solution)/shard_map/all_to_all | solution.py:354
  122.7 3.1 %collective-permute-start = (f32[16,384]{1,0:T(8,128)S(1)}, f32[16,384]{1,0:T(8,128)S(1)}, u32[]{:S(2)}, u32[]{:S(2)}) collective-permute-start(f32[16,384]{1,0:T(8,128)S(1)} %get-tuple-element.13), channel_id=1, source_target_pairs={{0,16},{16,0},{32,48},{48,32},{64,80},{80,64},{96,112},{112,96},{1... | collective-permute-start | bytes 73736 | tf_op jit(solution)/shard_map/ppermute | solution.py:451

commit v5 on v3

v5 whole, which is shorter than its diff:
```python
import functools
import math

import jax
import jax.numpy as jnp
import ml_dtypes
import numpy as np
from jax import lax
from jax.experimental import pallas as pl
from jax.experimental.pallas import tpu as pltpu
from jax.sharding import PartitionSpec as P

QH = 64
KVH = 8
HD = 128
N_INST = 32
N_TP = 16
ROWS = 16
SLOTS = 64
WIDTH = 512
CHIPS = N_INST // 2
HALF = SLOTS // 2
PIECE = 4 * HALF + 2 * ROWS + 16
DEAD = -1e30
SCALE = HD ** (-0.5)
F32 = jnp.float32
BF16 = jnp.bfloat16
FACTOR = SCALE * math.log2(math.e)
TWICE_HI = float(np.float32(1 / FACTOR).astype(ml_dtypes.bfloat16))
TWICE_LO = 1 / FACTOR - TWICE_HI


def iota(shape, axis):
    return lax.broadcasted_iota(jnp.int32, shape, axis)


def dot(a, b):
    return jnp.dot(a, b, preferred_element_type=F32)


def dot_nt(a, b):
    return lax.dot_general(a, b, (((1,), (1,)), ((), ())), preferred_element_type=F32)


def split3(x):
    hi = x.astype(BF16).astype(F32)
    rest = x - hi
    mid = rest.astype(BF16).astype(F32)
    return hi, mid, rest - mid


def spread3(x):
    hi, mid, low = split3(x)
    return hi + pltpu.roll(mid, 4, 1) + pltpu.roll(low, 8, 1)


def turn(x, by):
    return pltpu.roll(x, by % 128, 1) if by % 128 else x


def head_rows(h):
    return slice(h * ROWS, (h + 1) * ROWS)


def fold(x):
    lane = iota(x[..., :8, :].shape, x.ndim - 1)
    return jnp.where(lane < 64, x[..., :8, :], pltpu.roll(x[..., 8:, :], 64, x.ndim - 1))


def unfold(x):
    return jnp.concatenate([x, pltpu.roll(x, 64, x.ndim - 1)], axis=x.ndim - 2)


def spread_kernel(me_ref, first_ref, out_ref):
    row = iota((8, 128), 0)
    asked = jnp.zeros((8, 128), F32)
    for t in range(N_TP):
        part = first_ref[t, :, WIDTH:].astype(F32)
        line = turn(part[:8] + turn(part[8:], N_INST), 64 * (t // 8))
        asked = asked + jnp.where(row == t % 8, line, 0.0)
    asked = asked.astype(BF16)
    queries = first_ref[me_ref[1], :, :WIDTH]
    for z in range(CHIPS):
        for h in range(4):
            out_ref[z, head_rows(h), :] = queries[:, h * HD : (h + 1) * HD]
        out_ref[z, 4 * ROWS :, :] = asked


def places(me, mine_ref, g):
    k = iota((256, 128), 0)
    n = iota((256, 128), 1)
    local = jnp.bitwise_and(jnp.right_shift(k, 1), 7)
    order = jnp.where(n == local * 16 + jnp.right_shift(k, 4), 1.0, 0.0).astype(BF16)
    asked = mine_ref[g * 8 : (g + 1) * 8, 4 * ROWS :, :].astype(F32)
    asked = dot(order, unfold(asked).reshape(128, 128).astype(BF16))
    column = 2 * jnp.right_shift(me, 1) + N_INST * jnp.bitwise_and(k, 1)
    ones = jnp.ones((128, 128), BF16)
    base = local.astype(F32) * 16.0
    return [
        dot(jnp.where(n == column + d, asked, 0.0).astype(BF16), ones) + base
        for d in range(2)
    ]


def pick_kernel(me_ref, mine_ref, out_ref, target_ref):
    lane = iota((256, 128), 1).astype(F32)
    for g in range(2):
        block = jnp.concatenate(
            [
                mine_ref[g * 8 : (g + 1) * 8, head_rows(h), :].reshape(128, HD)
                for h in range(4)
            ],
            axis=1,
        )
        for d, target in enumerate(places(me_ref[0], mine_ref, g)):
            onehot = jnp.where(lane == target, 1.0, 0.0).astype(BF16)
            picked = dot(onehot, block).astype(BF16)
            out_ref[d * N_TP : (d + 1) * N_TP, g * 16 : (g + 1) * 16, :] = picked.reshape(
                N_TP, 16, WIDTH
            )
            target_ref[g, :, d * 256 : (d + 1) * 256] = target.T[:8]


def masks_kernel(lent_ref, out_ref):
    token = iota((512, 128), 0)
    block = jnp.right_shift(token, 4)
    place = jnp.bitwise_and(token, 15)
    length = lent_ref[2:3, :]
    first = (block == lent_ref[0:1, :]) & (place < length)
    other = (block == lent_ref[1:2, :]) & (place + 16 < length)
    twice = first & other
    upper = jnp.where(first | other, jnp.where(twice, TWICE_HI, 0.0), DEAD)
    lower = jnp.where(twice, TWICE_LO, 0.0)
    out_ref[...] = jnp.where(iota((512, 128), 1) < SLOTS, upper, lower).astype(BF16)


HEADS = [(tt, h) for tt in range(2) for h in range(4)]


def pool(query, pick, keys, values, count):
    query = jnp.concatenate([query, jnp.concatenate([pick] * 8, axis=0)], axis=1)
    scores = dot_nt(query, keys)
    weights = []
    peaks = []
    for j in range(8):
        part = scores[j * count : (j + 1) * count]
        peak = jnp.max(part, axis=1, keepdims=True)
        weights.append(jnp.exp2((part - peak) * FACTOR).astype(BF16))
        peaks.append(peak)
    mixed = dot(jnp.concatenate(weights, axis=0), values)
    total = mixed[:, HD:]
    return (mixed[:, :HD] / total).astype(BF16), peaks, total


def columns(tt, peaks, total, count):
    lane = iota((count, 128), 1)
    top = jnp.zeros((count, 128), F32)
    amount = jnp.ones((count, 128), F32)
    for h in range(4):
        j = tt * 4 + h
        top = jnp.where(lane == h, peaks[j], top)
        amount = jnp.where(lane == h, total[j * count : (j + 1) * count], amount)
    lse = jnp.where(top > DEAD / 2, top * SCALE + jnp.log(amount), DEAD)
    return jnp.where(lane < 4, lse, 0.0)


def home_kernel(home_ref, first_ref, k_ref, v_ref, out_ref, lse_ref):
    token = iota((256, 128), 0)
    live = (jnp.right_shift(token, 4) == home_ref[0:1, :]) & (
        jnp.bitwise_and(token, 15) < home_ref[1:2, :]
    )
    mask = jnp.where(live, 0.0, DEAD).astype(BF16)
    pick = jnp.where(iota((ROWS, 128), 1) == iota((ROWS, 128), 0), 1.0, 0.0).astype(BF16)
    ones = jnp.ones((256, 128), BF16)
    for k in range(KVH):
        cut = slice(k * HD, (k + 1) * HD)
        keys = jnp.concatenate([k_ref[:, :, cut].reshape(256, HD), mask], axis=1)
        values = jnp.concatenate([v_ref[:, :, cut].reshape(256, HD), ones], axis=1)
        query = [first_ref[2 * k + tt, :, h * HD : (h + 1) * HD] for tt, h in HEADS]
        mixed, peaks, total = pool(jnp.concatenate(query, axis=0), pick, keys, values, ROWS)
        for tt in range(2):
            lse_ref[2 * k + tt] = columns(tt, peaks, total, ROWS)
        for j, (tt, h) in enumerate(HEADS):
            out_ref[2 * k + tt, head_rows(h), :] = mixed[j * ROWS : (j + 1) * ROWS]


def attend_kernel(x_ref, mask_ref, home_ref, home_lse_ref, k_ref, v_ref, out_ref):
    lane = iota((SLOTS, 128), 1)
    pick = jnp.where(
        jnp.bitwise_and(lane, SLOTS - 1) == iota((SLOTS, 128), 0), 1.0, 0.0
    ).astype(BF16)
    mask = mask_ref[...]
    ones = jnp.ones((512, 128), BF16)
    rest = jnp.zeros((ROWS, 128), F32)
    for k in range(KVH):
        cut = slice(k * HD, (k + 1) * HD)
        keys = jnp.concatenate([k_ref[:, :, cut].reshape(512, HD), mask], axis=1)
        values = jnp.concatenate([v_ref[:, :, cut].reshape(512, HD), ones], axis=1)
        query = [
            x_ref[d * N_TP + 2 * k + tt, :, h * HD : (h + 1) * HD]
            for tt, h in HEADS
            for d in range(2)
        ]
        mixed, peaks, total = pool(jnp.concatenate(query, axis=0), pick, keys, values, SLOTS)
        for tt in range(2):
            lse = columns(tt, peaks, total, SLOTS)
            home_lse = home_lse_ref[2 * k + tt]
            column = [lse[:HALF], home_lse, rest, lse[HALF:], home_lse, rest]
            lse = spread3(jnp.concatenate(column, axis=0)).T[:16]
            for d in range(2):
                to = d * N_TP + 2 * k + tt
                for h in range(4):
                    at = (tt * 4 + h) * SLOTS + d * HALF
                    out_ref[to, h * HALF : (h + 1) * HALF, :] = mixed[at : at + HALF]
                out_ref[to, 4 * HALF : PIECE - 16, :] = home_ref[
                    2 * k + tt, 2 * d * ROWS : 2 * (d + 1) * ROWS, :
                ]
                out_ref[to, PIECE - 16 :, :] = turn(lse, 64 * d).astype(BF16)


def merge_kernel(me_ref, target_ref, x_ref, out_ref, keep_ref, give_ref):
    core = jnp.bitwise_and(me_ref[0], 1)
    lane = iota((8, 128), 1)
    lses = []
    for t in range(2 * N_TP):
        parts = x_ref[t, PIECE - 16 :, :].astype(F32)
        lses.append(parts[0:4] + parts[4:8] + parts[8:12])
    lses = [jnp.concatenate([x, x], axis=0) for x in lses]

    def gather(sources, first):
        chunks = []
        for at in range(0, len(sources), 8):
            row = jnp.zeros((8, 128), F32)
            for j in range(8):
                moved = turn(lses[sources[at + j]], 16 * j - first)
                row = jnp.where(jnp.right_shift(lane, 4) == j, moved, row)
            chunks.append(row)
        return jnp.concatenate(chunks, axis=1)

    def join(mask, lse, values):
        score = jnp.where(mask, lse, DEAD)
        peak = jnp.max(score, axis=1, keepdims=True)
        weight = jnp.exp(score - peak)
        total = jnp.sum(weight, axis=1, keepdims=True)
        upper = weight.astype(BF16)
        lower = (weight - upper.astype(F32)).astype(BF16)
        both = dot(jnp.concatenate([upper, lower], axis=0), values)
        count = mask.shape[0]
        return (both[:count] + both[count:]) / total, peak + jnp.log(total)

    rows = iota((128, 512), 0).astype(F32)
    out_lane = iota((128, 128), 1)
    for g in range(2):
        lse = gather(list(range(2 * N_TP)), 16 * g)
        mask = rows == target_ref[g, 0:1, :]
        out_lse = jnp.zeros((128, 128), F32)
        block = slice(g * 8, (g + 1) * 8)
        for h in range(4):
            at = h * HALF + 16 * g
            values = x_ref[:, at : at + 16, :].reshape(512, HD)
            mixed, total = join(mask, lse[h : h + 1, :], values)
            out_lse = jnp.where(out_lane == h, total, out_lse)
            out_ref[block, head_rows(h), :] = mixed.astype(BF16).reshape(8, ROWS, HD)
        out_lse = fold(spread3(out_lse).reshape(8, ROWS, 128))
        out_ref[block, 4 * ROWS :, :] = out_lse.astype(BF16)
    mask = iota((ROWS, 256), 0) == jnp.bitwise_and(iota((ROWS, 256), 1), 15)
    home_lane = iota((ROWS, 128), 1)
    homes = []
    for d in range(2):
        lse = gather(list(range(d * N_TP, (d + 1) * N_TP)), HALF)
        lse = jnp.where(core == 0, lse[0:2], lse[2:4])
        out_lse = jnp.zeros((ROWS, 128), F32)
        parts = []
        for hh in range(2):
            at = 4 * HALF + hh * ROWS
            values = x_ref[d * N_TP : (d + 1) * N_TP, at : at + ROWS, :].reshape(256, HD)
            mixed, total = join(mask, lse[hh : hh + 1, :], values)
            parts.append(mixed)
            out_lse = jnp.where(home_lane == hh, total, out_lse)
        homes.append(jnp.concatenate(parts + [out_lse], axis=1))
    keep_ref[...] = jnp.where(core == 0, homes[0], homes[1])
    give_ref[...] = jnp.where(core == 0, homes[1], homes[0])


def final_kernel(me_ref, keep_ref, come_ref, x_ref, out_ref):
    core = jnp.bitwise_and(me_ref[0], 1)
    low = jnp.where(core == 0, keep_ref[...], come_ref[...])
    high = jnp.where(core == 0, come_ref[...], keep_ref[...])
    lane = iota((ROWS, 128), 1)
    lse = jnp.where(lane < 2, low[:, 2 * HD :], pltpu.roll(high[:, 2 * HD :], 2, 1))
    lses = [lse]
    for c in range(CHIPS):
        parts = unfold(x_ref[c, 4 * ROWS :, :].astype(F32))
        lses.append(parts + turn(parts, -4) + turn(parts, -8))
    peak = functools.reduce(jnp.maximum, lses)
    weights = [jnp.exp(lse - peak) for lse in lses]
    total = sum(weights)
    for h in range(4):
        home = (low if h < 2 else high)[:, (h % 2) * HD : (h % 2 + 1) * HD]
        mixed = weights[0][:, h : h + 1] * home
        for c in range(CHIPS):
            mixed = mixed + weights[c + 1][:, h : h + 1] * x_ref[c, head_rows(h), :].astype(F32)
        out_ref[:, h * HD : (h + 1) * HD] = (mixed / total[:, h : h + 1]).astype(BF16)


VMEM = pl.BlockSpec(memory_space=pltpu.VMEM)
SMEM = pl.BlockSpec(memory_space=pltpu.SMEM)
PARAMS = pltpu.CompilerParams(vmem_limit_bytes=24 * 1024 * 1024)


def exchange(x, axis, groups=None):
    return lax.all_to_all(
        x, axis, split_axis=0, concat_axis=0, axis_index_groups=groups, tiled=True
    )


def call(kernel, name, out_shape, args, smem=0):
    specs = [SMEM] * smem + [VMEM] * (len(args) - smem)
    return pl.pallas_call(
        kernel,
        out_shape=out_shape,
        in_specs=specs,
        out_specs=jax.tree.map(lambda _: VMEM, out_shape),
        compiler_params=PARAMS,
        name=name,
    )(*args)


def per_device(
    queries,
    home_keys,
    home_values,
    home_table,
    home_len,
    lent_keys,
    lent_values,
    lend_row,
    lend_table,
    lend_len,
):
    same_core = [[2 * z + core for z in range(CHIPS)] for core in range(2)]
    plane = [[(2 * z) * N_TP + j for j in range(2 * N_TP)] for z in range(CHIPS)]
    sibling = [(i, i ^ 1) for i in range(N_INST)]
    block = (CHIPS, 4 * ROWS + 8, HD)
    me = jnp.stack([lax.axis_index("inst"), lax.axis_index("tp")]).astype(jnp.int32)

    asked = jnp.pad(lend_row.reshape(N_INST, 2).T.astype(BF16), ((0, 0), (0, 128 - N_INST)))
    asked = jnp.broadcast_to(asked[None, :, None], (N_TP, 2, 8, 128)).reshape(N_TP, ROWS, 128)
    sent = jnp.broadcast_to(queries[None], (N_TP, ROWS, WIDTH))
    first = exchange(jnp.concatenate([sent, asked], axis=2), "tp")
    sent = call(spread_kernel, "spread", jax.ShapeDtypeStruct(block, BF16), (me, first), smem=1)
    mine = exchange(sent, "inst", same_core)

    meta = jnp.concatenate(
        [lend_table.reshape(CHIPS, 2, 2, 2), lend_len.reshape(CHIPS, 2, 2, 1)], axis=3
    )
    meta = meta.transpose(3, 1, 0, 2).reshape(3, SLOTS)
    mask = call(
        masks_kernel,
        "masks",
        jax.ShapeDtypeStruct((512, 128), BF16),
        (jnp.concatenate([meta, meta], axis=1),),
    )
    meta = jnp.concatenate([home_table.reshape(ROWS, 1), home_len], axis=1).T
    meta = jnp.pad(meta, ((0, 0), (0, 128 - ROWS)), constant_values=16)
    home, home_lse = call(
        home_kernel,
        "home",
        (
            jax.ShapeDtypeStruct((N_TP, 4 * ROWS, HD), BF16),
            jax.ShapeDtypeStruct((N_TP, ROWS, 128), F32),
        ),
        (meta, first, home_keys, home_values),
    )
    mine, mask, home, home_lse = lax.optimization_barrier((mine, mask, home, home_lse))

    picked, target = call(
        pick_kernel,
        "pick",
        (
            jax.ShapeDtypeStruct((2 * N_TP, HALF, WIDTH), BF16),
            jax.ShapeDtypeStruct((2, 8, 512), F32),
        ),
        (me, mine),
        smem=1,
    )
    arrived = exchange(picked, ("inst", "tp"), plane)
    partial = call(
        attend_kernel,
        "attend",
        jax.ShapeDtypeStruct((2 * N_TP, PIECE, HD), BF16),
        (arrived, mask, home, home_lse, lent_keys, lent_values),
    )
    returned = exchange(partial, ("inst", "tp"), plane)
    merged, keep, give = call(
        merge_kernel,
        "merge",
        (
            jax.ShapeDtypeStruct(block, BF16),
            jax.ShapeDtypeStruct((ROWS, 3 * HD), F32),
            jax.ShapeDtypeStruct((ROWS, 3 * HD), F32),
        ),
        (me, target, returned),
        smem=1,
    )
    come = lax.ppermute(give, "inst", sibling)
    back = exchange(merged, "inst", same_core)
    return call(
        final_kernel,
        "final",
        jax.ShapeDtypeStruct((ROWS, WIDTH), BF16),
        (me, keep, come, back),
        smem=1,
    )


def solution(mesh):
    in_specs = (
        P("inst", "tp"),
        P(("inst", "tp"), None, None),
        P(("inst", "tp"), None, None),
        P("inst", "tp", None),
        P("inst", "tp"),
        P(("inst", "tp"), None, None),
        P(("inst", "tp"), None, None),
        P("inst", None, "tp", None),
        P("inst", None, "tp", None, None),
        P("inst", None, "tp", None),
    )
    out_specs = P("inst", "tp")
    return jax.shard_map(
        per_device, mesh=mesh, in_specs=in_specs, out_specs=out_specs, check_vma=False
    )
```

time: 143 us -> 135 us (0.944)
  local copies, waits for them, and re-layouts: 13.5 us -> 1.41 us
  blocking collectives: 41.2 us -> 46.9 us
  waiting for transfers between devices: 45.9 us -> 41.4 us
  starting transfers between devices: 26.8 us -> 29.3 us
    unnamed x30 -> x16, local copies, waits for them, and re-layouts: 12.6 us -> 0.05 us
    all_to_all x2, blocking collectives: 41.2 us -> 46.9 us  [exchange(): lax.all_to_all(x, axis, split_axis=0, concat_axis=0, axis_index_groups=gr...]
    all_to_all x3, waiting for transfers between devices: 44.7 us -> 40.2 us  [exchange(): lax.all_to_all(x, axis, split_axis=0, concat_axis=0, axis_index_groups=gr...]
    all_to_all x3, starting transfers between devices: 24.9 us -> 27.4 us  [exchange(): lax.all_to_all(x, axis, split_axis=0, concat_axis=0, axis_index_groups=gr...]
    pallas_call x6 -> x7, Pallas kernels: 12.7 us -> 13.9 us  [call(): pl.pallas_call(kernel, out_shape=out_shape, in_specs=specs, out_specs=jax...]
  transfers between devices with their start and end apart: 4 -> 4, of which waited for: 4 -> 4; matrix products, arithmetic and copies ran while one was open for 0% -> 1% of each run, Pallas kernels for 1% -> 2%
where the time goes in v5:
time: 135 us
  blocking collectives  46.9 us (35%)
  waiting for transfers between devices  41.4 us (31%)
  starting transfers between devices  29.3 us (22%)
  Pallas kernels  13.9 us (10%)
  other arithmetic  1.6 us (1%)
  local copies, waits for them, and re-layouts  1.41 us (1%)
    all_to_all x2, blocking collectives, exchange(): lax.all_to_all(x, axis, split_axis=0, concat_axis=0, axis_index_groups=gr...  46.9 us
    all_to_all x3, waiting for transfers between devices, exchange(): lax.all_to_all(x, axis, split_axis=0, concat_axis=0, axis_index_groups=gr...  40.2 us
    all_to_all x3, starting transfers between devices, exchange(): lax.all_to_all(x, axis, split_axis=0, concat_axis=0, axis_index_groups=gr...  27.4 us
    pallas_call x7, Pallas kernels, call(): pl.pallas_call(kernel, out_shape=out_shape, in_specs=specs, out_specs=jax...  13.9 us
  transfers between devices with their start and end apart: 4, of which 4 were waited for; matrix products, arithmetic and copies ran while one was open for 1% of the time, Pallas kernels for 2%

profile of v5, /device:TPU:64, one launch (start us, length us, event | category | flops | bytes accessed | tf_op | source)
XLA Modules:
  0.0 134.7 jit_solution(8122758961218452313)
XLA Ops:
  0.0 0.7 convert_bitcast_fusion
  0.7 0.0 copy-start.5
  0.7 0.0 copy-start.4
  0.7 0.7 broadcast_in_dim.16
  1.5 0.0 copy-start.6
  1.5 0.0 copy-start.7
  1.5 0.0 copy-start.2
  1.5 0.0 copy-start.3
  1.5 0.7 pad_maximum_fusion
  2.3 7.0 %all-to-all-start = ((bf16[16,16,640]{2,1,0:T(8,128)(2,1)}), bf16[16,16,640]{2,1,0:T(8,128)(2,1)S(1)}, u32[]{:S(2)}, u32[]{:S(2)}) async-start(bf16[16,16,640]{2,1,0:T(8,128)(2,1)} %pad_maximum_fusion), calls=%async_computation | async-start | bytes 655360 | tf_op jit(solution)/shard_map/all_to_all | solution.py:312
  9.3 0.1 pad_add_fusion.1.me_ref
  9.4 9.1 %all-to-all-done.first_ref = bf16[16,16,640]{2,1,0:T(8,128)(2,1)S(1)} async-done(((bf16[16,16,640]{2,1,0:T(8,128)(2,1)}), bf16[16,16,640]{2,1,0:T(8,128)(2,1)S(1)}, u32[]{:S(2)}, u32[]{:S(2)}) %all-to-all-start) | async-done | bytes 327712 | tf_op jit(solution)/shard_map/all_to_all | solution.py:312
  18.5 1.4 %spread.1 = bf16[16,72,128]{2,1,0:T(8,128)(2,1)} custom-call(s32[2]{0:T(128)S(1)} %pad_add_fusion.1.me_ref, bf16[16,16,640]{2,1,0:T(8,128)(2,1)S(1)} %all-to-all-done.first_ref), custom_call_target="tpu_custom_call" | custom-call | tf_op jit(solution)/shard_map/spread/pallas_call | solution.py:319
  19.9 14.8 %all-to-all-start.1 = ((bf16[16,72,128]{2,1,0:T(8,128)(2,1)}), bf16[16,72,128]{2,1,0:T(8,128)(2,1)S(1)}, u32[]{:S(2)}, u32[]{:S(2)}) async-start(bf16[16,72,128]{2,1,0:T(8,128)(2,1)} %spread.1), calls=%async_computation.1 | async-start | bytes 589824 | tf_op jit(solution)/shard_map/all_to_all | solution.py:312
  34.6 0.0 copy-done.5
  34.6 0.1 reshape.19
  34.7 0.1 copy.16
  34.8 0.0 copy-done.4
  34.8 0.1 reshape.18
  34.9 0.1 copy.15
  35.0 0.1 copy.17
  35.1 0.1 reshape.20
  35.3 0.1 pad_add_fusion.lent_ref
  35.3 0.1 masks.1.mask_ref
  35.5 0.0 copy-done.6
  35.5 0.0 copy-done.7
  35.5 0.0 copy-done.2
  35.5 0.0 copy-done.3
  35.6 2.3 %home.1 = (bf16[16,64,128]{2,1,0:T(8,128)(2,1)S(1)}, f32[16,16,128]{2,1,0:T(8,128)S(1)}) custom-call(s32[2,128]{1,0:T(2,128)S(1)} %pad.9.home_ref, bf16[16,16,640]{2,1,0:T(8,128)(2,1)S(1)} %all-to-all-done.first_ref, bf16[16,16,1024]{2,1,0:T(8,128)(2,1)S(1)} %copy-done.2, bf16[16,16,1024]{2,1,0:T(8,128)(2,1)S(1)} %copy-done.3), custom_call_target="tpu_custom_call" | custom-call | tf_op jit(solution)/shard_map/home/pallas_call | solution.py:319
  37.9 0.0 copy-start
  37.9 0.0 copy-start.1
  37.9 15.0 %all-to-all-done.1.mine_ref = bf16[16,72,128]{2,1,0:T(8,128)(2,1)S(1)} async-done(((bf16[16,72,128]{2,1,0:T(8,128)(2,1)}), bf16[16,72,128]{2,1,0:T(8,128)(2,1)S(1)}, u32[]{:S(2)}, u32[]{:S(2)}) %all-to-all-start.1) | async-done | bytes 294944 | tf_op jit(solution)/shard_map/all_to_all | solution.py:312
  52.9 1.5 %pick.1 = (bf16[32,32,512]{2,1,0:T(8,128)(2,1)S(1)}, f32[2,8,512]{2,1,0:T(8,128)S(1)}) custom-call(s32[2]{0:T(128)S(1)} %pad_add_fusion.1.me_ref, bf16[16,72,128]{2,1,0:T(8,128)(2,1)S(1)} %all-to-all-done.1.mine_ref), custom_call_target="tpu_custom_call" | custom-call | tf_op jit(solution)/shard_map/pick/pallas_call | solution.py:319
  54.5 21.7 %all_to_all.25.x_ref = bf16[32,32,512]{2,1,0:T(8,128)(2,1)S(1)} all-to-all(bf16[32,32,512]{2,1,0:T(8,128)(2,1)S(1)} %get-tuple-element.20), channel_id=1, replica_groups={{0,1,2,3,4,5,6,7,8,9,10,11,12,13,14,15,16,17,18,19,20,21,22,23,24,25,26..., dimensions={0} | all-to-all | bytes 2097152 | tf_op jit(solution)/shard_map/all_to_all | solution.py:312
  76.2 0.0 copy-done
  76.2 0.0 copy-done.1
  76.2 4.3 %attend.1 = bf16[32,176,128]{2,1,0:T(8,128)(2,1)S(1)} custom-call(bf16[32,32,512]{2,1,0:T(8,128)(2,1)S(1)} %all_to_all.25.x_ref, bf16[512,128]{1,0:T(8,128)(2,1)S(1)} %masks.1.mask_ref, bf16[16,64,128]{2,1,0:T(8,128)(2,1)S(1)} %get-tuple-element.22.home_ref, f32[16,16,128]{2,1,0:T(8,128)S(1)} %get-tuple-element.23.home_lse_ref, ...), custom_call_target="tpu_custom_call" | custom-call | tf_op jit(solution)/shard_map/attend/pallas_call | solution.py:319
  80.5 25.2 %all_to_all.26.x_ref = bf16[32,176,128]{2,1,0:T(8,128)(2,1)S(1)} all-to-all(bf16[32,176,128]{2,1,0:T(8,128)(2,1)S(1)} %attend.1), channel_id=1, replica_groups={{0,1,2,3,4,5,6,7,8,9,10,11,12,13,14,15,16,17,18,19,20,21,22,23,24,25,26..., dimensions={0} | all-to-all | bytes 2883584 | tf_op jit(solution)/shard_map/all_to_all | solution.py:312
  105.7 2.7 %merge.1 = (bf16[16,72,128]{2,1,0:T(8,128)(2,1)}, f32[16,384]{1,0:T(8,128)S(1)}, f32[16,384]{1,0:T(8,128)S(1)}) custom-call(s32[2]{0:T(128)S(1)} %pad_add_fusion.1.me_ref, f32[2,8,512]{2,1,0:T(8,128)S(1)} %get-tuple-element.19.target_ref, bf16[32,176,128]{2,1,0:T(8,128)(2,1)S(1)} %all_to_all.26.x_ref), custom_call_target="tpu_custom_call" | custom-call | tf_op jit(solution)/shard_map/merge/pallas_call | solution.py:319
  108.3 5.6 %all-to-all-start.4 = ((bf16[16,72,128]{2,1,0:T(8,128)(2,1)}), bf16[16,72,128]{2,1,0:T(8,128)(2,1)S(1)}, u32[]{:S(2)}, u32[]{:S(2)}) async-start(bf16[16,72,128]{2,1,0:T(8,128)(2,1)} %get-tuple-element.26), calls=%async_computation.4 | async-start | bytes 589824 | tf_op jit(solution)/shard_map/all_to_all | solution.py:312
  113.9 1.9 %collective-permute-start = (f32[16,384]{1,0:T(8,128)S(1)}, f32[16,384]{1,0:T(8,128)S(1)}, u32[]{:S(2)}, u32[]{:S(2)}) collective-permute-start(f32[16,384]{1,0:T(8,128)S(1)} %get-tuple-element.25), channel_id=1, source_target_pairs={{0,16},{16,0},{32,48},{48,32},{64,80},{80,64},{96,112},{112,96},{1... | collective-permute-start | bytes 73736 | tf_op jit(solution)/shard_map/ppermute | solution.py:406
  115.8 1.2 collective-permute-done.come_ref
  117.0 16.1 %all-to-all-done.4.x_ref = bf16[16,72,128]{2,1,0:T(8,128)(2,1)S(1)} async-done(((bf16[16,72,128]{2,1,0:T(8,128)(2,1)}), bf16[16,72,128]{2,1,0:T(8,128)(2,1)S(1)}, u32[]{:S(2)}, u32[]{:S(2)}) %all-to-all-start.4) | async-done | bytes 294944 | tf_op jit(solution)/shard_map/all_to_all | solution.py:312
  133.1 1.6 %final.1 = bf16[16,512]{1,0:T(8,128)(2,1)} custom-call(s32[2]{0:T(128)S(1)} %pad_add_fusion.1.me_ref, f32[16,384]{1,0:T(8,128)S(1)} %get-tuple-element.24.keep_ref, f32[16,384]{1,0:T(8,128)S(1)} %collective-permute-done.come_ref, bf16[16,72,128]{2,1,0:T(8,128)(2,1)S(1)} %all-to-all-done.4.x_ref), custom_call_target="tpu_custom_call" | custom-call | tf_op jit(solution)/shard_map/final/pallas_call | solution.py:319
  (6 shorter events, 0.0 us)
Async XLA Ops:
  0.7 33.9 %copy-start.5 = (s32[1,32,1,2]{1,3,2,0:T(2,128)S(1)}, s32[1,32,1,2]{1,3,2,0:T(2,128)}, u32[]{:S(2)}) copy-start(s32[1,32,1,2]{1,3,2,0:T(2,128)} %param.19) | copy-start | bytes 772
  0.7 34.1 %copy-start.4 = (s32[1,32,1,2,2]{1,4,3,2,0:T(2,128)S(1)}, s32[1,32,1,2,2]{1,4,3,2,0:T(2,128)}, u32[]{:S(2)}) copy-start(s32[1,32,1,2,2]{1,4,3,2,0:T(2,128)} %param.18) | copy-start | bytes 1540
  1.5 34.0 %copy-start.6 = (s32[16,1]{0,1:T(1,128)S(1)}, s32[16,1]{0,1:T(1,128)}, u32[]{:S(2)}) copy-start(s32[16,1]{0,1:T(1,128)} %param.14) | copy-start | bytes 196
  1.5 34.0 %copy-start.7 = (s32[16,1,1]{0,2,1:T(1,128)S(1)}, s32[16,1,1]{0,2,1:T(1,128)}, u32[]{:S(2)}) copy-start(s32[16,1,1]{0,2,1:T(1,128)} %param.13) | copy-start | bytes 196
  1.5 34.0 %copy-start.2 = (bf16[16,16,1024]{2,1,0:T(8,128)(2,1)S(1)}, bf16[16,16,1024]{2,1,0:T(8,128)(2,1)}, u32[]{:S(2)}) copy-start(bf16[16,16,1024]{2,1,0:T(8,128)(2,1)} %k_ref.2) | copy-start | bytes 1572868
  1.5 34.0 %copy-start.3 = (bf16[16,16,1024]{2,1,0:T(8,128)(2,1)S(1)}, bf16[16,16,1024]{2,1,0:T(8,128)(2,1)}, u32[]{:S(2)}) copy-start(bf16[16,16,1024]{2,1,0:T(8,128)(2,1)} %v_ref.2) | copy-start | bytes 1572868
  2.3 16.2 %all-to-all-start = ((bf16[16,16,640]{2,1,0:T(8,128)(2,1)}), bf16[16,16,640]{2,1,0:T(8,128)(2,1)S(1)}, u32[]{:S(2)}, u32[]{:S(2)}) async-start(bf16[16,16,640]{2,1,0:T(8,128)(2,1)} %pad_maximum_fusion), calls=%async_computation | async-start | bytes 655360 | tf_op jit(solution)/shard_map/all_to_all | solution.py:312
  19.9 33.0 %all-to-all-start.1 = ((bf16[16,72,128]{2,1,0:T(8,128)(2,1)}), bf16[16,72,128]{2,1,0:T(8,128)(2,1)S(1)}, u32[]{:S(2)}, u32[]{:S(2)}) async-start(bf16[16,72,128]{2,1,0:T(8,128)(2,1)} %spread.1), calls=%async_computation.1 | async-start | bytes 589824 | tf_op jit(solution)/shard_map/all_to_all | solution.py:312
  37.9 38.3 %copy-start = (bf16[32,16,1024]{2,1,0:T(8,128)(2,1)S(1)}, bf16[32,16,1024]{2,1,0:T(8,128)(2,1)}, u32[]{:S(2)}) copy-start(bf16[32,16,1024]{2,1,0:T(8,128)(2,1)} %k_ref.3) | copy-start | bytes 3145732
  37.9 38.3 %copy-start.1 = (bf16[32,16,1024]{2,1,0:T(8,128)(2,1)S(1)}, bf16[32,16,1024]{2,1,0:T(8,128)(2,1)}, u32[]{:S(2)}) copy-start(bf16[32,16,1024]{2,1,0:T(8,128)(2,1)} %v_ref.3) | copy-start | bytes 3145732
  108.3 24.8 %all-to-all-start.4 = ((bf16[16,72,128]{2,1,0:T(8,128)(2,1)}), bf16[16,72,128]{2,1,0:T(8,128)(2,1)S(1)}, u32[]{:S(2)}, u32[]{:S(2)}) async-start(bf16[16,72,128]{2,1,0:T(8,128)(2,1)} %get-tuple-element.26), calls=%async_computation.4 | async-start | bytes 589824 | tf_op jit(solution)/shard_map/all_to_all | solution.py:312
  113.9 3.1 %collective-permute-start = (f32[16,384]{1,0:T(8,128)S(1)}, f32[16,384]{1,0:T(8,128)S(1)}, u32[]{:S(2)}, u32[]{:S(2)}) collective-permute-start(f32[16,384]{1,0:T(8,128)S(1)} %get-tuple-element.25), channel_id=1, source_target_pairs={{0,16},{16,0},{32,48},{48,32},{64,80},{80,64},{96,112},{112,96},{1... | collective-permute-start | bytes 73736 | tf_op jit(solution)/shard_map/ppermute | solution.py:406

commit v6 on v5

--- a/solution.py
+++ b/solution.py
@@ -49,51 +49,53 @@
     return hi, mid, rest - mid
 
 
-def spread3(x):
+def thirds(x, lane):
     hi, mid, low = split3(x)
-    return hi + pltpu.roll(mid, 4, 1) + pltpu.roll(low, 8, 1)
-
-
-def turn(x, by):
-    return pltpu.roll(x, by % 128, 1) if by % 128 else x
+    return jnp.where(lane < 4, hi, jnp.where(lane < 8, mid, jnp.where(lane < 12, low, 0.0)))
 
 
 def head_rows(h):
     return slice(h * ROWS, (h + 1) * ROWS)
 
 
-def fold(x):
-    lane = iota(x[..., :8, :].shape, x.ndim - 1)
-    return jnp.where(lane < 64, x[..., :8, :], pltpu.roll(x[..., 8:, :], 64, x.ndim - 1))
-
-
-def unfold(x):
-    return jnp.concatenate([x, pltpu.roll(x, 64, x.ndim - 1)], axis=x.ndim - 2)
-
-
-def spread_kernel(me_ref, first_ref, out_ref):
+def spread_kernel(me_ref, first_ref, out_ref, block_s, sems):
     row = iota((8, 128), 0)
-    asked = jnp.zeros((8, 128), F32)
+    quarters = []
+    for half in range(2):
+        for s in range(2):
+            asked = jnp.zeros((8, 128), F32)
+            for t in range(8):
+                part = first_ref[8 * half + t, :, WIDTH:].astype(F32)
+                asked = jnp.where(row == t, part[8 * s : 8 * (s + 1)], asked)
+            quarters.append(asked)
+    asked = quarters[0]
+    for j in range(1, 4):
+        asked = asked + pltpu.roll(quarters[j], j * N_INST, 1)
+    queries = jnp.zeros((ROWS, WIDTH), F32)
     for t in range(N_TP):
-        part = first_ref[t, :, WIDTH:].astype(F32)
-        line = turn(part[:8] + turn(part[8:], N_INST), 64 * (t // 8))
-        asked = asked + jnp.where(row == t % 8, line, 0.0)
-    asked = asked.astype(BF16)
-    queries = first_ref[me_ref[1], :, :WIDTH]
-    for z in range(CHIPS):
-        for h in range(4):
-            out_ref[z, head_rows(h), :] = queries[:, h * HD : (h + 1) * HD]
-        out_ref[z, 4 * ROWS :, :] = asked
+        own = jnp.concatenate([me_ref[1]] * 2, axis=0)[:, :1] == t
+        queries = jnp.where(own, first_ref[t, :, :WIDTH].astype(F32), queries)
+    queries = queries.astype(BF16)
+    for h in range(4):
+        block_s[head_rows(h), :] = queries[:, h * HD : (h + 1) * HD]
+    block_s[4 * ROWS :, :] = asked.astype(BF16)
+    copies = [pltpu.make_async_copy(block_s, out_ref.at[z], sems.at[z]) for z in range(CHIPS)]
+    for copy in copies:
+        copy.start()
+    for copy in copies:
+        copy.wait()
 
 
 def places(me, mine_ref, g):
     k = iota((256, 128), 0)
     n = iota((256, 128), 1)
     local = jnp.bitwise_and(jnp.right_shift(k, 1), 7)
-    order = jnp.where(n == local * 16 + jnp.right_shift(k, 4), 1.0, 0.0).astype(BF16)
-    asked = mine_ref[g * 8 : (g + 1) * 8, 4 * ROWS :, :].astype(F32)
-    asked = dot(order, unfold(asked).reshape(128, 128).astype(BF16))
-    column = 2 * jnp.right_shift(me, 1) + N_INST * jnp.bitwise_and(k, 1)
+    source = local * 8 + jnp.bitwise_and(jnp.right_shift(k, 4), 7)
+    order = jnp.where(n == source, 1.0, 0.0).astype(BF16)
+    asked = mine_ref[g * 8 : (g + 1) * 8, 4 * ROWS :, :].astype(F32).reshape(64, 128)
+    asked = dot(order[:, :64], asked.astype(BF16))
+    column = 2 * N_INST * jnp.right_shift(k, 7) + N_INST * jnp.bitwise_and(k, 1)
+    column = column + 2 * jnp.right_shift(me, 1)
     ones = jnp.ones((128, 128), BF16)
     base = local.astype(F32) * 16.0
     return [
@@ -112,7 +114,7 @@
             ],
             axis=1,
         )
-        for d, target in enumerate(places(me_ref[0], mine_ref, g)):
+        for d, target in enumerate(places(me_ref[0, :1], mine_ref, g)):
             onehot = jnp.where(lane == target, 1.0, 0.0).astype(BF16)
             picked = dot(onehot, block).astype(BF16)
             out_ref[d * N_TP : (d + 1) * N_TP, g * 16 : (g + 1) * 16, :] = picked.reshape(
@@ -153,15 +155,14 @@
 
 
 def columns(tt, peaks, total, count):
-    lane = iota((count, 128), 1)
+    head = jnp.bitwise_and(iota((count, 128), 1), 3)
     top = jnp.zeros((count, 128), F32)
     amount = jnp.ones((count, 128), F32)
     for h in range(4):
         j = tt * 4 + h
-        top = jnp.where(lane == h, peaks[j], top)
-        amount = jnp.where(lane == h, total[j * count : (j + 1) * count], amount)
-    lse = jnp.where(top > DEAD / 2, top * SCALE + jnp.log(amount), DEAD)
-    return jnp.where(lane < 4, lse, 0.0)
+        top = jnp.where(head == h, peaks[j], top)
+        amount = jnp.where(head == h, total[j * count : (j + 1) * count], amount)
+    return jnp.where(top > DEAD / 2, top * SCALE + jnp.log(amount), DEAD)
 
 
 def home_kernel(home_ref, first_ref, k_ref, v_ref, out_ref, lse_ref):
@@ -206,7 +207,7 @@
             lse = columns(tt, peaks, total, SLOTS)
             home_lse = home_lse_ref[2 * k + tt]
             column = [lse[:HALF], home_lse, rest, lse[HALF:], home_lse, rest]
-            lse = spread3(jnp.concatenate(column, axis=0)).T[:16]
+            lse = thirds(jnp.concatenate(column, axis=0), iota((128, 128), 1)).T[:16].astype(BF16)
             for d in range(2):
                 to = d * N_TP + 2 * k + tt
                 for h in range(4):
@@ -215,43 +216,52 @@
                 out_ref[to, 4 * HALF : PIECE - 16, :] = home_ref[
                     2 * k + tt, 2 * d * ROWS : 2 * (d + 1) * ROWS, :
                 ]
-                out_ref[to, PIECE - 16 :, :] = turn(lse, 64 * d).astype(BF16)
+                out_ref[to, PIECE - 16 :, :] = lse
 
 
 def merge_kernel(me_ref, target_ref, x_ref, out_ref, keep_ref, give_ref):
-    core = jnp.bitwise_and(me_ref[0], 1)
-    lane = iota((8, 128), 1)
+    core = jnp.bitwise_and(me_ref[0, :1], 1)
+    rows = [
+        jnp.concatenate(
+            [x_ref[8 * chunk + j, PIECE - 16 :, :] for j in range(8)], axis=1
+        )
+        for chunk in range(4)
+    ]
+    k = iota((1024, 3 * 128), 0)
+    n = iota((1024, 3 * 128), 1)
+    place = jnp.bitwise_and(n, 127)
+    source = 128 * jnp.right_shift(place, 4) + 64 * jnp.concatenate([core] * 3, axis=1)
+    source = source + 16 * jnp.right_shift(n, 7) + jnp.bitwise_and(place, 15)
+    moved = dot(jnp.concatenate(rows, axis=0), jnp.where(k == source, 1.0, 0.0).astype(BF16))
     lses = []
-    for t in range(2 * N_TP):
-        parts = x_ref[t, PIECE - 16 :, :].astype(F32)
-        lses.append(parts[0:4] + parts[4:8] + parts[8:12])
-    lses = [jnp.concatenate([x, x], axis=0) for x in lses]
-
-    def gather(sources, first):
-        chunks = []
-        for at in range(0, len(sources), 8):
-            row = jnp.zeros((8, 128), F32)
-            for j in range(8):
-                moved = turn(lses[sources[at + j]], 16 * j - first)
-                row = jnp.where(jnp.right_shift(lane, 4) == j, moved, row)
-            chunks.append(row)
-        return jnp.concatenate(chunks, axis=1)
+    for chunk in range(4):
+        part = moved[16 * chunk : 16 * (chunk + 1)]
+        lses.append(part[0:4] + part[4:8] + part[8:12])
+
+    def gather(group, chunks):
+        cut = slice(group * 128, (group + 1) * 128)
+        return jnp.concatenate([lses[chunk][:, cut] for chunk in chunks], axis=1)
+
+    ones = jnp.ones((512, HD), BF16)
 
     def join(mask, lse, values):
         score = jnp.where(mask, lse, DEAD)
         peak = jnp.max(score, axis=1, keepdims=True)
         weight = jnp.exp(score - peak)
-        total = jnp.sum(weight, axis=1, keepdims=True)
         upper = weight.astype(BF16)
         lower = (weight - upper.astype(F32)).astype(BF16)
+        values = jnp.concatenate([values, ones[: values.shape[0]]], axis=1)
         both = dot(jnp.concatenate([upper, lower], axis=0), values)
         count = mask.shape[0]
-        return (both[:count] + both[count:]) / total, peak + jnp.log(total)
+        both = both[:count] + both[count:]
+        return both[:, :HD] / both[:, HD:], peak + jnp.log(both[:, HD:])
 
     rows = iota((128, 512), 0).astype(F32)
-    out_lane = iota((128, 128), 1)
+    row = jnp.bitwise_and(iota((128, 128), 0), 8)
+    lane = iota((128, 128), 1) - 8 * row
+    head = jnp.bitwise_and(lane, 3)
     for g in range(2):
-        lse = gather(list(range(2 * N_TP)), 16 * g)
+        lse = gather(g, range(4))
         mask = rows == target_ref[g, 0:1, :]
         out_lse = jnp.zeros((128, 128), F32)
         block = slice(g * 8, (g + 1) * 8)
@@ -259,52 +269,56 @@
             at = h * HALF + 16 * g
             values = x_ref[:, at : at + 16, :].reshape(512, HD)
             mixed, total = join(mask, lse[h : h + 1, :], values)
-            out_lse = jnp.where(out_lane == h, total, out_lse)
+            out_lse = jnp.where(head == h, total, out_lse)
             out_ref[block, head_rows(h), :] = mixed.astype(BF16).reshape(8, ROWS, HD)
-        out_lse = fold(spread3(out_lse).reshape(8, ROWS, 128))
-        out_ref[block, 4 * ROWS :, :] = out_lse.astype(BF16)
+        out_lse = jnp.where(lane >= 0, thirds(out_lse, lane), 0.0).reshape(8, ROWS, 128)
+        out_ref[block, 4 * ROWS :, :] = (out_lse[:, :8] + out_lse[:, 8:]).astype(BF16)
     mask = iota((ROWS, 256), 0) == jnp.bitwise_and(iota((ROWS, 256), 1), 15)
-    home_lane = iota((ROWS, 128), 1)
     homes = []
     for d in range(2):
-        lse = gather(list(range(d * N_TP, (d + 1) * N_TP)), HALF)
-        lse = jnp.where(core == 0, lse[0:2], lse[2:4])
-        out_lse = jnp.zeros((ROWS, 128), F32)
+        lse = gather(2, range(2 * d, 2 * d + 2))
+        lse = jnp.where(core[:, :1] == 0, lse[0:2], lse[2:4])
         parts = []
         for hh in range(2):
             at = 4 * HALF + hh * ROWS
             values = x_ref[d * N_TP : (d + 1) * N_TP, at : at + ROWS, :].reshape(256, HD)
-            mixed, total = join(mask, lse[hh : hh + 1, :], values)
-            parts.append(mixed)
-            out_lse = jnp.where(home_lane == hh, total, out_lse)
-        homes.append(jnp.concatenate(parts + [out_lse], axis=1))
-    keep_ref[...] = jnp.where(core == 0, homes[0], homes[1])
-    give_ref[...] = jnp.where(core == 0, homes[1], homes[0])
+            parts.extend(join(mask, lse[hh : hh + 1, :], values))
+        homes.append(jnp.concatenate(parts, axis=1))
+    keep_ref[...] = jnp.where(core[:, :1] == 0, homes[0], homes[1])
+    give_ref[...] = jnp.where(core[:, :1] == 0, homes[1], homes[0])
 
 
 def final_kernel(me_ref, keep_ref, come_ref, x_ref, out_ref):
-    core = jnp.bitwise_and(me_ref[0], 1)
-    low = jnp.where(core == 0, keep_ref[...], come_ref[...])
-    high = jnp.where(core == 0, come_ref[...], keep_ref[...])
-    lane = iota((ROWS, 128), 1)
-    lse = jnp.where(lane < 2, low[:, 2 * HD :], pltpu.roll(high[:, 2 * HD :], 2, 1))
-    lses = [lse]
-    for c in range(CHIPS):
-        parts = unfold(x_ref[c, 4 * ROWS :, :].astype(F32))
-        lses.append(parts + turn(parts, -4) + turn(parts, -8))
-    peak = functools.reduce(jnp.maximum, lses)
-    weights = [jnp.exp(lse - peak) for lse in lses]
-    total = sum(weights)
+    core = jnp.bitwise_and(me_ref[0, :1], 1)
+    low = jnp.where(core[:, :1] == 0, keep_ref[...], come_ref[...])
+    high = jnp.where(core[:, :1] == 0, come_ref[...], keep_ref[...])
+    blocks = [x_ref[c].astype(F32) for c in range(CHIPS)]
+    n = iota((128, 1024), 1)
+    lane = iota((128, 1024), 0) - 64 * jnp.right_shift(n, 9)
+    head = jnp.bitwise_and(jnp.right_shift(n, 7), 3)
+    part = (lane >= 0) & (lane < 12) & (jnp.bitwise_and(lane, 3) == head)
+    lses = jnp.concatenate([block[4 * ROWS :] for block in blocks], axis=0).astype(BF16)
+    lses = dot(lses, jnp.where(part, 1.0, 0.0).astype(BF16))
     for h in range(4):
-        home = (low if h < 2 else high)[:, (h % 2) * HD : (h % 2 + 1) * HD]
-        mixed = weights[0][:, h : h + 1] * home
-        for c in range(CHIPS):
-            mixed = mixed + weights[c + 1][:, h : h + 1] * x_ref[c, head_rows(h), :].astype(F32)
-        out_ref[:, h * HD : (h + 1) * HD] = (mixed / total[:, h : h + 1]).astype(BF16)
+        home = (low if h < 2 else high)[:, (h % 2) * 2 * HD : (h % 2 + 1) * 2 * HD]
+        halves = []
+        for half in range(2):
+            at = (half * 4 + h) * 128
+            rows = slice(half * 8, (half + 1) * 8)
+            parts = [lses[c * 8 : (c + 1) * 8, at : at + 128] for c in range(CHIPS)]
+            peak = functools.reduce(jnp.maximum, parts, home[rows, HD:])
+            total = jnp.exp(home[rows, HD:] - peak)
+            mixed = total * home[rows, :HD]
+            for c in range(CHIPS):
+                weight = jnp.exp(parts[c] - peak)
+                total = total + weight
+                at = h * ROWS + half * 8
+                mixed = mixed + weight * blocks[c][at : at + 8]
+            halves.append(mixed / total)
+        out_ref[:, h * HD : (h + 1) * HD] = jnp.concatenate(halves, axis=0).astype(BF16)
 
 
 VMEM = pl.BlockSpec(memory_space=pltpu.VMEM)
-SMEM = pl.BlockSpec(memory_space=pltpu.SMEM)
 PARAMS = pltpu.CompilerParams(vmem_limit_bytes=24 * 1024 * 1024)
 
 
@@ -314,12 +328,11 @@
     )
 
 
-def call(kernel, name, out_shape, args, smem=0):
-    specs = [SMEM] * smem + [VMEM] * (len(args) - smem)
+def call(kernel, name, out_shape, args):
     return pl.pallas_call(
         kernel,
         out_shape=out_shape,
-        in_specs=specs,
+        in_specs=[VMEM] * len(args),
         out_specs=jax.tree.map(lambda _: VMEM, out_shape),
         compiler_params=PARAMS,
         name=name,
@@ -343,12 +356,22 @@
     sibling = [(i, i ^ 1) for i in range(N_INST)]
     block = (CHIPS, 4 * ROWS + 8, HD)
     me = jnp.stack([lax.axis_index("inst"), lax.axis_index("tp")]).astype(jnp.int32)
+    me = jnp.broadcast_to(me[:, None, None], (2, 8, 128))
 
     asked = jnp.pad(lend_row.reshape(N_INST, 2).T.astype(BF16), ((0, 0), (0, 128 - N_INST)))
-    asked = jnp.broadcast_to(asked[None, :, None], (N_TP, 2, 8, 128)).reshape(N_TP, ROWS, 128)
-    sent = jnp.broadcast_to(queries[None], (N_TP, ROWS, WIDTH))
-    first = exchange(jnp.concatenate([sent, asked], axis=2), "tp")
-    sent = call(spread_kernel, "spread", jax.ShapeDtypeStruct(block, BF16), (me, first), smem=1)
+    asked = jnp.broadcast_to(asked[:, None], (2, 8, 128)).reshape(ROWS, 128)
+    sent, me = lax.optimization_barrier((jnp.concatenate([queries, asked], axis=1), me))
+    sent = jnp.broadcast_to(sent[None], (N_TP, ROWS, WIDTH + 128))
+    first = exchange(sent, "tp")
+    sent = pl.pallas_call(
+        spread_kernel,
+        out_shape=jax.ShapeDtypeStruct(block, BF16),
+        in_specs=[VMEM, VMEM],
+        out_specs=pl.BlockSpec(memory_space=pl.ANY),
+        scratch_shapes=[pltpu.VMEM(block[1:], BF16), pltpu.SemaphoreType.DMA((CHIPS,))],
+        compiler_params=PARAMS,
+        name="spread",
+    )(me, first)
     mine = exchange(sent, "inst", same_core)
 
     meta = jnp.concatenate(
@@ -382,7 +405,6 @@
             jax.ShapeDtypeStruct((2, 8, 512), F32),
         ),
         (me, mine),
-        smem=1,
     )
     arrived = exchange(picked, ("inst", "tp"), plane)
     partial = call(
@@ -397,11 +419,10 @@
         "merge",
         (
             jax.ShapeDtypeStruct(block, BF16),
-            jax.ShapeDtypeStruct((ROWS, 3 * HD), F32),
-            jax.ShapeDtypeStruct((ROWS, 3 * HD), F32),
+            jax.ShapeDtypeStruct((ROWS, 4 * HD), F32),
+            jax.ShapeDtypeStruct((ROWS, 4 * HD), F32),
         ),
         (me, target, returned),
-        smem=1,
     )
     come = lax.ppermute(give, "inst", sibling)
     back = exchange(merged, "inst", same_core)
@@ -410,7 +431,6 @@
         "final",
         jax.ShapeDtypeStruct((ROWS, WIDTH), BF16),
         (me, keep, come, back),
-        smem=1,
     )
 
 

time: 135 us -> 131 us (0.970)
  blocking collectives: 46.9 us -> 62.9 us
  waiting for transfers between devices: 41.4 us -> 32.3 us
  starting transfers between devices: 29.3 us -> 22.2 us
  Pallas kernels: 13.9 us -> 10.6 us
    all_to_all x2 -> x3, blocking collectives: 46.9 us -> 62.9 us  [exchange(): lax.all_to_all(x, axis, split_axis=0, concat_axis=0, axis_index_groups=gr...]
    all_to_all x3 -> x2, waiting for transfers between devices: 40.2 us -> 31.1 us  [exchange(): lax.all_to_all(x, axis, split_axis=0, concat_axis=0, axis_index_groups=gr...]
    all_to_all x3 -> x2, starting transfers between devices: 27.4 us -> 20.3 us  [exchange(): lax.all_to_all(x, axis, split_axis=0, concat_axis=0, axis_index_groups=gr...]
    pallas_call x7, Pallas kernels: 13.9 us -> 10.6 us  [the longest x6 9.69 us: call(): pl.pallas_call(kernel, out_shape=out_shape, in_specs=[VMEM] * len(args),...]
  transfers between devices with their start and end apart: 4 -> 3, of which waited for: 4 -> 3; matrix products, arithmetic and copies ran while one was open for 1% -> 1% of each run, Pallas kernels for 2% -> 2%
where the time goes in v6:
time: 131 us
  blocking collectives  62.9 us (48%)
  waiting for transfers between devices  32.3 us (25%)
  starting transfers between devices  22.2 us (17%)
  Pallas kernels  10.6 us (8%)
  other arithmetic  1.66 us (1%)
    all_to_all x3, blocking collectives, exchange(): lax.all_to_all(x, axis, split_axis=0, concat_axis=0, axis_index_groups=gr...  62.9 us
    all_to_all x2, waiting for transfers between devices, exchange(): lax.all_to_all(x, axis, split_axis=0, concat_axis=0, axis_index_groups=gr...  31.1 us
    all_to_all x2, starting transfers between devices, exchange(): lax.all_to_all(x, axis, split_axis=0, concat_axis=0, axis_index_groups=gr...  20.3 us
    pallas_call x6, Pallas kernels, call(): pl.pallas_call(kernel, out_shape=out_shape, in_specs=[VMEM] * len(args),...  9.69 us
  transfers between devices with their start and end apart: 3, of which 3 were waited for; matrix products, arithmetic and copies ran while one was open for 1% of the time, Pallas kernels for 2%

profile of v6, /device:TPU:64, one launch (start us, length us, event | category | flops | bytes accessed | tf_op | source)
XLA Modules:
  0.0 130.6 jit_solution(3227371531230467883)
XLA Ops:
  0.0 0.0 copy-start.5
  0.0 0.0 copy-start.4
  0.0 0.0 copy-start.6
  0.0 0.0 copy-start.7
  0.0 0.0 copy-start.3
  0.0 0.0 copy-start.2
  0.0 0.8 convert_bitcast_fusion
  0.8 0.1 pad_add_fusion.1
  0.9 0.7 pad_maximum_fusion
  1.6 0.1 broadcast_in_dim.7.me_ref
  1.7 16.0 %all_to_all.25.first_ref = bf16[16,16,640]{2,1,0:T(8,128)(2,1)S(1)} all-to-all(bf16[16,16,640]{2,1,0:T(8,128)(2,1)S(1)} %broadcast_in_dim.8), channel_id=1, replica_groups=mesh['inst'=32,'tp'=16] {'tp'}, dimensions={0} | all-to-all | bytes 655360 | tf_op jit(solution)/shard_map/all_to_all | solution.py:326
  17.7 0.9 spread.1
  18.7 14.8 %all-to-all-start.1 = ((bf16[16,72,128]{2,1,0:T(8,128)(2,1)}), bf16[16,72,128]{2,1,0:T(8,128)(2,1)S(1)}, u32[]{:S(2)}, u32[]{:S(2)}) async-start(bf16[16,72,128]{2,1,0:T(8,128)(2,1)} %spread.1), calls=%async_computation.1 | async-start | bytes 589824 | tf_op jit(solution)/shard_map/all_to_all | solution.py:326
  33.5 0.0 copy-done.5
  33.5 0.1 reshape.22
  33.5 0.1 copy.16
  33.6 0.0 copy-done.4
  33.6 0.1 reshape.21
  33.7 0.1 copy.15
  33.8 0.1 copy.17
  34.0 0.1 reshape.23
  34.1 0.1 pad_add_fusion.lent_ref
  34.1 0.1 masks.1.mask_ref
  34.3 0.0 copy-done.6
  34.3 0.0 copy-done.7
  34.3 0.0 copy-done.3
  34.4 0.0 copy-done.2
  34.4 2.3 %home.1 = (bf16[16,64,128]{2,1,0:T(8,128)(2,1)S(1)}, f32[16,16,128]{2,1,0:T(8,128)S(1)}) custom-call(s32[2,128]{1,0:T(2,128)S(1)} %pad.9.home_ref, bf16[16,16,640]{2,1,0:T(8,128)(2,1)S(1)} %all_to_all.25.first_ref, bf16[16,16,1024]{2,1,0:T(8,128)(2,1)S(1)} %copy-done.2, bf16[16,16,1024]{2,1,0:T(8,128)(2,1)S(1)} %copy-done.3), custom_call_target="tpu_custom_call" | custom-call | tf_op jit(solution)/shard_map/home/pallas_call | solution.py:332
  36.7 0.0 copy-start
  36.7 0.0 copy-start.1
  36.7 15.0 %all-to-all-done.1.mine_ref = bf16[16,72,128]{2,1,0:T(8,128)(2,1)S(1)} async-done(((bf16[16,72,128]{2,1,0:T(8,128)(2,1)}), bf16[16,72,128]{2,1,0:T(8,128)(2,1)S(1)}, u32[]{:S(2)}, u32[]{:S(2)}) %all-to-all-start.1) | async-done | bytes 294944 | tf_op jit(solution)/shard_map/all_to_all | solution.py:326
  51.7 0.9 pick.1
  52.7 21.7 %all_to_all.26.x_ref = bf16[32,32,512]{2,1,0:T(8,128)(2,1)S(1)} all-to-all(bf16[32,32,512]{2,1,0:T(8,128)(2,1)S(1)} %get-tuple-element.24), channel_id=1, replica_groups={{0,1,2,3,4,5,6,7,8,9,10,11,12,13,14,15,16,17,18,19,20,21,22,23,24,25,26..., dimensions={0} | all-to-all | bytes 2097152 | tf_op jit(solution)/shard_map/all_to_all | solution.py:326
  74.4 0.0 copy-done
  74.4 0.0 copy-done.1
  74.4 3.2 %attend.1 = bf16[32,176,128]{2,1,0:T(8,128)(2,1)S(1)} custom-call(bf16[32,32,512]{2,1,0:T(8,128)(2,1)S(1)} %all_to_all.26.x_ref, bf16[512,128]{1,0:T(8,128)(2,1)S(1)} %masks.1.mask_ref, bf16[16,64,128]{2,1,0:T(8,128)(2,1)S(1)} %get-tuple-element.26.home_ref, f32[16,16,128]{2,1,0:T(8,128)S(1)} %get-tuple-element.27.home_lse_ref, ...), custom_call_target="tpu_custom_call" | custom-call | tf_op jit(solution)/shard_map/attend/pallas_call | solution.py:332
  77.6 25.2 %all_to_all.27.x_ref = bf16[32,176,128]{2,1,0:T(8,128)(2,1)S(1)} all-to-all(bf16[32,176,128]{2,1,0:T(8,128)(2,1)S(1)} %attend.1), channel_id=1, replica_groups={{0,1,2,3,4,5,6,7,8,9,10,11,12,13,14,15,16,17,18,19,20,21,22,23,24,25,26..., dimensions={0} | all-to-all | bytes 2883584 | tf_op jit(solution)/shard_map/all_to_all | solution.py:326
  102.7 2.1 %merge.1 = (bf16[16,72,128]{2,1,0:T(8,128)(2,1)}, f32[16,512]{1,0:T(8,128)S(1)}, f32[16,512]{1,0:T(8,128)S(1)}) custom-call(s32[2,8,128]{2,1,0:T(8,128)S(1)} %broadcast_in_dim.7.me_ref, f32[2,8,512]{2,1,0:T(8,128)S(1)} %get-tuple-element.23.target_ref, bf16[32,176,128]{2,1,0:T(8,128)(2,1)S(1)} %all_to_all.27.x_ref), custom_call_target="tpu_custom_call" | custom-call | tf_op jit(solution)/shard_map/merge/pallas_call | solution.py:332
  104.9 5.6 %all-to-all-start.4 = ((bf16[16,72,128]{2,1,0:T(8,128)(2,1)}), bf16[16,72,128]{2,1,0:T(8,128)(2,1)S(1)}, u32[]{:S(2)}, u32[]{:S(2)}) async-start(bf16[16,72,128]{2,1,0:T(8,128)(2,1)} %get-tuple-element.30), calls=%async_computation.4 | async-start | bytes 589824 | tf_op jit(solution)/shard_map/all_to_all | solution.py:326
  110.4 1.9 %collective-permute-start = (f32[16,512]{1,0:T(8,128)S(1)}, f32[16,512]{1,0:T(8,128)S(1)}, u32[]{:S(2)}, u32[]{:S(2)}) collective-permute-start(f32[16,512]{1,0:T(8,128)S(1)} %get-tuple-element.29), channel_id=1, source_target_pairs={{0,16},{16,0},{32,48},{48,32},{64,80},{80,64},{96,112},{112,96},{1... | collective-permute-start | bytes 98312 | tf_op jit(solution)/shard_map/ppermute | solution.py:427
  112.3 1.2 collective-permute-done.come_ref
  113.5 16.1 %all-to-all-done.4.x_ref = bf16[16,72,128]{2,1,0:T(8,128)(2,1)S(1)} async-done(((bf16[16,72,128]{2,1,0:T(8,128)(2,1)}), bf16[16,72,128]{2,1,0:T(8,128)(2,1)S(1)}, u32[]{:S(2)}, u32[]{:S(2)}) %all-to-all-start.4) | async-done | bytes 294944 | tf_op jit(solution)/shard_map/all_to_all | solution.py:326
  129.6 1.0 final.1
  (6 shorter events, 0.1 us)
Async XLA Ops:
  0.0 33.5 %copy-start.5 = (s32[1,32,1,2]{1,3,2,0:T(2,128)S(1)}, s32[1,32,1,2]{1,3,2,0:T(2,128)}, u32[]{:S(2)}) copy-start(s32[1,32,1,2]{1,3,2,0:T(2,128)} %param.19) | copy-start | bytes 772
  0.0 33.6 %copy-start.4 = (s32[1,32,1,2,2]{1,4,3,2,0:T(2,128)S(1)}, s32[1,32,1,2,2]{1,4,3,2,0:T(2,128)}, u32[]{:S(2)}) copy-start(s32[1,32,1,2,2]{1,4,3,2,0:T(2,128)} %param.18) | copy-start | bytes 1540
  0.0 34.3 %copy-start.6 = (s32[16,1]{0,1:T(1,128)S(1)}, s32[16,1]{0,1:T(1,128)}, u32[]{:S(2)}) copy-start(s32[16,1]{0,1:T(1,128)} %param.14) | copy-start | bytes 196
  0.0 34.3 %copy-start.7 = (s32[16,1,1]{0,2,1:T(1,128)S(1)}, s32[16,1,1]{0,2,1:T(1,128)}, u32[]{:S(2)}) copy-start(s32[16,1,1]{0,2,1:T(1,128)} %param.13) | copy-start | bytes 196
  0.0 34.3 %copy-start.3 = (bf16[16,16,1024]{2,1,0:T(8,128)(2,1)S(1)}, bf16[16,16,1024]{2,1,0:T(8,128)(2,1)}, u32[]{:S(2)}) copy-start(bf16[16,16,1024]{2,1,0:T(8,128)(2,1)} %v_ref.2) | copy-start | bytes 1572868
  0.0 34.3 %copy-start.2 = (bf16[16,16,1024]{2,1,0:T(8,128)(2,1)S(1)}, bf16[16,16,1024]{2,1,0:T(8,128)(2,1)}, u32[]{:S(2)}) copy-start(bf16[16,16,1024]{2,1,0:T(8,128)(2,1)} %k_ref.2) | copy-start | bytes 1572868
  18.7 33.0 %all-to-all-start.1 = ((bf16[16,72,128]{2,1,0:T(8,128)(2,1)}), bf16[16,72,128]{2,1,0:T(8,128)(2,1)S(1)}, u32[]{:S(2)}, u32[]{:S(2)}) async-start(bf16[16,72,128]{2,1,0:T(8,128)(2,1)} %spread.1), calls=%async_computation.1 | async-start | bytes 589824 | tf_op jit(solution)/shard_map/all_to_all | solution.py:326
  36.7 37.7 %copy-start = (bf16[32,16,1024]{2,1,0:T(8,128)(2,1)S(1)}, bf16[32,16,1024]{2,1,0:T(8,128)(2,1)}, u32[]{:S(2)}) copy-start(bf16[32,16,1024]{2,1,0:T(8,128)(2,1)} %k_ref.3) | copy-start | bytes 3145732
  36.7 37.7 %copy-start.1 = (bf16[32,16,1024]{2,1,0:T(8,128)(2,1)S(1)}, bf16[32,16,1024]{2,1,0:T(8,128)(2,1)}, u32[]{:S(2)}) copy-start(bf16[32,16,1024]{2,1,0:T(8,128)(2,1)} %v_ref.3) | copy-start | bytes 3145732
  104.9 24.8 %all-to-all-start.4 = ((bf16[16,72,128]{2,1,0:T(8,128)(2,1)}), bf16[16,72,128]{2,1,0:T(8,128)(2,1)S(1)}, u32[]{:S(2)}, u32[]{:S(2)}) async-start(bf16[16,72,128]{2,1,0:T(8,128)(2,1)} %get-tuple-element.30), calls=%async_computation.4 | async-start | bytes 589824 | tf_op jit(solution)/shard_map/all_to_all | solution.py:326
  110.4 3.1 %collective-permute-start = (f32[16,512]{1,0:T(8,128)S(1)}, f32[16,512]{1,0:T(8,128)S(1)}, u32[]{:S(2)}, u32[]{:S(2)}) collective-permute-start(f32[16,512]{1,0:T(8,128)S(1)} %get-tuple-element.29), channel_id=1, source_target_pairs={{0,16},{16,0},{32,48},{48,32},{64,80},{80,64},{96,112},{112,96},{1... | collective-permute-start | bytes 98312 | tf_op jit(solution)/shard_map/ppermute | solution.py:427

commit v7 on v6

--- a/solution.py
+++ b/solution.py
@@ -20,7 +20,7 @@
 WIDTH = 512
 CHIPS = N_INST // 2
 HALF = SLOTS // 2
-PIECE = 4 * HALF + 2 * ROWS + 16
+PIECE = 4 * HALF + 2 * ROWS + 8
 DEAD = -1e30
 SCALE = HD ** (-0.5)
 F32 = jnp.float32
@@ -207,61 +207,70 @@
             lse = columns(tt, peaks, total, SLOTS)
             home_lse = home_lse_ref[2 * k + tt]
             column = [lse[:HALF], home_lse, rest, lse[HALF:], home_lse, rest]
-            lse = thirds(jnp.concatenate(column, axis=0), iota((128, 128), 1)).T[:16].astype(BF16)
+            lse = thirds(jnp.concatenate(column, axis=0), iota((128, 128), 1)).T
+            other = pltpu.roll(lse[:16], 64, 1)
+            near = iota((8, 128), 1) < 64
             for d in range(2):
                 to = d * N_TP + 2 * k + tt
                 for h in range(4):
                     at = (tt * 4 + h) * SLOTS + d * HALF
                     out_ref[to, h * HALF : (h + 1) * HALF, :] = mixed[at : at + HALF]
-                out_ref[to, 4 * HALF : PIECE - 16, :] = home_ref[
+                out_ref[to, 4 * HALF : PIECE - 8, :] = home_ref[
                     2 * k + tt, 2 * d * ROWS : 2 * (d + 1) * ROWS, :
                 ]
-                out_ref[to, PIECE - 16 :, :] = lse
-
-
-def merge_kernel(me_ref, target_ref, x_ref, out_ref, keep_ref, give_ref):
-    core = jnp.bitwise_and(me_ref[0, :1], 1)
-    rows = [
-        jnp.concatenate(
-            [x_ref[8 * chunk + j, PIECE - 16 :, :] for j in range(8)], axis=1
-        )
-        for chunk in range(4)
-    ]
-    k = iota((1024, 3 * 128), 0)
-    n = iota((1024, 3 * 128), 1)
-    place = jnp.bitwise_and(n, 127)
-    source = 128 * jnp.right_shift(place, 4) + 64 * jnp.concatenate([core] * 3, axis=1)
-    source = source + 16 * jnp.right_shift(n, 7) + jnp.bitwise_and(place, 15)
-    moved = dot(jnp.concatenate(rows, axis=0), jnp.where(k == source, 1.0, 0.0).astype(BF16))
-    lses = []
-    for chunk in range(4):
-        part = moved[16 * chunk : 16 * (chunk + 1)]
-        lses.append(part[0:4] + part[4:8] + part[8:12])
-
-    def gather(group, chunks):
-        cut = slice(group * 128, (group + 1) * 128)
-        return jnp.concatenate([lses[chunk][:, cut] for chunk in chunks], axis=1)
-
-    ones = jnp.ones((512, HD), BF16)
-
-    def join(mask, lse, values):
-        score = jnp.where(mask, lse, DEAD)
-        peak = jnp.max(score, axis=1, keepdims=True)
-        weight = jnp.exp(score - peak)
-        upper = weight.astype(BF16)
-        lower = (weight - upper.astype(F32)).astype(BF16)
-        values = jnp.concatenate([values, ones[: values.shape[0]]], axis=1)
-        both = dot(jnp.concatenate([upper, lower], axis=0), values)
-        count = mask.shape[0]
-        both = both[:count] + both[count:]
-        return both[:, :HD] / both[:, HD:], peak + jnp.log(both[:, HD:])
-
+                pair = (other[:8], lse[8:16]) if d else (lse[:8], other[8:])
+                out_ref[to, PIECE - 8 :, :] = jnp.where(near, *pair).astype(BF16)
+
+
+def settled(x_ref, groups):
+    wide = 2 * len(groups) * 128
+    k = iota((128, wide), 0)
+    n = iota((128, wide), 1)
+    source = 64 * jnp.bitwise_and(jnp.right_shift(n, 7), 1) + jnp.bitwise_and(n, 15)
+    for j, group in enumerate(groups):
+        source = source + jnp.where(jnp.right_shift(n, 8) == j, 16 * group, 0)
+    rows = x_ref[:, PIECE - 8 :, :].astype(F32).reshape(2 * N_TP * 8, 128).astype(BF16)
+    moved = dot(rows, jnp.where(k == source, 1.0, 0.0).astype(BF16))
+    place = jnp.right_shift(iota((8, 128), 1), 4)
+
+    def settle(chunk, part):
+        row = jnp.zeros((8, 128), F32)
+        for j in range(8):
+            at = (8 * chunk + j) * 8
+            row = jnp.where(place == j, moved[at : at + 8, part * 128 : (part + 1) * 128], row)
+        return row
+
+    out = []
+    for j in range(len(groups)):
+        chunks = []
+        for chunk in range(4):
+            upper = settle(chunk, 2 * j)
+            chunks.append(upper[0:4] + upper[4:8] + settle(chunk, 2 * j + 1)[0:4])
+        out.append(chunks)
+    return out
+
+
+def join(mask, lse, values):
+    score = jnp.where(mask, lse, DEAD)
+    peak = jnp.max(score, axis=1, keepdims=True)
+    weight = jnp.exp(score - peak)
+    upper = weight.astype(BF16)
+    lower = (weight - upper.astype(F32)).astype(BF16)
+    values = jnp.concatenate([values, jnp.ones(values.shape, BF16)], axis=1)
+    both = dot(jnp.concatenate([upper, lower], axis=0), values)
+    count = mask.shape[0]
+    both = both[:count] + both[count:]
+    return both[:, :HD] / both[:, HD:], peak + jnp.log(both[:, HD:])
+
+
+def merge_kernel(target_ref, x_ref, out_ref):
+    lses = settled(x_ref, (0, 1))
     rows = iota((128, 512), 0).astype(F32)
     row = jnp.bitwise_and(iota((128, 128), 0), 8)
     lane = iota((128, 128), 1) - 8 * row
     head = jnp.bitwise_and(lane, 3)
     for g in range(2):
-        lse = gather(g, range(4))
+        lse = jnp.concatenate(lses[g], axis=1)
         mask = rows == target_ref[g, 0:1, :]
         out_lse = jnp.zeros((128, 128), F32)
         block = slice(g * 8, (g + 1) * 8)
@@ -273,10 +282,15 @@
             out_ref[block, head_rows(h), :] = mixed.astype(BF16).reshape(8, ROWS, HD)
         out_lse = jnp.where(lane >= 0, thirds(out_lse, lane), 0.0).reshape(8, ROWS, 128)
         out_ref[block, 4 * ROWS :, :] = (out_lse[:, :8] + out_lse[:, 8:]).astype(BF16)
+
+
+def home_merge_kernel(me_ref, x_ref, keep_ref, give_ref):
+    core = jnp.bitwise_and(me_ref[0, :1], 1)
+    lses = settled(x_ref, (2,))[0]
     mask = iota((ROWS, 256), 0) == jnp.bitwise_and(iota((ROWS, 256), 1), 15)
     homes = []
     for d in range(2):
-        lse = gather(2, range(2 * d, 2 * d + 2))
+        lse = jnp.concatenate(lses[2 * d : 2 * d + 2], axis=1)
         lse = jnp.where(core[:, :1] == 0, lse[0:2], lse[2:4])
         parts = []
         for hh in range(2):
@@ -358,9 +372,11 @@
     me = jnp.stack([lax.axis_index("inst"), lax.axis_index("tp")]).astype(jnp.int32)
     me = jnp.broadcast_to(me[:, None, None], (2, 8, 128))
 
-    asked = jnp.pad(lend_row.reshape(N_INST, 2).T.astype(BF16), ((0, 0), (0, 128 - N_INST)))
-    asked = jnp.broadcast_to(asked[:, None], (2, 8, 128)).reshape(ROWS, 128)
-    sent, me = lax.optimization_barrier((jnp.concatenate([queries, asked], axis=1), me))
+    asked = jnp.broadcast_to(lend_row.reshape(N_INST, 2).T.astype(BF16)[:, None], (2, 8, N_INST))
+    sent = jnp.concatenate(
+        [queries.reshape(2, 8, WIDTH), asked, jnp.zeros((2, 8, 128 - N_INST), BF16)], axis=2
+    )
+    sent, me = lax.optimization_barrier((sent.reshape(ROWS, WIDTH + 128), me))
     sent = jnp.broadcast_to(sent[None], (N_TP, ROWS, WIDTH + 128))
     first = exchange(sent, "tp")
     sent = pl.pallas_call(
@@ -414,15 +430,14 @@
         (arrived, mask, home, home_lse, lent_keys, lent_values),
     )
     returned = exchange(partial, ("inst", "tp"), plane)
-    merged, keep, give = call(
-        merge_kernel,
-        "merge",
-        (
-            jax.ShapeDtypeStruct(block, BF16),
-            jax.ShapeDtypeStruct((ROWS, 4 * HD), F32),
-            jax.ShapeDtypeStruct((ROWS, 4 * HD), F32),
-        ),
-        (me, target, returned),
+    merged = call(
+        merge_kernel, "merge", jax.ShapeDtypeStruct(block, BF16), (target, returned)
+    )
+    keep, give = call(
+        home_merge_kernel,
+        "home_merge",
+        tuple(jax.ShapeDtypeStruct((ROWS, 4 * HD), F32) for _ in range(2)),
+        (me, returned),
     )
     come = lax.ppermute(give, "inst", sibling)
     back = exchange(merged, "inst", same_core)

time: 131 us -> 131 us (level)
    pallas_call x6 -> x7, Pallas kernels: 9.69 us -> 10.1 us  [call(): pl.pallas_call(kernel, out_shape=out_shape, in_specs=[VMEM] * len(args),...]
where the time goes in v7:
time: 131 us; the launch traced here: 130 us
  blocking collectives  62.2 us (47%)
  waiting for transfers between devices  31.9 us (24%)
  starting transfers between devices  22.3 us (17%)
  Pallas kernels  11 us (8%)
  other arithmetic  1.66 us (1%)
    all_to_all x3, blocking collectives, exchange(): lax.all_to_all(x, axis, split_axis=0, concat_axis=0, axis_index_groups=gr...  62.2 us
    all_to_all x2, waiting for transfers between devices, exchange(): lax.all_to_all(x, axis, split_axis=0, concat_axis=0, axis_index_groups=gr...  30.7 us
    all_to_all x2, starting transfers between devices, exchange(): lax.all_to_all(x, axis, split_axis=0, concat_axis=0, axis_index_groups=gr...  20.3 us
    pallas_call x7, Pallas kernels, call(): pl.pallas_call(kernel, out_shape=out_shape, in_specs=[VMEM] * len(args),...  10.1 us
  transfers between devices with their start and end apart: 3, of which 3 were waited for; matrix products, arithmetic and copies ran while one was open for 1% of the time, Pallas kernels for 2%

profile of v7, /device:TPU:64, one launch (start us, length us, event | category | flops | bytes accessed | tf_op | source)
XLA Modules:
  0.0 130.1 jit_solution(605694523541052109)
XLA Ops:
  0.0 0.0 copy-start.5
  0.0 0.0 copy-start.4
  0.0 0.0 copy-start.6
  0.0 0.0 copy-start.7
  0.0 0.0 copy-start.3
  0.0 0.0 copy-start.2
  0.0 0.8 convert_bitcast_fusion
  0.8 0.1 pad_add_fusion.1
  0.9 0.1 pad.15.clone
  1.0 0.7 maximum_maximum_fusion
  1.7 0.1 broadcast_in_dim.10.me_ref
  1.8 16.0 %all_to_all.25.first_ref = bf16[16,16,640]{2,1,0:T(8,128)(2,1)S(1)} all-to-all(bf16[16,16,640]{2,1,0:T(8,128)(2,1)S(1)} %broadcast_in_dim.11), channel_id=1, replica_groups=mesh['inst'=32,'tp'=16] {'tp'}, dimensions={0} | all-to-all | bytes 655360 | tf_op jit(solution)/shard_map/all_to_all | solution.py:340
  17.8 0.9 spread.1
  18.8 14.8 %all-to-all-start.1 = ((bf16[16,72,128]{2,1,0:T(8,128)(2,1)}), bf16[16,72,128]{2,1,0:T(8,128)(2,1)S(1)}, u32[]{:S(2)}, u32[]{:S(2)}) async-start(bf16[16,72,128]{2,1,0:T(8,128)(2,1)} %spread.1), calls=%async_computation.1 | async-start | bytes 589824 | tf_op jit(solution)/shard_map/all_to_all | solution.py:340
  33.5 0.0 copy-done.5
  33.5 0.1 reshape.24
  33.6 0.1 copy.16
  33.7 0.0 copy-done.4
  33.7 0.1 reshape.23
  33.8 0.1 copy.15
  33.9 0.1 copy.17
  34.0 0.1 reshape.25
  34.1 0.1 pad_add_fusion.lent_ref
  34.2 0.1 masks.1.mask_ref
  34.4 0.0 copy-done.6
  34.4 0.0 copy-done.7
  34.4 0.0 copy-done.3
  34.4 0.0 copy-done.2
  34.4 2.3 %home.1 = (bf16[16,64,128]{2,1,0:T(8,128)(2,1)S(1)}, f32[16,16,128]{2,1,0:T(8,128)S(1)}) custom-call(s32[2,128]{1,0:T(2,128)S(1)} %pad.4.home_ref, bf16[16,16,640]{2,1,0:T(8,128)(2,1)S(1)} %all_to_all.25.first_ref, bf16[16,16,1024]{2,1,0:T(8,128)(2,1)S(1)} %copy-done.2, bf16[16,16,1024]{2,1,0:T(8,128)(2,1)S(1)} %copy-done.3), custom_call_target="tpu_custom_call" | custom-call | tf_op jit(solution)/shard_map/home/pallas_call | solution.py:346
  36.8 0.0 copy-start
  36.8 0.0 copy-start.1
  36.8 15.0 %all-to-all-done.1.mine_ref = bf16[16,72,128]{2,1,0:T(8,128)(2,1)S(1)} async-done(((bf16[16,72,128]{2,1,0:T(8,128)(2,1)}), bf16[16,72,128]{2,1,0:T(8,128)(2,1)S(1)}, u32[]{:S(2)}, u32[]{:S(2)}) %all-to-all-start.1) | async-done | bytes 294944 | tf_op jit(solution)/shard_map/all_to_all | solution.py:340
  51.8 0.9 pick.1
  52.7 21.7 %all_to_all.26.x_ref = bf16[32,32,512]{2,1,0:T(8,128)(2,1)S(1)} all-to-all(bf16[32,32,512]{2,1,0:T(8,128)(2,1)S(1)} %get-tuple-element.22), channel_id=1, replica_groups={{0,1,2,3,4,5,6,7,8,9,10,11,12,13,14,15,16,17,18,19,20,21,22,23,24,25,26..., dimensions={0} | all-to-all | bytes 2097152 | tf_op jit(solution)/shard_map/all_to_all | solution.py:340
  74.5 0.0 copy-done
  74.5 0.0 copy-done.1
  74.5 3.2 %attend.1 = bf16[32,168,128]{2,1,0:T(8,128)(2,1)S(1)} custom-call(bf16[32,32,512]{2,1,0:T(8,128)(2,1)S(1)} %all_to_all.26.x_ref, bf16[512,128]{1,0:T(8,128)(2,1)S(1)} %masks.1.mask_ref, bf16[16,64,128]{2,1,0:T(8,128)(2,1)S(1)} %get-tuple-element.24.home_ref, f32[16,16,128]{2,1,0:T(8,128)S(1)} %get-tuple-element.25.home_lse_ref, ...), custom_call_target="tpu_custom_call" | custom-call | tf_op jit(solution)/shard_map/attend/pallas_call | solution.py:346
  77.7 24.5 %all_to_all.27.x_ref = bf16[32,168,128]{2,1,0:T(8,128)(2,1)S(1)} all-to-all(bf16[32,168,128]{2,1,0:T(8,128)(2,1)S(1)} %attend.1), channel_id=1, replica_groups={{0,1,2,3,4,5,6,7,8,9,10,11,12,13,14,15,16,17,18,19,20,21,22,23,24,25,26..., dimensions={0} | all-to-all | bytes 2752512 | tf_op jit(solution)/shard_map/all_to_all | solution.py:340
  102.2 2.0 %merge.1 = bf16[16,72,128]{2,1,0:T(8,128)(2,1)} custom-call(f32[2,8,512]{2,1,0:T(8,128)S(1)} %get-tuple-element.28.target_ref, bf16[32,168,128]{2,1,0:T(8,128)(2,1)S(1)} %all_to_all.27.x_ref), custom_call_target="tpu_custom_call" | custom-call | tf_op jit(solution)/shard_map/merge/pallas_call | solution.py:346
  104.2 5.6 %all-to-all-start.4 = ((bf16[16,72,128]{2,1,0:T(8,128)(2,1)}), bf16[16,72,128]{2,1,0:T(8,128)(2,1)S(1)}, u32[]{:S(2)}, u32[]{:S(2)}) async-start(bf16[16,72,128]{2,1,0:T(8,128)(2,1)} %merge.1), calls=%async_computation.4 | async-start | bytes 589824 | tf_op jit(solution)/shard_map/all_to_all | solution.py:340
  109.8 0.5 home_merge.1
  110.2 1.9 %collective-permute-start = (f32[16,512]{1,0:T(8,128)S(1)}, f32[16,512]{1,0:T(8,128)S(1)}, u32[]{:S(2)}, u32[]{:S(2)}) collective-permute-start(f32[16,512]{1,0:T(8,128)S(1)} %get-tuple-element.27), channel_id=1, source_target_pairs={{0,16},{16,0},{32,48},{48,32},{64,80},{80,64},{96,112},{112,96},{1... | collective-permute-start | bytes 98312 | tf_op jit(solution)/shard_map/ppermute | solution.py:442
  112.2 1.2 collective-permute-done.come_ref
  113.3 15.7 %all-to-all-done.4.x_ref = bf16[16,72,128]{2,1,0:T(8,128)(2,1)S(1)} async-done(((bf16[16,72,128]{2,1,0:T(8,128)(2,1)}), bf16[16,72,128]{2,1,0:T(8,128)(2,1)S(1)}, u32[]{:S(2)}, u32[]{:S(2)}) %all-to-all-start.4) | async-done | bytes 294944 | tf_op jit(solution)/shard_map/all_to_all | solution.py:340
  129.1 1.0 final.1
  (6 shorter events, 0.1 us)
Async XLA Ops:
  0.0 33.5 %copy-start.5 = (s32[1,32,1,2]{1,3,2,0:T(2,128)S(1)}, s32[1,32,1,2]{1,3,2,0:T(2,128)}, u32[]{:S(2)}) copy-start(s32[1,32,1,2]{1,3,2,0:T(2,128)} %param.19) | copy-start | bytes 772
  0.0 33.7 %copy-start.4 = (s32[1,32,1,2,2]{1,4,3,2,0:T(2,128)S(1)}, s32[1,32,1,2,2]{1,4,3,2,0:T(2,128)}, u32[]{:S(2)}) copy-start(s32[1,32,1,2,2]{1,4,3,2,0:T(2,128)} %param.18) | copy-start | bytes 1540
  0.0 34.4 %copy-start.6 = (s32[16,1]{0,1:T(1,128)S(1)}, s32[16,1]{0,1:T(1,128)}, u32[]{:S(2)}) copy-start(s32[16,1]{0,1:T(1,128)} %param.14) | copy-start | bytes 196
  0.0 34.4 %copy-start.7 = (s32[16,1,1]{0,2,1:T(1,128)S(1)}, s32[16,1,1]{0,2,1:T(1,128)}, u32[]{:S(2)}) copy-start(s32[16,1,1]{0,2,1:T(1,128)} %param.13) | copy-start | bytes 196
  0.0 34.4 %copy-start.3 = (bf16[16,16,1024]{2,1,0:T(8,128)(2,1)S(1)}, bf16[16,16,1024]{2,1,0:T(8,128)(2,1)}, u32[]{:S(2)}) copy-start(bf16[16,16,1024]{2,1,0:T(8,128)(2,1)} %v_ref.2) | copy-start | bytes 1572868
  0.0 34.4 %copy-start.2 = (bf16[16,16,1024]{2,1,0:T(8,128)(2,1)S(1)}, bf16[16,16,1024]{2,1,0:T(8,128)(2,1)}, u32[]{:S(2)}) copy-start(bf16[16,16,1024]{2,1,0:T(8,128)(2,1)} %k_ref.2) | copy-start | bytes 1572868
  18.8 33.0 %all-to-all-start.1 = ((bf16[16,72,128]{2,1,0:T(8,128)(2,1)}), bf16[16,72,128]{2,1,0:T(8,128)(2,1)S(1)}, u32[]{:S(2)}, u32[]{:S(2)}) async-start(bf16[16,72,128]{2,1,0:T(8,128)(2,1)} %spread.1), calls=%async_computation.1 | async-start | bytes 589824 | tf_op jit(solution)/shard_map/all_to_all | solution.py:340
  36.8 37.7 %copy-start = (bf16[32,16,1024]{2,1,0:T(8,128)(2,1)S(1)}, bf16[32,16,1024]{2,1,0:T(8,128)(2,1)}, u32[]{:S(2)}) copy-start(bf16[32,16,1024]{2,1,0:T(8,128)(2,1)} %k_ref.3) | copy-start | bytes 3145732
  36.8 37.7 %copy-start.1 = (bf16[32,16,1024]{2,1,0:T(8,128)(2,1)S(1)}, bf16[32,16,1024]{2,1,0:T(8,128)(2,1)}, u32[]{:S(2)}) copy-start(bf16[32,16,1024]{2,1,0:T(8,128)(2,1)} %v_ref.3) | copy-start | bytes 3145732
  104.2 24.8 %all-to-all-start.4 = ((bf16[16,72,128]{2,1,0:T(8,128)(2,1)}), bf16[16,72,128]{2,1,0:T(8,128)(2,1)S(1)}, u32[]{:S(2)}, u32[]{:S(2)}) async-start(bf16[16,72,128]{2,1,0:T(8,128)(2,1)} %merge.1), calls=%async_computation.4 | async-start | bytes 589824 | tf_op jit(solution)/shard_map/all_to_all | solution.py:340
  110.2 3.1 %collective-permute-start = (f32[16,512]{1,0:T(8,128)S(1)}, f32[16,512]{1,0:T(8,128)S(1)}, u32[]{:S(2)}, u32[]{:S(2)}) collective-permute-start(f32[16,512]{1,0:T(8,128)S(1)} %get-tuple-element.27), channel_id=1, source_target_pairs={{0,16},{16,0},{32,48},{48,32},{64,80},{80,64},{96,112},{112,96},{1... | collective-permute-start | bytes 98312 | tf_op jit(solution)/shard_map/ppermute | solution.py:442

commit v8 on v7

--- a/solution.py
+++ b/solution.py
@@ -140,11 +140,11 @@
 
 
 def pool(query, pick, keys, values, count):
-    query = jnp.concatenate([query, jnp.concatenate([pick] * 8, axis=0)], axis=1)
+    query = jnp.concatenate([query, jnp.concatenate([pick] * (query.shape[0] // count), axis=0)], axis=1)
     scores = dot_nt(query, keys)
     weights = []
     peaks = []
-    for j in range(8):
+    for j in range(query.shape[0] // count):
         part = scores[j * count : (j + 1) * count]
         peak = jnp.max(part, axis=1, keepdims=True)
         weights.append(jnp.exp2((part - peak) * FACTOR).astype(BF16))
@@ -197,14 +197,14 @@
         cut = slice(k * HD, (k + 1) * HD)
         keys = jnp.concatenate([k_ref[:, :, cut].reshape(512, HD), mask], axis=1)
         values = jnp.concatenate([v_ref[:, :, cut].reshape(512, HD), ones], axis=1)
-        query = [
-            x_ref[d * N_TP + 2 * k + tt, :, h * HD : (h + 1) * HD]
-            for tt, h in HEADS
-            for d in range(2)
-        ]
-        mixed, peaks, total = pool(jnp.concatenate(query, axis=0), pick, keys, values, SLOTS)
         for tt in range(2):
-            lse = columns(tt, peaks, total, SLOTS)
+            query = [
+                x_ref[d * N_TP + 2 * k + tt, :, h * HD : (h + 1) * HD]
+                for h in range(4)
+                for d in range(2)
+            ]
+            mixed, peaks, total = pool(jnp.concatenate(query, axis=0), pick, keys, values, SLOTS)
+            lse = columns(0, peaks, total, SLOTS)
             home_lse = home_lse_ref[2 * k + tt]
             column = [lse[:HALF], home_lse, rest, lse[HALF:], home_lse, rest]
             lse = thirds(jnp.concatenate(column, axis=0), iota((128, 128), 1)).T
@@ -213,7 +213,7 @@
             for d in range(2):
                 to = d * N_TP + 2 * k + tt
                 for h in range(4):
-                    at = (tt * 4 + h) * SLOTS + d * HALF
+                    at = h * SLOTS + d * HALF
                     out_ref[to, h * HALF : (h + 1) * HALF, :] = mixed[at : at + HALF]
                 out_ref[to, 4 * HALF : PIECE - 8, :] = home_ref[
                     2 * k + tt, 2 * d * ROWS : 2 * (d + 1) * ROWS, :

time: 131 us -> 130 us (level)
  no operation moved by 1% of the time
where the time goes in v8:
time: 130 us
  blocking collectives  62.2 us (48%)
  waiting for transfers between devices  31.9 us (25%)
  starting transfers between devices  22.3 us (17%)
  Pallas kernels  10.9 us (8%)
  other arithmetic  1.66 us (1%)
    all_to_all x3, blocking collectives, exchange(): lax.all_to_all(x, axis, split_axis=0, concat_axis=0, axis_index_groups=gr...  62.2 us
    all_to_all x2, waiting for transfers between devices, exchange(): lax.all_to_all(x, axis, split_axis=0, concat_axis=0, axis_index_groups=gr...  30.7 us
    all_to_all x2, starting transfers between devices, exchange(): lax.all_to_all(x, axis, split_axis=0, concat_axis=0, axis_index_groups=gr...  20.3 us
    pallas_call x7, Pallas kernels, call(): pl.pallas_call(kernel, out_shape=out_shape, in_specs=[VMEM] * len(args),...  9.92 us
  transfers between devices with their start and end apart: 3, of which 3 were waited for; matrix products, arithmetic and copies ran while one was open for 1% of the time, Pallas kernels for 2%

profile of v8, /device:TPU:64, one launch (start us, length us, event | category | flops | bytes accessed | tf_op | source)
XLA Modules:
  0.0 129.9 jit_solution(2959251551941363079)
XLA Ops:
  0.0 0.0 copy-start.5
  0.0 0.0 copy-start.4
  0.0 0.0 copy-start.6
  0.0 0.0 copy-start.7
  0.0 0.0 copy-start.3
  0.0 0.0 copy-start.2
  0.0 0.8 convert_bitcast_fusion
  0.8 0.1 pad_add_fusion.1
  0.9 0.1 pad.15.clone
  1.0 0.7 maximum_maximum_fusion
  1.7 0.1 broadcast_in_dim.10.me_ref
  1.8 16.0 %all_to_all.25.first_ref = bf16[16,16,640]{2,1,0:T(8,128)(2,1)S(1)} all-to-all(bf16[16,16,640]{2,1,0:T(8,128)(2,1)S(1)} %broadcast_in_dim.11), channel_id=1, replica_groups=mesh['inst'=32,'tp'=16] {'tp'}, dimensions={0} | all-to-all | bytes 655360 | tf_op jit(solution)/shard_map/all_to_all | solution.py:340
  17.8 0.9 spread.1
  18.8 14.8 %all-to-all-start.1 = ((bf16[16,72,128]{2,1,0:T(8,128)(2,1)}), bf16[16,72,128]{2,1,0:T(8,128)(2,1)S(1)}, u32[]{:S(2)}, u32[]{:S(2)}) async-start(bf16[16,72,128]{2,1,0:T(8,128)(2,1)} %spread.1), calls=%async_computation.1 | async-start | bytes 589824 | tf_op jit(solution)/shard_map/all_to_all | solution.py:340
  33.5 0.0 copy-done.5
  33.5 0.1 reshape.24
  33.6 0.1 copy.16
  33.7 0.0 copy-done.4
  33.7 0.1 reshape.23
  33.8 0.1 copy.15
  33.9 0.1 copy.17
  34.0 0.1 reshape.25
  34.1 0.1 pad_add_fusion.lent_ref
  34.2 0.1 masks.1.mask_ref
  34.4 0.0 copy-done.6
  34.4 0.0 copy-done.7
  34.4 0.0 copy-done.3
  34.4 0.0 copy-done.2
  34.4 2.3 %home.1 = (bf16[16,64,128]{2,1,0:T(8,128)(2,1)S(1)}, f32[16,16,128]{2,1,0:T(8,128)S(1)}) custom-call(s32[2,128]{1,0:T(2,128)S(1)} %pad.4.home_ref, bf16[16,16,640]{2,1,0:T(8,128)(2,1)S(1)} %all_to_all.25.first_ref, bf16[16,16,1024]{2,1,0:T(8,128)(2,1)S(1)} %copy-done.2, bf16[16,16,1024]{2,1,0:T(8,128)(2,1)S(1)} %copy-done.3), custom_call_target="tpu_custom_call" | custom-call | tf_op jit(solution)/shard_map/home/pallas_call | solution.py:346
  36.8 0.0 copy-start
  36.8 0.0 copy-start.1
  36.8 15.0 %all-to-all-done.1.mine_ref = bf16[16,72,128]{2,1,0:T(8,128)(2,1)S(1)} async-done(((bf16[16,72,128]{2,1,0:T(8,128)(2,1)}), bf16[16,72,128]{2,1,0:T(8,128)(2,1)S(1)}, u32[]{:S(2)}, u32[]{:S(2)}) %all-to-all-start.1) | async-done | bytes 294944 | tf_op jit(solution)/shard_map/all_to_all | solution.py:340
  51.8 0.9 pick.1
  52.7 21.7 %all_to_all.26.x_ref = bf16[32,32,512]{2,1,0:T(8,128)(2,1)S(1)} all-to-all(bf16[32,32,512]{2,1,0:T(8,128)(2,1)S(1)} %get-tuple-element.22), channel_id=1, replica_groups={{0,1,2,3,4,5,6,7,8,9,10,11,12,13,14,15,16,17,18,19,20,21,22,23,24,25,26..., dimensions={0} | all-to-all | bytes 2097152 | tf_op jit(solution)/shard_map/all_to_all | solution.py:340
  74.5 0.0 copy-done
  74.5 0.0 copy-done.1
  74.5 3.1 %attend.1 = bf16[32,168,128]{2,1,0:T(8,128)(2,1)S(1)} custom-call(bf16[32,32,512]{2,1,0:T(8,128)(2,1)S(1)} %all_to_all.26.x_ref, bf16[512,128]{1,0:T(8,128)(2,1)S(1)} %masks.1.mask_ref, bf16[16,64,128]{2,1,0:T(8,128)(2,1)S(1)} %get-tuple-element.24.home_ref, f32[16,16,128]{2,1,0:T(8,128)S(1)} %get-tuple-element.25.home_lse_ref, ...), custom_call_target="tpu_custom_call" | custom-call | tf_op jit(solution)/shard_map/attend/pallas_call | solution.py:346
  77.6 24.5 %all_to_all.27.x_ref = bf16[32,168,128]{2,1,0:T(8,128)(2,1)S(1)} all-to-all(bf16[32,168,128]{2,1,0:T(8,128)(2,1)S(1)} %attend.1), channel_id=1, replica_groups={{0,1,2,3,4,5,6,7,8,9,10,11,12,13,14,15,16,17,18,19,20,21,22,23,24,25,26..., dimensions={0} | all-to-all | bytes 2752512 | tf_op jit(solution)/shard_map/all_to_all | solution.py:340
  102.1 2.0 %merge.1 = bf16[16,72,128]{2,1,0:T(8,128)(2,1)} custom-call(f32[2,8,512]{2,1,0:T(8,128)S(1)} %get-tuple-element.28.target_ref, bf16[32,168,128]{2,1,0:T(8,128)(2,1)S(1)} %all_to_all.27.x_ref), custom_call_target="tpu_custom_call" | custom-call | tf_op jit(solution)/shard_map/merge/pallas_call | solution.py:346
  104.0 5.6 %all-to-all-start.4 = ((bf16[16,72,128]{2,1,0:T(8,128)(2,1)}), bf16[16,72,128]{2,1,0:T(8,128)(2,1)S(1)}, u32[]{:S(2)}, u32[]{:S(2)}) async-start(bf16[16,72,128]{2,1,0:T(8,128)(2,1)} %merge.1), calls=%async_computation.4 | async-start | bytes 589824 | tf_op jit(solution)/shard_map/all_to_all | solution.py:340
  109.6 0.5 home_merge.1
  110.1 1.9 %collective-permute-start = (f32[16,512]{1,0:T(8,128)S(1)}, f32[16,512]{1,0:T(8,128)S(1)}, u32[]{:S(2)}, u32[]{:S(2)}) collective-permute-start(f32[16,512]{1,0:T(8,128)S(1)} %get-tuple-element.27), channel_id=1, source_target_pairs={{0,16},{16,0},{32,48},{48,32},{64,80},{80,64},{96,112},{112,96},{1... | collective-permute-start | bytes 98312 | tf_op jit(solution)/shard_map/ppermute | solution.py:442
  112.0 1.2 collective-permute-done.come_ref
  113.2 15.7 %all-to-all-done.4.x_ref = bf16[16,72,128]{2,1,0:T(8,128)(2,1)S(1)} async-done(((bf16[16,72,128]{2,1,0:T(8,128)(2,1)}), bf16[16,72,128]{2,1,0:T(8,128)(2,1)S(1)}, u32[]{:S(2)}, u32[]{:S(2)}) %all-to-all-start.4) | async-done | bytes 294944 | tf_op jit(solution)/shard_map/all_to_all | solution.py:340
  128.9 1.0 final.1
  (6 shorter events, 0.1 us)
Async XLA Ops:
  0.0 33.5 %copy-start.5 = (s32[1,32,1,2]{1,3,2,0:T(2,128)S(1)}, s32[1,32,1,2]{1,3,2,0:T(2,128)}, u32[]{:S(2)}) copy-start(s32[1,32,1,2]{1,3,2,0:T(2,128)} %param.19) | copy-start | bytes 772
  0.0 33.7 %copy-start.4 = (s32[1,32,1,2,2]{1,4,3,2,0:T(2,128)S(1)}, s32[1,32,1,2,2]{1,4,3,2,0:T(2,128)}, u32[]{:S(2)}) copy-start(s32[1,32,1,2,2]{1,4,3,2,0:T(2,128)} %param.18) | copy-start | bytes 1540
  0.0 34.4 %copy-start.6 = (s32[16,1]{0,1:T(1,128)S(1)}, s32[16,1]{0,1:T(1,128)}, u32[]{:S(2)}) copy-start(s32[16,1]{0,1:T(1,128)} %param.14) | copy-start | bytes 196
  0.0 34.4 %copy-start.7 = (s32[16,1,1]{0,2,1:T(1,128)S(1)}, s32[16,1,1]{0,2,1:T(1,128)}, u32[]{:S(2)}) copy-start(s32[16,1,1]{0,2,1:T(1,128)} %param.13) | copy-start | bytes 196
  0.0 34.4 %copy-start.3 = (bf16[16,16,1024]{2,1,0:T(8,128)(2,1)S(1)}, bf16[16,16,1024]{2,1,0:T(8,128)(2,1)}, u32[]{:S(2)}) copy-start(bf16[16,16,1024]{2,1,0:T(8,128)(2,1)} %v_ref.2) | copy-start | bytes 1572868
  0.0 34.4 %copy-start.2 = (bf16[16,16,1024]{2,1,0:T(8,128)(2,1)S(1)}, bf16[16,16,1024]{2,1,0:T(8,128)(2,1)}, u32[]{:S(2)}) copy-start(bf16[16,16,1024]{2,1,0:T(8,128)(2,1)} %k_ref.2) | copy-start | bytes 1572868
  18.8 33.0 %all-to-all-start.1 = ((bf16[16,72,128]{2,1,0:T(8,128)(2,1)}), bf16[16,72,128]{2,1,0:T(8,128)(2,1)S(1)}, u32[]{:S(2)}, u32[]{:S(2)}) async-start(bf16[16,72,128]{2,1,0:T(8,128)(2,1)} %spread.1), calls=%async_computation.1 | async-start | bytes 589824 | tf_op jit(solution)/shard_map/all_to_all | solution.py:340
  36.8 37.7 %copy-start = (bf16[32,16,1024]{2,1,0:T(8,128)(2,1)S(1)}, bf16[32,16,1024]{2,1,0:T(8,128)(2,1)}, u32[]{:S(2)}) copy-start(bf16[32,16,1024]{2,1,0:T(8,128)(2,1)} %k_ref.3) | copy-start | bytes 3145732
  36.8 37.7 %copy-start.1 = (bf16[32,16,1024]{2,1,0:T(8,128)(2,1)S(1)}, bf16[32,16,1024]{2,1,0:T(8,128)(2,1)}, u32[]{:S(2)}) copy-start(bf16[32,16,1024]{2,1,0:T(8,128)(2,1)} %v_ref.3) | copy-start | bytes 3145732
  104.0 24.8 %all-to-all-start.4 = ((bf16[16,72,128]{2,1,0:T(8,128)(2,1)}), bf16[16,72,128]{2,1,0:T(8,128)(2,1)S(1)}, u32[]{:S(2)}, u32[]{:S(2)}) async-start(bf16[16,72,128]{2,1,0:T(8,128)(2,1)} %merge.1), calls=%async_computation.4 | async-start | bytes 589824 | tf_op jit(solution)/shard_map/all_to_all | solution.py:340
  110.1 3.1 %collective-permute-start = (f32[16,512]{1,0:T(8,128)S(1)}, f32[16,512]{1,0:T(8,128)S(1)}, u32[]{:S(2)}, u32[]{:S(2)}) collective-permute-start(f32[16,512]{1,0:T(8,128)S(1)} %get-tuple-element.27), channel_id=1, source_target_pairs={{0,16},{16,0},{32,48},{48,32},{64,80},{80,64},{96,112},{112,96},{1... | collective-permute-start | bytes 98312 | tf_op jit(solution)/shard_map/ppermute | solution.py:442
